TPU v7x, 32 devices: a whole 2x2x4 slice. The times are simulated.
32 devices in a mesh: groups: 2 (over y), expert: 4 (over z), et: 4 (over x, core).
Axes of the slice: x: 2, y: 2, z: 4, core: 2. Of those that a mesh axis runs over, the one named last changes fastest.
Arguments:
- tokens: bfloat16 [4096, 2048], P(('groups', 'expert', 'et')), parts along dimension 0, may hold values from -6 to 6
- grad_out: bfloat16 [4096, 2048], P(('groups', 'expert', 'et')), parts along dimension 0, may hold values from -3 to 3
- routes: int32 [4096, 1], P(('groups', 'expert', 'et')), parts along dimension 0, may hold values from 0 to 3; in each aligned block of 128 rows (0 to 127, 128 to 255, ...) at most 64 rows name the same one
- order: int32 [32, 128], P(('groups', 'expert', 'et')), parts along dimension 0, may hold values from 0 to 127, each once within a row
- w_gate: bfloat16 [4, 2048, 2048], P('expert', None, 'et'), may hold values from -0.125 to 0.125
- w_up: bfloat16 [4, 2048, 2048], P('expert', None, 'et'), may hold values from -0.125 to 0.125
- w_down: bfloat16 [4, 2048, 2048], P('expert', 'et'), may hold values from -0.125 to 0.125
Outputs:
- grad_tokens: bfloat16 [4096, 2048], P(('groups', 'expert', 'et')), parts along dimension 0
- grad_gate: bfloat16 [8, 2048, 2048], P(('groups', 'expert'), None, 'et'), parts along dimension 0
- grad_up: bfloat16 [8, 2048, 2048], P(('groups', 'expert'), None, 'et'), parts along dimension 0
- grad_down: bfloat16 [8, 2048, 2048], P(('groups', 'expert'), 'et'), parts along dimension 0
There are 2 independent parts, one for each index of `groups`. A program takes and returns all parts, laid end to end along the dimension named above; an argument that names none is the same for every part. Nothing has to cross between parts.
Inputs may be any that keep to these rules, and one draw needn't show every extreme that they name: `routes`: in each aligned block of 128 rows (the rows of one device) no expert is named by more than 64 rows. `order`: each row holds every number of 0 to 127 once.
All inputs are finite; a program needn't handle non-finite values.
Results may differ from a plain program's by a relative error of at most 0.005.
Values may be sent and summed in bfloat16 or wider, within the bound.
No kernel may reach another device: no remote copies, remote signals or barrier semaphores. Data moves between devices by JAX's collectives and lax.ppermute only.
A program may use at most 128 MiB of HBM per device.

v0:
```python
import jax
import jax.numpy as jnp
from jax import lax
from jax.sharding import PartitionSpec as P


def slot_table(routes, order, slot_cap, slot_count):
    route = routes[:, 0]
    priority = order[0]
    same = route[:, None] == route[None, :]
    earlier = priority[None, :] < priority[:, None]
    rank = jnp.sum((same & earlier).astype(jnp.int32), axis=1)
    slot = route * slot_cap + rank
    kept = rank < slot_cap
    positions = lax.broadcasted_iota(jnp.int32, (slot_count, route.shape[0]), 0)
    return ((positions == slot[None, :]) & kept[None, :]).astype(jnp.bfloat16)


def expert_backward(inputs, cotangent, gate_w, up_w, down_w):
    gate = jnp.dot(inputs, gate_w, preferred_element_type=jnp.float32)
    upper = jnp.dot(inputs, up_w, preferred_element_type=jnp.float32)
    sig = jax.nn.sigmoid(gate)
    active = gate * sig
    slope = sig * (1.0 + gate * (1.0 - sig))
    hidden = (active * upper).astype(jnp.bfloat16)
    grad_hidden = lax.dot_general(
        cotangent, down_w, (((1,), (1,)), ((), ())), preferred_element_type=jnp.float32
    )
    grad_upper = (grad_hidden * active).astype(jnp.bfloat16)
    grad_gated = (grad_hidden * upper * slope).astype(jnp.bfloat16)
    down_grad = lax.dot_general(
        hidden, cotangent, (((0,), (0,)), ((), ())), preferred_element_type=jnp.float32
    )
    gate_grad = lax.dot_general(
        inputs, grad_gated, (((0,), (0,)), ((), ())), preferred_element_type=jnp.float32
    )
    up_grad = lax.dot_general(
        inputs, grad_upper, (((0,), (0,)), ((), ())), preferred_element_type=jnp.float32
    )
    input_grad = lax.dot_general(
        grad_gated, gate_w, (((1,), (1,)), ((), ())), preferred_element_type=jnp.float32
    )
    input_grad = input_grad + lax.dot_general(
        grad_upper, up_w, (((1,), (1,)), ((), ())), preferred_element_type=jnp.float32
    )
    return (gate_grad, up_grad, down_grad, input_grad)


def on_device(tokens, grad_out, routes, order, w_gate, w_up, w_down):
    expert_count = lax.axis_size("expert")
    local_tokens = tokens.shape[0]
    model_width = tokens.shape[1]
    slot_cap = local_tokens // expert_count
    slot_count = expert_count * slot_cap
    select = slot_table(routes, order, slot_cap, slot_count)
    send_in = (
        jnp.dot(select, tokens, preferred_element_type=jnp.float32)
        .astype(jnp.bfloat16)
        .reshape(expert_count, slot_cap, model_width)
    )
    send_cot = (
        jnp.dot(select, grad_out, preferred_element_type=jnp.float32)
        .astype(jnp.bfloat16)
        .reshape(expert_count, slot_cap, model_width)
    )
    got_in, got_cot = (
        lax.all_to_all(send_in, "expert", split_axis=0, concat_axis=0, tiled=True),
        lax.all_to_all(send_cot, "expert", split_axis=0, concat_axis=0, tiled=True),
    )
    got_in = got_in.reshape(slot_count, model_width)
    got_cot = got_cot.reshape(slot_count, model_width)
    gate_w = w_gate[0]
    up_w = w_up[0]
    down_w = w_down[0]
    all_in, all_cot = (
        lax.all_gather(got_in, "et", axis=0, tiled=True),
        lax.all_gather(got_cot, "et", axis=0, tiled=True),
    )
    gate_grad, up_grad, down_grad, partials = expert_backward(all_in, all_cot, gate_w, up_w, down_w)
    own_rows = lax.psum_scatter(partials, "et", scatter_dimension=0, tiled=True)
    sent_back = own_rows.astype(jnp.bfloat16).reshape(expert_count, slot_cap, model_width)
    arrived = lax.all_to_all(sent_back, "expert", split_axis=0, concat_axis=0, tiled=True).reshape(
        slot_count, model_width
    )
    grad_tokens = lax.dot_general(
        select, arrived, (((0,), (0,)), ((), ())), preferred_element_type=jnp.float32
    ).astype(jnp.bfloat16)
    return (
        grad_tokens,
        gate_grad.astype(jnp.bfloat16)[None],
        up_grad.astype(jnp.bfloat16)[None],
        down_grad.astype(jnp.bfloat16)[None],
    )


def solution(mesh):
    return jax.shard_map(
        on_device,
        mesh=mesh,
        in_specs=(
            P(("groups", "expert", "et"), None),
            P(("groups", "expert", "et"), None),
            P(("groups", "expert", "et"), None),
            P(("groups", "expert", "et"), None),
            P("expert", None, "et"),
            P("expert", None, "et"),
            P("expert", "et", None),
        ),
        out_specs=(
            P(("groups", "expert", "et"), None),
            P(("groups", "expert"), None, "et"),
            P(("groups", "expert"), None, "et"),
            P(("groups", "expert"), "et", None),
        ),
        check_vma=False,
    )
```

profile of v0, /device:TPU:0, one launch (start us, length us, event | category | flops | bytes accessed | tf_op | source)
XLA Modules:
  0.0 160.0 jit_solution(9792882126500369284)
XLA Ops:
  7.2 0.0 copy-start
  7.2 0.0 all-gather.5.cloned.1.call-start
  7.2 1.1 convert_reduce_fusion
  8.3 0.7 multiply_add_fusion
  9.0 1.3 convolution_convert_fusion.4
  10.3 20.7 %all_to_all.15 = bf16[4,32,2048]{2,1,0:T(8,128)(2,1)} all-to-all(bf16[4,32,2048]{2,1,0:T(8,128)(2,1)S(1)} %bitcast.44), channel_id=1, replica_groups=mesh['groups'=2,'expert'=4,'et'=4] {'expert'}, dimensions={0} | all-to-all | bytes 1048576 | tf_op jit(solution)/shard_map/all_to_all | solution.py:67
  31.0 0.0 all-gather.5.cloned.1.call-update
  31.0 0.0 all-gather.3.cloned.1.call-start
  31.1 0.3 convolution_convert_fusion.5
  31.4 16.7 %all_to_all.16 = bf16[4,32,2048]{2,1,0:T(8,128)(2,1)} all-to-all(bf16[4,32,2048]{2,1,0:T(8,128)(2,1)S(1)} %bitcast.45), channel_id=1, replica_groups=mesh['groups'=2,'expert'=4,'et'=4] {'expert'}, dimensions={0} | all-to-all | bytes 1048576 | tf_op jit(solution)/shard_map/all_to_all | solution.py:68
  48.1 0.0 all-gather.3.cloned.1.call-update
  48.2 0.0 reduce-scatter.2.cloned.1.call-start
  48.2 4.7 %all-gather.5.cloned.1.call-done = bf16[512,2048]{1,0:T(8,128)(2,1)} async-done(((bf16[128,2048]{1,0:T(8,128)(2,1)}), bf16[512,2048]{1,0:T(8,128)(2,1)}) %all-gather.5.cloned.1.call-update) | async-done | bytes 2097168 | tf_op jit(solution)/shard_map/all_gather | solution.py:76
  52.9 4.0 %fusion.5 = f32[512,512]{1,0:T(8,128)} fusion(bf16[512,2048]{1,0:T(8,128)(2,1)} %all-gather.5.cloned.1.call-done, bf16[1,2048,512]{2,1,0:T(8,128)(2,1)S(1)} %copy-done), kind=kOutput, calls=%fused_computation.12 | convolution fusion | flops 1073741824 | bytes 5242880 | tf_op jit(solution)/shard_map/dot_general | solution.py:20
  56.9 0.0 copy-done.1
  56.9 2.3 %fusion.8 = f32[512,512]{1,0:T(8,128)} fusion(bf16[512,2048]{1,0:T(8,128)(2,1)S(1)} %copy-done.5, bf16[1,2048,512]{2,1,0:T(8,128)(2,1)S(1)} %copy-done.1), kind=kOutput, calls=%fused_computation.15 | convolution fusion | flops 1073741824 | bytes 5242880 | tf_op jit(solution)/shard_map/dot_general | solution.py:21
  59.2 17.9 %all-gather.3.cloned.1.call-done = bf16[512,2048]{1,0:T(8,128)(2,1)} async-done(((bf16[128,2048]{1,0:T(8,128)(2,1)}), bf16[512,2048]{1,0:T(8,128)(2,1)}) %all-gather.3.cloned.1.call-update) | async-done | bytes 2097168 | tf_op jit(solution)/shard_map/all_gather | solution.py:77
  77.1 4.4 %multiply_convert_fusion.1 = (bf16[512,512]{1,0:T(8,128)(2,1)S(1)}, bf16[512,512]{1,0:T(8,128)(2,1)S(1)}) fusion(f32[512,512]{1,0:T(8,128)} %fusion.5, f32[512,512]{1,0:T(8,128)} %fusion.8, bf16[512,2048]{1,0:T(8,128)(2,1)} %all-gather.3.cloned.1.call-done, bf16[1,512,2048]{2,1,0:T(8,128)(2,1)} %param.13), kind=kOutput, calls=%fused_computation.20 | convolution fusion | flops 1077149696 | bytes 7340032 | tf_op jit(solution)/shard_map/dot_general | solution.py:26
  81.5 0.0 copy-start.4
  81.5 0.0 copy-start.2
  81.5 1.3 fusion.3
  82.8 0.5 copy-done.2
  83.2 3.3 %convolution_add_fusion = f32[512,2048]{1,0:T(8,128)} fusion(f32[512,2048]{1,0:T(8,128)S(1)} %fusion.3, bf16[512,512]{1,0:T(8,128)(2,1)S(1)} %get-tuple-element.4, bf16[1,2048,512]{2,1,0:T(8,128)(2,1)S(1)} %copy-done.2), kind=kOutput, calls=%fused_computation | convolution fusion | flops 1074790400 | bytes 11010048 | tf_op jit(solution)/shard_map/dot_general | solution.py:43
  86.5 0.0 reduce-scatter.2.cloned.1.call-update
  86.5 44.7 %reduce-scatter.2.cloned.1.call-done = f32[128,2048]{1,0:T(8,128)} async-done(((f32[512,2048]{1,0:T(8,128)}), f32[128,2048]{1,0:T(8,128)}) %reduce-scatter.2.cloned.1.call-update) | async-done | bytes 1048592 | tf_op jit(solution)/shard_map/reduce_scatter | solution.py:80
  131.2 2.1 %convert_element_type.39 = bf16[128,2048]{1,0:T(8,128)(2,1)} convert(f32[128,2048]{1,0:T(8,128)} %reduce-scatter.2.cloned.1.call-done) | non-fusion elementwise | flops 262144 | bytes 1572864 | tf_op jit(solution)/shard_map/convert_element_type | solution.py:81
  133.3 4.6 %all-to-all-start.2 = ((bf16[4,32,2048]{2,1,0:T(8,128)(2,1)}), bf16[4,32,2048]{2,1,0:T(8,128)(2,1)S(1)}, u32[]{:S(2)}, u32[]{:S(2)}) async-start(bf16[4,32,2048]{2,1,0:T(8,128)(2,1)} %bitcast.9), calls=%async_computation.3 | async-start | bytes 1048576 | tf_op jit(solution)/shard_map/all_to_all | solution.py:82
  137.9 4.4 %fusion.1 = bf16[1,2048,512]{2,1,0:T(8,128)(2,1)} fusion(bf16[512,2048]{1,0:T(8,128)(2,1)} %all-gather.5.cloned.1.call-done, bf16[512,512]{1,0:T(8,128)(2,1)} %copy-done.4), kind=kOutput, calls=%fused_computation.5 | convolution fusion | flops 1074790400 | bytes 4718592 | tf_op jit(solution)/shard_map/dot_general | solution.py:37
  142.3 2.6 %fusion = bf16[1,2048,512]{2,1,0:T(8,128)(2,1)} fusion(bf16[512,2048]{1,0:T(8,128)(2,1)S(1)} %copy-done.6, bf16[512,512]{1,0:T(8,128)(2,1)S(1)} %get-tuple-element.5), kind=kOutput, calls=%fused_computation.4 | convolution fusion | flops 1074790400 | bytes 4718592 | tf_op jit(solution)/shard_map/dot_general | solution.py:34
  144.9 2.7 %fusion.2 = bf16[1,512,2048]{2,1,0:T(8,128)(2,1)} fusion(bf16[512,2048]{1,0:T(8,128)(2,1)S(1)} %copy-done.7, f32[512,512]{1,0:T(8,128)S(1)} %copy-done.9, f32[512,512]{1,0:T(8,128)S(1)} %copy-done.8), kind=kOutput, calls=%fused_computation.6 | convolution fusion | flops 1076363264 | bytes 6291456 | tf_op jit(solution)/shard_map/dot_general | solution.py:31
  147.6 4.7 %all-to-all-done.2 = bf16[4,32,2048]{2,1,0:T(8,128)(2,1)S(1)} async-done(((bf16[4,32,2048]{2,1,0:T(8,128)(2,1)}), bf16[4,32,2048]{2,1,0:T(8,128)(2,1)S(1)}, u32[]{:S(2)}, u32[]{:S(2)}) %all-to-all-start.2) | async-done | bytes 524320 | tf_op jit(solution)/shard_map/all_to_all | solution.py:82
  152.4 1.1 convolution_convert_fusion.3
  (16 shorter events, 0.0 us)
Async XLA Ops:
  7.2 45.7 %copy-start = (bf16[1,2048,512]{2,1,0:T(8,128)(2,1)S(1)}, bf16[1,2048,512]{2,1,0:T(8,128)(2,1)}, u32[]{:S(2)}) copy-start(bf16[1,2048,512]{2,1,0:T(8,128)(2,1)} %param.11) | copy-start | bytes 6291460
  7.2 23.9 %copy-start.3 = (bf16[128,2048]{1,0:T(8,128)(2,1)S(1)}, bf16[128,2048]{1,0:T(8,128)(2,1)}, u32[]{:S(2)}) copy-start(bf16[128,2048]{1,0:T(8,128)(2,1)} %param.8) | copy-start | bytes 1572868
  7.2 45.7 %all-gather.5.cloned.1.call-start = ((), (), s32[]{:S(2)}) async-start(), calls=%async_computation.5 | async-start | bytes 2621440 | tf_op jit(solution)/shard_map/all_gather | solution.py:76
  31.0 46.0 %all-gather.3.cloned.1.call-start = ((), (), s32[]{:S(2)}) async-start(), calls=%async_computation.4 | async-start | bytes 2621440 | tf_op jit(solution)/shard_map/all_gather | solution.py:77
  48.2 83.0 %reduce-scatter.2.cloned.1.call-start = ((), (), s32[]{:S(2)}) async-start(), calls=%async_computation.6 | async-start | bytes 5242880 | tf_op jit(solution)/shard_map/reduce_scatter | solution.py:80
  52.9 4.0 %copy-start.1 = (bf16[1,2048,512]{2,1,0:T(8,128)(2,1)S(1)}, bf16[1,2048,512]{2,1,0:T(8,128)(2,1)}, u32[]{:S(2)}) copy-start(bf16[1,2048,512]{2,1,0:T(8,128)(2,1)} %param.12) | copy-start | bytes 6291460
  52.9 4.0 %copy-start.5 = (bf16[512,2048]{1,0:T(8,128)(2,1)S(1)}, bf16[512,2048]{1,0:T(8,128)(2,1)}, u32[]{:S(2)}) copy-start(bf16[512,2048]{1,0:T(8,128)(2,1)} %all-gather.5.cloned.1.call-done) | copy-start | bytes 6291460
  81.5 1.3 copy-start.4
  81.5 1.8 %copy-start.2 = (bf16[1,2048,512]{2,1,0:T(8,128)(2,1)S(1)}, bf16[1,2048,512]{2,1,0:T(8,128)(2,1)}, u32[]{:S(2)}) copy-start(bf16[1,2048,512]{2,1,0:T(8,128)(2,1)} %param.12) | copy-start | bytes 6291460
  133.3 19.1 %all-to-all-start.2 = ((bf16[4,32,2048]{2,1,0:T(8,128)(2,1)}), bf16[4,32,2048]{2,1,0:T(8,128)(2,1)S(1)}, u32[]{:S(2)}, u32[]{:S(2)}) async-start(bf16[4,32,2048]{2,1,0:T(8,128)(2,1)} %bitcast.9), calls=%async_computation.3 | async-start | bytes 1048576 | tf_op jit(solution)/shard_map/all_to_all | solution.py:82
  137.9 4.4 %copy-start.6 = (bf16[512,2048]{1,0:T(8,128)(2,1)S(1)}, bf16[512,2048]{1,0:T(8,128)(2,1)}, u32[]{:S(2)}) copy-start(bf16[512,2048]{1,0:T(8,128)(2,1)} %all-gather.5.cloned.1.call-done) | copy-start | bytes 6291460
  142.3 2.6 %copy-start.7 = (bf16[512,2048]{1,0:T(8,128)(2,1)S(1)}, bf16[512,2048]{1,0:T(8,128)(2,1)}, u32[]{:S(2)}) copy-start(bf16[512,2048]{1,0:T(8,128)(2,1)} %all-gather.3.cloned.1.call-done) | copy-start | bytes 6291460
  142.3 2.6 %copy-start.8 = (f32[512,512]{1,0:T(8,128)S(1)}, f32[512,512]{1,0:T(8,128)}, u32[]{:S(2)}) copy-start(f32[512,512]{1,0:T(8,128)} %fusion.5) | copy-start | bytes 3145732
  142.3 2.6 %copy-start.9 = (f32[512,512]{1,0:T(8,128)S(1)}, f32[512,512]{1,0:T(8,128)}, u32[]{:S(2)}) copy-start(f32[512,512]{1,0:T(8,128)} %fusion.8) | copy-start | bytes 3145732
Sparse Core Ops, SparseCore 0:
  31.2 21.6 all-gather.4
  54.5 22.5 all-gather.2
  86.6 44.4 reduce-scatter.1
where the time goes:
time: 160 us
  waiting for transfers between devices  72 us (45%)
  blocking collectives  37.4 us (23%)
  matrix products  27.7 us (17%)
  between operations  13.8 us (9%)
  starting transfers between devices  4.72 us (3%)
  other arithmetic  3.81 us (2%)
    reduce_scatter x1, waiting for transfers between devices, on_device(): own_rows = lax.psum_scatter(partials, 'et', scatter_dimension=0, tiled=True)  44.7 us
    all_to_all x1, blocking collectives, on_device(): lax.all_to_all(send_in, 'expert', split_axis=0, concat_axis=0, tiled=True)  20.7 us
    all_gather x1, waiting for transfers between devices, on_device(): lax.all_gather(got_cot, 'et', axis=0, tiled=True)  17.9 us
    all_to_all x1, blocking collectives, on_device(): lax.all_to_all(send_cot, 'expert', split_axis=0, concat_axis=0, tiled=True)  16.7 us
    all_to_all x1, waiting for transfers between devices, on_device(): lax.all_to_all(sent_back, 'expert', split_axis=0, concat_axis=0, tiled=True)  4.75 us
    all_gather x1, waiting for transfers between devices, on_device(): lax.all_gather(got_in, 'et', axis=0, tiled=True)  4.68 us
    all_to_all x1, starting transfers between devices, on_device(): lax.all_to_all(sent_back, 'expert', split_axis=0, concat_axis=0, tiled=True)  4.6 us
    dot_general x1, matrix products, expert_backward(): lax.dot_general(inputs, grad_upper, (((0,), (0,)), ((), ())), preferred_e...  4.44 us
  transfers between devices with their start and end apart: 4, of which 4 were waited for; matrix products, arithmetic and copies ran while one was open for 10% of the time, Pallas kernels for 0%

commit v1 on v0

v1 whole, which is shorter than its diff:
```python
import functools

import jax
import jax.numpy as jnp
from jax import lax
from jax.experimental import pallas as pl
from jax.experimental.pallas import tpu as pltpu
from jax.sharding import PartitionSpec as P

BF16 = jnp.bfloat16
F32 = jnp.float32
GROUPS = 4
VMEM = pl.BlockSpec(memory_space=pltpu.VMEM)
NT = (((1,), (1,)), ((), ()))
TN = (((0,), (0,)), ((), ()))


def params(mib):
    return pltpu.CompilerParams(vmem_limit_bytes=mib * 1024 * 1024)


def cost(flops, moved):
    return pl.CostEstimate(flops=flops, bytes_accessed=moved, transcendentals=0)


def select_kernel(slot_cap, me, tokens, grad_out, routes, order, *outs):
    sends, back = outs[:-1], outs[-1]
    count = tokens.shape[0]
    width = tokens.shape[1]
    rows = lax.broadcasted_iota(jnp.int32, (count, count), 0)
    lanes = lax.broadcasted_iota(jnp.int32, (count, count), 1)
    eye = rows == lanes
    route_col = jnp.broadcast_to(routes[...], (count, count))
    route_row = jnp.sum(jnp.where(eye, route_col, 0), axis=0, keepdims=True)
    order_row = order[...]
    order_col = jnp.sum(jnp.where(eye, order_row, 0), axis=1, keepdims=True)
    ahead = (route_col == route_row) & (order_col < order_row)
    rank = jnp.sum(ahead.astype(jnp.int32), axis=0, keepdims=True)
    place = jnp.bitwise_xor(route_row, me[0]) * slot_cap + rank
    place = jnp.where(rank < slot_cap, place, -1)
    select = (rows == place).astype(F32).astype(BF16)
    place_col = jnp.sum(jnp.where(eye, place, 0), axis=1, keepdims=True)
    back[...] = (lanes == place_col).astype(F32).astype(BF16)
    step = count // len(sends)
    moved_in = jnp.dot(select, tokens[...], preferred_element_type=F32).astype(BF16)
    moved_cot = jnp.dot(select, grad_out[...], preferred_element_type=F32).astype(BF16)
    for g, send in enumerate(sends):
        send[:, :width] = moved_in[g * step : (g + 1) * step]
        send[:, width:] = moved_cot[g * step : (g + 1) * step]


def select_rows(tokens, grad_out, routes, order, slot_cap, me):
    count, width = tokens.shape
    step = count // GROUPS
    return pl.pallas_call(
        functools.partial(select_kernel, slot_cap),
        out_shape=[jax.ShapeDtypeStruct((step, 2 * width), BF16)] * GROUPS
        + [jax.ShapeDtypeStruct((count, count), BF16)],
        in_specs=[pl.BlockSpec(memory_space=pltpu.SMEM)] + [VMEM] * 4,
        out_specs=[VMEM] * (GROUPS + 1),
        compiler_params=params(16),
        cost_estimate=cost(4 * count * count * width, 8 * count * width),
        name="select_rows",
    )(me, tokens, grad_out, routes, order)


def chunk_kernel(n, *refs):
    blocks = refs[:n]
    gate_w, up_w, down_w = refs[n : n + 3]
    hidden_out, gated_out, upper_out, away_out, keep_out = refs[n + 3 : n + 8]
    xs, ys = refs[n + 8 :]
    rows = blocks[0].shape[0]
    width = gate_w.shape[0]
    for m, block in enumerate(blocks):
        xs[m * rows : (m + 1) * rows] = block[:, :width]
        ys[m * rows : (m + 1) * rows] = block[:, width:]
    inputs = xs[...]
    gate = jnp.dot(inputs, gate_w[...], preferred_element_type=F32)
    upper = jnp.dot(inputs, up_w[...], preferred_element_type=F32)
    sig = jax.nn.sigmoid(gate)
    active = gate * sig
    slope = sig * (1.0 + gate * (1.0 - sig))
    hidden_out[...] = (active * upper).astype(BF16)
    grad_hidden = lax.dot_general(ys[...], down_w[...], NT, preferred_element_type=F32)
    grad_upper = (grad_hidden * active).astype(BF16)
    grad_gated = (grad_hidden * upper * slope).astype(BF16)
    gated_out[...] = grad_gated
    upper_out[...] = grad_upper
    back = lax.dot_general(grad_gated, gate_w[...], NT, preferred_element_type=F32)
    back = back + lax.dot_general(grad_upper, up_w[...], NT, preferred_element_type=F32)
    for m in range(0, n, 2):
        at = m // 2 * rows
        keep_out[at : at + rows] = back[m * rows : (m + 1) * rows]
        away_out[at : at + rows] = back[(m + 1) * rows : (m + 2) * rows].astype(BF16)


def chunk_backward(blocks, gate_w, up_w, down_w):
    n = len(blocks)
    rows = blocks[0].shape[0]
    width, units = gate_w.shape
    total = n * rows
    return pl.pallas_call(
        functools.partial(chunk_kernel, n),
        out_shape=[jax.ShapeDtypeStruct((total, units), BF16)] * 3
        + [
            jax.ShapeDtypeStruct((total // 2, width), BF16),
            jax.ShapeDtypeStruct((total // 2, width), F32),
        ],
        in_specs=[VMEM] * (n + 3),
        out_specs=[VMEM] * 5,
        scratch_shapes=[pltpu.VMEM((total, width), BF16)] * 2,
        compiler_params=params(32),
        cost_estimate=cost(10 * total * width * units, 6 * width * units),
        name="chunk_backward",
    )(*blocks, gate_w, up_w, down_w)


def weights_kernel(n, *refs):
    blocks = refs[:n]
    hidden, gated, upper = (refs[n + i * GROUPS : n + (i + 1) * GROUPS] for i in range(3))
    gate_out, up_out, down_out = refs[n + 3 * GROUPS : n + 3 * GROUPS + 3]
    xs, ys, hs, gs, us = refs[n + 3 * GROUPS + 3 :]
    step = pl.program_id(0)
    rows = blocks[0].shape[0]
    width = xs.shape[1]

    @pl.when(step == 0)
    def _():
        for m, block in enumerate(blocks):
            xs[m * rows : (m + 1) * rows] = block[:, :width]
            ys[m * rows : (m + 1) * rows] = block[:, width:]
        many = hidden[0].shape[0]
        for g in range(GROUPS):
            hs[g * many : (g + 1) * many] = hidden[g][...]
            gs[g * many : (g + 1) * many] = gated[g][...]
            us[g * many : (g + 1) * many] = upper[g][...]

    part = gate_out.shape[0]
    at = pl.ds(pl.multiple_of(step * part, part), part)
    inputs = xs[:, at]
    gate_out[...] = lax.dot_general(inputs, gs[...], TN, preferred_element_type=F32).astype(BF16)
    up_out[...] = lax.dot_general(inputs, us[...], TN, preferred_element_type=F32).astype(BF16)
    down_out[...] = lax.dot_general(hs[...], ys[:, at], TN, preferred_element_type=F32).astype(BF16)


def weight_grads(blocks, hidden, gated, upper, width, units):
    n = len(blocks)
    total = n * blocks[0].shape[0]
    steps = 4
    part = width // steps

    def whole(a):
        return pl.BlockSpec(a.shape, lambda i: (0, 0))

    operands = (*blocks, *hidden, *gated, *upper)
    return pl.pallas_call(
        functools.partial(weights_kernel, n),
        grid=(steps,),
        out_shape=[
            jax.ShapeDtypeStruct((width, units), BF16),
            jax.ShapeDtypeStruct((width, units), BF16),
            jax.ShapeDtypeStruct((units, width), BF16),
        ],
        in_specs=[whole(a) for a in operands],
        out_specs=[
            pl.BlockSpec((part, units), lambda i: (i, 0)),
            pl.BlockSpec((part, units), lambda i: (i, 0)),
            pl.BlockSpec((units, part), lambda i: (0, i)),
        ],
        scratch_shapes=[pltpu.VMEM((total, width), BF16)] * 2 + [pltpu.VMEM((total, units), BF16)] * 3,
        compiler_params=params(48),
        cost_estimate=cost(6 * total * width * units, 6 * width * units),
        name="weight_grads",
    )(*operands)


def place_kernel(back, *refs):
    groups, out = refs[:-1], refs[-1]
    rows = jnp.concatenate([group[...] for group in groups], axis=0)
    out[...] = jnp.dot(back[...], rows, preferred_element_type=F32).astype(BF16)


def place_rows(back, groups):
    count, width = back.shape[0], groups[0].shape[1]
    return pl.pallas_call(
        place_kernel,
        out_shape=jax.ShapeDtypeStruct((count, width), BF16),
        in_specs=[VMEM] * (1 + len(groups)),
        out_specs=VMEM,
        compiler_params=params(16),
        cost_estimate=cost(2 * count * count * width, 4 * count * width),
        name="place_rows",
    )(back, *groups)


def on_device(tokens, grad_out, routes, order, w_gate, w_up, w_down):
    experts = lax.axis_size("expert")
    shards = lax.axis_size("et")
    local_tokens, width = tokens.shape
    slot_cap = local_tokens // experts
    per_group = experts // GROUPS
    me = lax.axis_index("expert").astype(jnp.int32).reshape(1)

    def over_expert(a, k):
        if k == 0:
            return a
        return lax.ppermute(a, "expert", [(i, i ^ k) for i in range(experts)])

    def over_et(a, m):
        return lax.ppermute(a, "et", [(i, i ^ m) for i in range(shards)])

    def exchange(a, g):
        parts = []
        for i in range(per_group):
            piece = a if per_group == 1 else a[i * slot_cap : (i + 1) * slot_cap]
            parts.append(over_expert(piece, g * per_group + i))
        return parts[0] if per_group == 1 else jnp.concatenate(parts, axis=0)

    *sends, back = select_rows(tokens, grad_out, routes, order, slot_cap, me)
    gate_w, up_w, down_w = w_gate[0], w_up[0], w_down[0]
    units = gate_w.shape[1]
    rows = local_tokens // GROUPS
    sequence = [0, 1, 3, 2]
    all_blocks, hidden, gated, upper, returned = [], [], [], [], [None] * GROUPS
    for g in sequence:
        first = exchange(sends[g], g)
        blocks = [first] + [None] * (shards - 1)
        for m in range(2, shards, 2):
            blocks[m] = over_et(first, m)
        for m in range(0, shards, 2):
            blocks[m + 1] = over_et(blocks[m], 1)
        h, gg, gu, away, keep = chunk_backward(blocks, gate_w, up_w, down_w)
        all_blocks += blocks
        hidden.append(h)
        gated.append(gg)
        upper.append(gu)
        summed = keep + over_et(away, 1).astype(F32)
        own = summed[:rows]
        for m in range(2, shards, 2):
            part = summed[m // 2 * rows : (m // 2 + 1) * rows].astype(BF16)
            own = own + over_et(part, m).astype(F32)
        returned[g] = exchange(own.astype(BF16), g)
    gate_grad, up_grad, down_grad = weight_grads(all_blocks, hidden, gated, upper, width, units)
    grad_tokens = place_rows(back, returned)
    return grad_tokens, gate_grad[None], up_grad[None], down_grad[None]


def solution(mesh):
    return jax.shard_map(
        on_device,
        mesh=mesh,
        in_specs=(
            P(("groups", "expert", "et"), None),
            P(("groups", "expert", "et"), None),
            P(("groups", "expert", "et"), None),
            P(("groups", "expert", "et"), None),
            P("expert", None, "et"),
            P("expert", None, "et"),
            P("expert", "et", None),
        ),
        out_specs=(
            P(("groups", "expert", "et"), None),
            P(("groups", "expert"), None, "et"),
            P(("groups", "expert"), None, "et"),
            P(("groups", "expert"), "et", None),
        ),
        check_vma=False,
    )
```

time: 160 us -> 85.4 us (0.53)
  blocking collectives: 37.4 us -> 0 us
  waiting for transfers between devices: 72 us -> 38.6 us
  matrix products: 27.7 us -> 0 us
  Pallas kernels: 0 us -> 18.2 us
  starting transfers between devices: 4.72 us -> 18.8 us
  between operations: 13.8 us -> 0.82 us
  local copies, waits for them, and re-layouts: 0.52 us -> 8.34 us
  other arithmetic: 3.81 us -> 0.29 us
    reduce_scatter x1 -> x0, waiting for transfers between devices: 44.7 us -> none  [on_device(): own_rows = lax.psum_scatter(partials, 'et', scatter_dimension=0, tiled=True)]
    ppermute x0 -> x26, waiting for transfers between devices: none -> 38.6 us  [the longest x6 26.9 us: over_expert(): return lax.ppermute(a, 'expert', [(i, i ^ k) for i in range(experts)])]
    all_to_all x2 -> x0, blocking collectives: 37.4 us -> none  [the longest x1 20.7 us: on_device(): lax.all_to_all(send_in, 'expert', split_axis=0, concat_axis=0, tiled=True)]
    dot_general x11 -> x0, matrix products: 27.7 us -> none  [the longest x1 4.44 us: expert_backward(): lax.dot_general(inputs, grad_upper, (((0,), (0,)), ((), ())), preferred_e...]
    all_gather x2 -> x0, waiting for transfers between devices: 22.6 us -> none  [the longest x1 17.9 us: on_device(): lax.all_gather(got_cot, 'et', axis=0, tiled=True)]
    ppermute x0 -> x26, starting transfers between devices: none -> 18.8 us  [the longest x20 11.9 us: over_et(): return lax.ppermute(a, 'et', [(i, i ^ m) for i in range(shards)])]
    pallas_call x0 -> x7, Pallas kernels: none -> 18.2 us  [the longest x4 11.1 us: chunk_backward(): pl.pallas_call(functools.partial(chunk_kernel, n), out_shape=[jax.ShapeDt...]
    unnamed x20 -> x19, local copies, waits for them, and re-layouts: 0.52 us -> 8.28 us
  transfers between devices with their start and end apart: 4 -> 26, of which waited for: 4 -> 12; matrix products, arithmetic and copies ran while one was open for 10% -> 0% of each run, Pallas kernels for 0% -> 19%
where the time goes in v1:
time: 85.4 us; the launch traced here: 85 us
  waiting for transfers between devices  38.6 us (45%)
  starting transfers between devices  18.8 us (22%)
  Pallas kernels  18.2 us (21%)
  local copies, waits for them, and re-layouts  8.34 us (10%)
    ppermute x6, waiting for transfers between devices, over_expert(): return lax.ppermute(a, 'expert', [(i, i ^ k) for i in range(experts)])  26.9 us
    ppermute x20, starting transfers between devices, over_et(): return lax.ppermute(a, 'et', [(i, i ^ m) for i in range(shards)])  11.9 us
    ppermute x20, waiting for transfers between devices, over_et(): return lax.ppermute(a, 'et', [(i, i ^ m) for i in range(shards)])  11.7 us
    pallas_call x4, Pallas kernels, chunk_backward(): pl.pallas_call(functools.partial(chunk_kernel, n), out_shape=[jax.ShapeDt...  11.1 us
    unnamed x19, local copies, waits for them, and re-layouts  8.28 us
    ppermute x6, starting transfers between devices, over_expert(): return lax.ppermute(a, 'expert', [(i, i ^ k) for i in range(experts)])  6.97 us
    pallas_call x1, Pallas kernels, weight_grads(): pl.pallas_call(functools.partial(weights_kernel, n), grid=(steps,), out_s...  5.41 us
  transfers between devices with their start and end apart: 26, of which 12 were waited for; matrix products, arithmetic and copies ran while one was open for 0% of the time, Pallas kernels for 19%

profile of v1, /device:TPU:0, one launch (start us, length us, event | category | flops | bytes accessed | tf_op | source)
XLA Modules:
  0.0 85.0 jit_solution(4394872517664924816)
XLA Ops:
  0.6 0.8 copy.11.routes
  1.4 1.0 %copy-done.6 = bf16[128,2048]{1,0:T(8,128)(2,1)S(1)} copy-done((bf16[128,2048]{1,0:T(8,128)(2,1)S(1)}, bf16[128,2048]{1,0:T(8,128)(2,1)}, u32[]{:S(2)}) %copy-start.6) | copy-done | bytes 524312
  2.4 1.0 %copy-done.7 = bf16[128,2048]{1,0:T(8,128)(2,1)S(1)} copy-done((bf16[128,2048]{1,0:T(8,128)(2,1)S(1)}, bf16[128,2048]{1,0:T(8,128)(2,1)}, u32[]{:S(2)}) %copy-start.7) | copy-done | bytes 524312
  3.5 0.7 copy-done.8
  4.7 3.0 %collective-permute-start.1 = (bf16[32,4096]{1,0:T(8,128)(2,1)S(1)}, bf16[32,4096]{1,0:T(8,128)(2,1)S(1)}, u32[]{:S(2)}, u32[]{:S(2)}) collective-permute-start(bf16[32,4096]{1,0:T(8,128)(2,1)S(1)} %get-tuple-element.33.refs_0_), channel_id=1, source_target_pairs={{0,2},{1,3},{2,0},{3,1},{4,6},{5,7},{6,4},{7,5},{8,10},{9,11},{10,... | collective-permute-start | bytes 786440 | tf_op jit(solution)/shard_map/ppermute | solution.py:210
  7.7 3.6 %collective-permute-start.19 = (bf16[32,4096]{1,0:T(8,128)(2,1)S(1)}, bf16[32,4096]{1,0:T(8,128)(2,1)S(1)}, u32[]{:S(2)}, u32[]{:S(2)}) collective-permute-start(bf16[32,4096]{1,0:T(8,128)(2,1)S(1)} %get-tuple-element.42), channel_id=1, source_target_pairs={{0,12},{4,8},{8,4},{12,0},{1,13},{5,9},{9,5},{13,1},{2,14},{6,10},... | collective-permute-start | bytes 786440 | tf_op jit(solution)/shard_map/ppermute | solution.py:207
  11.3 0.8 collective-permute-start.12
  12.1 1.9 %collective-permute-done.1.refs_2_ = bf16[32,4096]{1,0:T(8,128)(2,1)S(1)} collective-permute-done((bf16[32,4096]{1,0:T(8,128)(2,1)S(1)}, bf16[32,4096]{1,0:T(8,128)(2,1)S(1)}, u32[]{:S(2)}, u32[]{:S(2)}) %collective-permute-start.1) | collective-permute-done | bytes 262176 | tf_op jit(solution)/shard_map/ppermute | solution.py:210
  14.0 4.8 %collective-permute-done.19.refs_0_.refs_8_ = bf16[32,4096]{1,0:T(8,128)(2,1)S(1)} collective-permute-done((bf16[32,4096]{1,0:T(8,128)(2,1)S(1)}, bf16[32,4096]{1,0:T(8,128)(2,1)S(1)}, u32[]{:S(2)}, u32[]{:S(2)}) %collective-permute-start.19) | collective-permute-done | bytes 262176 | tf_op jit(solution)/shard_map/ppermute | solution.py:207
  19.1 4.8 %collective-permute-done.5.refs_0_.refs_4_ = bf16[32,4096]{1,0:T(8,128)(2,1)S(1)} collective-permute-done((bf16[32,4096]{1,0:T(8,128)(2,1)S(1)}, bf16[32,4096]{1,0:T(8,128)(2,1)S(1)}, u32[]{:S(2)}, u32[]{:S(2)}) %collective-permute-start.5) | collective-permute-done | bytes 262176 | tf_op jit(solution)/shard_map/ppermute | solution.py:207
  23.9 9.4 %collective-permute-done.12.refs_0_.refs_12_ = bf16[32,4096]{1,0:T(8,128)(2,1)S(1)} collective-permute-done((bf16[32,4096]{1,0:T(8,128)(2,1)S(1)}, bf16[32,4096]{1,0:T(8,128)(2,1)S(1)}, u32[]{:S(2)}, u32[]{:S(2)}) %collective-permute-start.12) | collective-permute-done | bytes 262176 | tf_op jit(solution)/shard_map/ppermute | solution.py:207
  33.9 1.5 %collective-permute-start.14 = (bf16[32,4096]{1,0:T(8,128)(2,1)S(1)}, bf16[32,4096]{1,0:T(8,128)(2,1)S(1)}, u32[]{:S(2)}, u32[]{:S(2)}) collective-permute-start(bf16[32,4096]{1,0:T(8,128)(2,1)S(1)} %collective-permute-done.12.refs_0_.refs_12_), channel_id=1, source_target_pairs={{0,2},{1,3},{2,0},{3,1},{4,6},{5,7},{6,4},{7,5},{8,10},{9,11},{10,... | collective-permute-start | bytes 786440 | tf_op jit(solution)/shard_map/ppermute | solution.py:210
  35.4 1.6 %copy-done = bf16[1,2048,512]{2,1,0:T(8,128)(2,1)S(1)} copy-done((bf16[1,2048,512]{2,1,0:T(8,128)(2,1)S(1)}, bf16[1,2048,512]{2,1,0:T(8,128)(2,1)}, u32[]{:S(2)}) %copy-start) | copy-done | bytes 2097176
  37.0 1.6 %copy-done.2 = bf16[1,2048,512]{2,1,0:T(8,128)(2,1)S(1)} copy-done((bf16[1,2048,512]{2,1,0:T(8,128)(2,1)S(1)}, bf16[1,2048,512]{2,1,0:T(8,128)(2,1)}, u32[]{:S(2)}) %copy-start.2) | copy-done | bytes 2097176
  38.6 1.6 %copy-done.4 = bf16[1,512,2048]{2,1,0:T(8,128)(2,1)S(1)} copy-done((bf16[1,512,2048]{2,1,0:T(8,128)(2,1)S(1)}, bf16[1,512,2048]{2,1,0:T(8,128)(2,1)}, u32[]{:S(2)}) %copy-start.4) | copy-done | bytes 2097176
  40.2 2.8 %chunk_backward.4 = (bf16[128,512]{1,0:T(8,128)(2,1)S(1)}, bf16[128,512]{1,0:T(8,128)(2,1)S(1)}, bf16[128,512]{1,0:T(8,128)(2,1)S(1)}, bf16[64,2048]{1,0:T(8,128)(2,1)S(1)}, f32[64,2048]{1,0:T(8,128)S(1)}) custom-call(bf16[32,4096]{1,0:T(8,128)(2,1)S(1)} %get-tuple-element.33.refs_0_, bf16[32,4096]{1,0:T(8,128)(2,1)S(1)} %collective-permute-done.refs_1_, ...), custom_call_target="tpu_custom_call" | custom-call | flops 1342177280 | bytes 6291456 | tf_op jit(solution)/shard_map/chunk_backward/pallas_call | solution.py:102
  43.5 2.8 %collective-permute-done.14.refs_2_.refs_14_ = bf16[32,4096]{1,0:T(8,128)(2,1)S(1)} collective-permute-done((bf16[32,4096]{1,0:T(8,128)(2,1)S(1)}, bf16[32,4096]{1,0:T(8,128)(2,1)S(1)}, u32[]{:S(2)}, u32[]{:S(2)}) %collective-permute-start.14) | collective-permute-done | bytes 262176 | tf_op jit(solution)/shard_map/ppermute | solution.py:210
  47.4 1.6 %collective-permute-done.22.refs_3_.refs_11_ = bf16[32,4096]{1,0:T(8,128)(2,1)S(1)} collective-permute-done((bf16[32,4096]{1,0:T(8,128)(2,1)S(1)}, bf16[32,4096]{1,0:T(8,128)(2,1)S(1)}, u32[]{:S(2)}, u32[]{:S(2)}) %collective-permute-start.22) | collective-permute-done | bytes 262176 | tf_op jit(solution)/shard_map/ppermute | solution.py:210
  49.5 2.8 %chunk_backward.7 = (bf16[128,512]{1,0:T(8,128)(2,1)S(1)}, bf16[128,512]{1,0:T(8,128)(2,1)S(1)}, bf16[128,512]{1,0:T(8,128)(2,1)S(1)}, bf16[64,2048]{1,0:T(8,128)(2,1)S(1)}, f32[64,2048]{1,0:T(8,128)S(1)}) custom-call(bf16[32,4096]{1,0:T(8,128)(2,1)S(1)} %collective-permute-done.19.refs_0_.refs_8_, ...), custom_call_target="tpu_custom_call" | custom-call | flops 1342177280 | bytes 6291456 | tf_op jit(solution)/shard_map/chunk_backward/pallas_call | solution.py:102
  52.4 2.8 %chunk_backward.6 = (bf16[128,512]{1,0:T(8,128)(2,1)S(1)}, bf16[128,512]{1,0:T(8,128)(2,1)S(1)}, bf16[128,512]{1,0:T(8,128)(2,1)S(1)}, bf16[64,2048]{1,0:T(8,128)(2,1)S(1)}, f32[64,2048]{1,0:T(8,128)S(1)}) custom-call(bf16[32,4096]{1,0:T(8,128)(2,1)S(1)} %collective-permute-done.12.refs_0_.refs_12_, ...), custom_call_target="tpu_custom_call" | custom-call | flops 1342177280 | bytes 6291456 | tf_op jit(solution)/shard_map/chunk_backward/pallas_call | solution.py:102
  55.7 2.8 %chunk_backward.5 = (bf16[128,512]{1,0:T(8,128)(2,1)S(1)}, bf16[128,512]{1,0:T(8,128)(2,1)S(1)}, bf16[128,512]{1,0:T(8,128)(2,1)S(1)}, bf16[64,2048]{1,0:T(8,128)(2,1)S(1)}, f32[64,2048]{1,0:T(8,128)S(1)}) custom-call(bf16[32,4096]{1,0:T(8,128)(2,1)S(1)} %collective-permute-done.5.refs_0_.refs_4_, ...), custom_call_target="tpu_custom_call" | custom-call | flops 1342177280 | bytes 6291456 | tf_op jit(solution)/shard_map/chunk_backward/pallas_call | solution.py:102
  58.6 5.4 %weight_grads.1 = (bf16[2048,512]{1,0:T(8,128)(2,1)}, bf16[2048,512]{1,0:T(8,128)(2,1)}, bf16[512,2048]{1,0:T(8,128)(2,1)}) custom-call(bf16[32,4096]{1,0:T(8,128)(2,1)S(1)} %get-tuple-element.33.refs_0_, bf16[32,4096]{1,0:T(8,128)(2,1)S(1)} %collective-permute-done.refs_1_, bf16[32,4096]{1,0:T(8,128)(2,1)S(1)} %collective-permute-done.1.refs_2_, ...), custom_call_target="tpu_custom_call" | custom-call | flops 3221225472 | bytes 6291456 | tf_op jit(solution)/shard_map/weight_grads/pallas_call | solution.py:156
  64.1 1.6 %collective-permute-start.24 = (bf16[32,2048]{1,0:T(8,128)(2,1)S(1)}, bf16[32,2048]{1,0:T(8,128)(2,1)S(1)}, u32[]{:S(2)}, u32[]{:S(2)}) collective-permute-start(bf16[32,2048]{1,0:T(8,128)(2,1)S(1)} %slice.60), channel_id=1, source_target_pairs={{0,2},{1,3},{2,0},{3,1},{4,6},{5,7},{6,4},{7,5},{8,10},{9,11},{10,... | collective-permute-start | bytes 393224 | tf_op jit(solution)/shard_map/ppermute | solution.py:210
  66.4 1.6 %collective-permute-start.10 = (bf16[32,2048]{1,0:T(8,128)(2,1)S(1)}, bf16[32,2048]{1,0:T(8,128)(2,1)S(1)}, u32[]{:S(2)}, u32[]{:S(2)}) collective-permute-start(bf16[32,2048]{1,0:T(8,128)(2,1)S(1)} %slice.62), channel_id=1, source_target_pairs={{0,2},{1,3},{2,0},{3,1},{4,6},{5,7},{6,4},{7,5},{8,10},{9,11},{10,... | collective-permute-start | bytes 393224 | tf_op jit(solution)/shard_map/ppermute | solution.py:210
  68.0 2.5 %collective-permute-done.24 = bf16[32,2048]{1,0:T(8,128)(2,1)S(1)} collective-permute-done((bf16[32,2048]{1,0:T(8,128)(2,1)S(1)}, bf16[32,2048]{1,0:T(8,128)(2,1)S(1)}, u32[]{:S(2)}, u32[]{:S(2)}) %collective-permute-start.24) | collective-permute-done | bytes 131104 | tf_op jit(solution)/shard_map/ppermute | solution.py:210
  70.5 2.1 %collective-permute-start.25 = (bf16[32,2048]{1,0:T(8,128)(2,1)S(1)}, bf16[32,2048]{1,0:T(8,128)(2,1)S(1)}, u32[]{:S(2)}, u32[]{:S(2)}) collective-permute-start(bf16[32,2048]{1,0:T(8,128)(2,1)S(1)} %fusion), channel_id=1, source_target_pairs={{0,12},{4,8},{8,4},{12,0},{1,13},{5,9},{9,5},{13,1},{2,14},{6,10},... | collective-permute-start | bytes 393224 | tf_op jit(solution)/shard_map/ppermute | solution.py:207
  72.6 0.7 collective-permute-done.17
  73.4 2.2 %collective-permute-done.10 = bf16[32,2048]{1,0:T(8,128)(2,1)S(1)} collective-permute-done((bf16[32,2048]{1,0:T(8,128)(2,1)S(1)}, bf16[32,2048]{1,0:T(8,128)(2,1)S(1)}, u32[]{:S(2)}, u32[]{:S(2)}) %collective-permute-start.10) | collective-permute-done | bytes 131104 | tf_op jit(solution)/shard_map/ppermute | solution.py:210
  76.1 2.5 %collective-permute-done.25.refs_3_ = bf16[32,2048]{1,0:T(8,128)(2,1)S(1)} collective-permute-done((bf16[32,2048]{1,0:T(8,128)(2,1)S(1)}, bf16[32,2048]{1,0:T(8,128)(2,1)S(1)}, u32[]{:S(2)}, u32[]{:S(2)}) %collective-permute-start.25) | collective-permute-done | bytes 131104 | tf_op jit(solution)/shard_map/ppermute | solution.py:207
  78.6 4.1 %collective-permute-done.18.refs_2_ = bf16[32,2048]{1,0:T(8,128)(2,1)S(1)} collective-permute-done((bf16[32,2048]{1,0:T(8,128)(2,1)S(1)}, bf16[32,2048]{1,0:T(8,128)(2,1)S(1)}, u32[]{:S(2)}, u32[]{:S(2)}) %collective-permute-start.18) | collective-permute-done | bytes 131104 | tf_op jit(solution)/shard_map/ppermute | solution.py:207
  82.6 1.3 %collective-permute-done.11.refs_1_ = bf16[32,2048]{1,0:T(8,128)(2,1)S(1)} collective-permute-done((bf16[32,2048]{1,0:T(8,128)(2,1)S(1)}, bf16[32,2048]{1,0:T(8,128)(2,1)S(1)}, u32[]{:S(2)}, u32[]{:S(2)}) %collective-permute-start.11) | collective-permute-done | bytes 131104 | tf_op jit(solution)/shard_map/ppermute | solution.py:207
  84.0 1.1 %place_rows.1 = bf16[128,2048]{1,0:T(8,128)(2,1)} custom-call(bf16[128,128]{1,0:T(8,128)(2,1)S(1)} %get-tuple-element.32.back, bf16[32,2048]{1,0:T(8,128)(2,1)S(1)} %fusion.3.refs_0_, bf16[32,2048]{1,0:T(8,128)(2,1)S(1)} %collective-permute-done.11.refs_1_, bf16[32,2048]{1,0:T(8,128)(2,1)S(1)} %collective-permute-done.18.refs_2_, ...), custom_call_target="tpu_custom_call" | custom-call | flops 67108864 | bytes 1048576 | tf_op jit(solution)/shard_map/place_rows/pallas_call | solution.py:185
  (58 shorter events, 5.7 us)
Async XLA Ops:
  4.7 9.3 %collective-permute-start.1 = (bf16[32,4096]{1,0:T(8,128)(2,1)S(1)}, bf16[32,4096]{1,0:T(8,128)(2,1)S(1)}, u32[]{:S(2)}, u32[]{:S(2)}) collective-permute-start(bf16[32,4096]{1,0:T(8,128)(2,1)S(1)} %get-tuple-element.33.refs_0_), channel_id=1, source_target_pairs={{0,2},{1,3},{2,0},{3,1},{4,6},{5,7},{6,4},{7,5},{8,10},{9,11},{10,... | collective-permute-start | bytes 786440 | tf_op jit(solution)/shard_map/ppermute | solution.py:210
  7.7 11.1 %collective-permute-start.19 = (bf16[32,4096]{1,0:T(8,128)(2,1)S(1)}, bf16[32,4096]{1,0:T(8,128)(2,1)S(1)}, u32[]{:S(2)}, u32[]{:S(2)}) collective-permute-start(bf16[32,4096]{1,0:T(8,128)(2,1)S(1)} %get-tuple-element.42), channel_id=1, source_target_pairs={{0,12},{4,8},{8,4},{12,0},{1,13},{5,9},{9,5},{13,1},{2,14},{6,10},... | collective-permute-start | bytes 786440 | tf_op jit(solution)/shard_map/ppermute | solution.py:207
  11.3 12.6 %collective-permute-start.5 = (bf16[32,4096]{1,0:T(8,128)(2,1)S(1)}, bf16[32,4096]{1,0:T(8,128)(2,1)S(1)}, u32[]{:S(2)}, u32[]{:S(2)}) collective-permute-start(bf16[32,4096]{1,0:T(8,128)(2,1)S(1)} %get-tuple-element.36), channel_id=1, source_target_pairs={{0,4},{4,0},{8,12},{12,8},{1,5},{5,1},{9,13},{13,9},{2,6},{6,2},{1... | collective-permute-start | bytes 786440 | tf_op jit(solution)/shard_map/ppermute | solution.py:207
  11.3 22.0 %collective-permute-start.12 = (bf16[32,4096]{1,0:T(8,128)(2,1)S(1)}, bf16[32,4096]{1,0:T(8,128)(2,1)S(1)}, u32[]{:S(2)}, u32[]{:S(2)}) collective-permute-start(bf16[32,4096]{1,0:T(8,128)(2,1)S(1)} %get-tuple-element.39), channel_id=1, source_target_pairs={{0,8},{4,12},{8,0},{12,4},{1,9},{5,13},{9,1},{13,5},{2,10},{6,14},... | collective-permute-start | bytes 786440 | tf_op jit(solution)/shard_map/ppermute | solution.py:207
  12.1 21.8 %collective-permute-start = (bf16[32,4096]{1,0:T(8,128)(2,1)S(1)}, bf16[32,4096]{1,0:T(8,128)(2,1)S(1)}, u32[]{:S(2)}, u32[]{:S(2)}) collective-permute-start(bf16[32,4096]{1,0:T(8,128)(2,1)S(1)} %get-tuple-element.33.refs_0_), channel_id=1, source_target_pairs={{0,1},{1,0},{2,3},{3,2},{4,5},{5,4},{6,7},{7,6},{8,9},{9,8},{10,11... | collective-permute-start | bytes 786440 | tf_op jit(solution)/shard_map/ppermute | solution.py:210
  14.0 21.4 %collective-permute-start.2 = (bf16[32,4096]{1,0:T(8,128)(2,1)S(1)}, bf16[32,4096]{1,0:T(8,128)(2,1)S(1)}, u32[]{:S(2)}, u32[]{:S(2)}) collective-permute-start(bf16[32,4096]{1,0:T(8,128)(2,1)S(1)} %collective-permute-done.1.refs_2_), channel_id=1, source_target_pairs={{0,1},{1,0},{2,3},{3,2},{4,5},{5,4},{6,7},{7,6},{8,9},{9,8},{10,11... | collective-permute-start | bytes 786440 | tf_op jit(solution)/shard_map/ppermute | solution.py:210
  18.8 27.5 %collective-permute-start.21 = (bf16[32,4096]{1,0:T(8,128)(2,1)S(1)}, bf16[32,4096]{1,0:T(8,128)(2,1)S(1)}, u32[]{:S(2)}, u32[]{:S(2)}) collective-permute-start(bf16[32,4096]{1,0:T(8,128)(2,1)S(1)} %collective-permute-done.19.refs_0_.refs_8_), channel_id=1, source_target_pairs={{0,2},{1,3},{2,0},{3,1},{4,6},{5,7},{6,4},{7,5},{8,10},{9,11},{10,... | collective-permute-start | bytes 786440 | tf_op jit(solution)/shard_map/ppermute | solution.py:210
  23.9 22.9 %collective-permute-start.20 = (bf16[32,4096]{1,0:T(8,128)(2,1)S(1)}, bf16[32,4096]{1,0:T(8,128)(2,1)S(1)}, u32[]{:S(2)}, u32[]{:S(2)}) collective-permute-start(bf16[32,4096]{1,0:T(8,128)(2,1)S(1)} %collective-permute-done.19.refs_0_.refs_8_), channel_id=1, source_target_pairs={{0,1},{1,0},{2,3},{3,2},{4,5},{5,4},{6,7},{7,6},{8,9},{9,8},{10,11... | collective-permute-start | bytes 786440 | tf_op jit(solution)/shard_map/ppermute | solution.py:210
  33.3 9.7 %collective-permute-start.7 = (bf16[32,4096]{1,0:T(8,128)(2,1)S(1)}, bf16[32,4096]{1,0:T(8,128)(2,1)S(1)}, u32[]{:S(2)}, u32[]{:S(2)}) collective-permute-start(bf16[32,4096]{1,0:T(8,128)(2,1)S(1)} %collective-permute-done.5.refs_0_.refs_4_), channel_id=1, source_target_pairs={{0,2},{1,3},{2,0},{3,1},{4,6},{5,7},{6,4},{7,5},{8,10},{9,11},{10,... | collective-permute-start | bytes 786440 | tf_op jit(solution)/shard_map/ppermute | solution.py:210
  33.9 12.4 %collective-permute-start.14 = (bf16[32,4096]{1,0:T(8,128)(2,1)S(1)}, bf16[32,4096]{1,0:T(8,128)(2,1)S(1)}, u32[]{:S(2)}, u32[]{:S(2)}) collective-permute-start(bf16[32,4096]{1,0:T(8,128)(2,1)S(1)} %collective-permute-done.12.refs_0_.refs_12_), channel_id=1, source_target_pairs={{0,2},{1,3},{2,0},{3,1},{4,6},{5,7},{6,4},{7,5},{8,10},{9,11},{10,... | collective-permute-start | bytes 786440 | tf_op jit(solution)/shard_map/ppermute | solution.py:210
  35.4 1.6 %copy-start = (bf16[1,2048,512]{2,1,0:T(8,128)(2,1)S(1)}, bf16[1,2048,512]{2,1,0:T(8,128)(2,1)}, u32[]{:S(2)}) copy-start(bf16[1,2048,512]{2,1,0:T(8,128)(2,1)} %param.11) | copy-start | bytes 6291460
  37.0 1.6 %copy-start.2 = (bf16[1,2048,512]{2,1,0:T(8,128)(2,1)S(1)}, bf16[1,2048,512]{2,1,0:T(8,128)(2,1)}, u32[]{:S(2)}) copy-start(bf16[1,2048,512]{2,1,0:T(8,128)(2,1)} %param.12) | copy-start | bytes 6291460
  38.6 1.6 %copy-start.4 = (bf16[1,512,2048]{2,1,0:T(8,128)(2,1)S(1)}, bf16[1,512,2048]{2,1,0:T(8,128)(2,1)}, u32[]{:S(2)}) copy-start(bf16[1,512,2048]{2,1,0:T(8,128)(2,1)} %param.13) | copy-start | bytes 6291460
  40.1 9.3 %copy-start.1 = (bf16[1,2048,512]{2,1,0:T(8,128)(2,1)S(1)}, bf16[1,2048,512]{2,1,0:T(8,128)(2,1)}, u32[]{:S(2)}) copy-start(bf16[1,2048,512]{2,1,0:T(8,128)(2,1)} %param.11) | copy-start | bytes 6291460
  40.1 9.3 %copy-start.3 = (bf16[1,2048,512]{2,1,0:T(8,128)(2,1)S(1)}, bf16[1,2048,512]{2,1,0:T(8,128)(2,1)}, u32[]{:S(2)}) copy-start(bf16[1,2048,512]{2,1,0:T(8,128)(2,1)} %param.12) | copy-start | bytes 6291460
  40.2 9.3 %copy-start.5 = (bf16[1,512,2048]{2,1,0:T(8,128)(2,1)S(1)}, bf16[1,512,2048]{2,1,0:T(8,128)(2,1)}, u32[]{:S(2)}) copy-start(bf16[1,512,2048]{2,1,0:T(8,128)(2,1)} %param.13) | copy-start | bytes 6291460
  42.9 3.9 %collective-permute-start.3 = (bf16[64,2048]{1,0:T(8,128)(2,1)S(1)}, bf16[64,2048]{1,0:T(8,128)(2,1)S(1)}, u32[]{:S(2)}, u32[]{:S(2)}) collective-permute-start(bf16[64,2048]{1,0:T(8,128)(2,1)S(1)} %get-tuple-element.35), channel_id=1, source_target_pairs={{0,1},{1,0},{2,3},{3,2},{4,5},{5,4},{6,7},{7,6},{8,9},{9,8},{10,11... | collective-permute-start | bytes 786440 | tf_op jit(solution)/shard_map/ppermute | solution.py:210
  43.0 12.7 %collective-permute-start.6 = (bf16[32,4096]{1,0:T(8,128)(2,1)S(1)}, bf16[32,4096]{1,0:T(8,128)(2,1)S(1)}, u32[]{:S(2)}, u32[]{:S(2)}) collective-permute-start(bf16[32,4096]{1,0:T(8,128)(2,1)S(1)} %collective-permute-done.5.refs_0_.refs_4_), channel_id=1, source_target_pairs={{0,1},{1,0},{2,3},{3,2},{4,5},{5,4},{6,7},{7,6},{8,9},{9,8},{10,11... | collective-permute-start | bytes 786440 | tf_op jit(solution)/shard_map/ppermute | solution.py:210
  46.3 6.0 %collective-permute-start.13 = (bf16[32,4096]{1,0:T(8,128)(2,1)S(1)}, bf16[32,4096]{1,0:T(8,128)(2,1)S(1)}, u32[]{:S(2)}, u32[]{:S(2)}) collective-permute-start(bf16[32,4096]{1,0:T(8,128)(2,1)S(1)} %collective-permute-done.12.refs_0_.refs_12_), channel_id=1, source_target_pairs={{0,1},{1,0},{2,3},{3,2},{4,5},{5,4},{6,7},{7,6},{8,9},{9,8},{10,11... | collective-permute-start | bytes 786440 | tf_op jit(solution)/shard_map/ppermute | solution.py:210
  46.3 9.4 %collective-permute-start.8 = (bf16[32,4096]{1,0:T(8,128)(2,1)S(1)}, bf16[32,4096]{1,0:T(8,128)(2,1)S(1)}, u32[]{:S(2)}, u32[]{:S(2)}) collective-permute-start(bf16[32,4096]{1,0:T(8,128)(2,1)S(1)} %collective-permute-done.7.refs_2_.refs_6_), channel_id=1, source_target_pairs={{0,1},{1,0},{2,3},{3,2},{4,5},{5,4},{6,7},{7,6},{8,9},{9,8},{10,11... | collective-permute-start | bytes 786440 | tf_op jit(solution)/shard_map/ppermute | solution.py:210
  46.8 5.6 %collective-permute-start.15 = (bf16[32,4096]{1,0:T(8,128)(2,1)S(1)}, bf16[32,4096]{1,0:T(8,128)(2,1)S(1)}, u32[]{:S(2)}, u32[]{:S(2)}) collective-permute-start(bf16[32,4096]{1,0:T(8,128)(2,1)S(1)} %collective-permute-done.14.refs_2_.refs_14_), channel_id=1, source_target_pairs={{0,1},{1,0},{2,3},{3,2},{4,5},{5,4},{6,7},{7,6},{8,9},{9,8},{10,11... | collective-permute-start | bytes 786440 | tf_op jit(solution)/shard_map/ppermute | solution.py:210
  46.9 2.1 %collective-permute-start.22 = (bf16[32,4096]{1,0:T(8,128)(2,1)S(1)}, bf16[32,4096]{1,0:T(8,128)(2,1)S(1)}, u32[]{:S(2)}, u32[]{:S(2)}) collective-permute-start(bf16[32,4096]{1,0:T(8,128)(2,1)S(1)} %collective-permute-done.21.refs_2_.refs_10_), channel_id=1, source_target_pairs={{0,1},{1,0},{2,3},{3,2},{4,5},{5,4},{6,7},{7,6},{8,9},{9,8},{10,11... | collective-permute-start | bytes 786440 | tf_op jit(solution)/shard_map/ppermute | solution.py:210
  48.9 27.1 %collective-permute-start.4 = (bf16[32,2048]{1,0:T(8,128)(2,1)S(1)}, bf16[32,2048]{1,0:T(8,128)(2,1)S(1)}, u32[]{:S(2)}, u32[]{:S(2)}) collective-permute-start(bf16[32,2048]{1,0:T(8,128)(2,1)S(1)} %slice.63), channel_id=1, source_target_pairs={{0,2},{1,3},{2,0},{3,1},{4,6},{5,7},{6,4},{7,5},{8,10},{9,11},{10,... | collective-permute-start | bytes 393224 | tf_op jit(solution)/shard_map/ppermute | solution.py:210
  52.3 11.7 %collective-permute-start.23 = (bf16[64,2048]{1,0:T(8,128)(2,1)S(1)}, bf16[64,2048]{1,0:T(8,128)(2,1)S(1)}, u32[]{:S(2)}, u32[]{:S(2)}) collective-permute-start(bf16[64,2048]{1,0:T(8,128)(2,1)S(1)} %get-tuple-element.44), channel_id=1, source_target_pairs={{0,1},{1,0},{2,3},{3,2},{4,5},{5,4},{6,7},{7,6},{8,9},{9,8},{10,11... | collective-permute-start | bytes 786440 | tf_op jit(solution)/shard_map/ppermute | solution.py:210
  55.2 10.5 %collective-permute-start.16 = (bf16[64,2048]{1,0:T(8,128)(2,1)S(1)}, bf16[64,2048]{1,0:T(8,128)(2,1)S(1)}, u32[]{:S(2)}, u32[]{:S(2)}) collective-permute-start(bf16[64,2048]{1,0:T(8,128)(2,1)S(1)} %get-tuple-element.41), channel_id=1, source_target_pairs={{0,1},{1,0},{2,3},{3,2},{4,5},{5,4},{6,7},{7,6},{8,9},{9,8},{10,11... | collective-permute-start | bytes 786440 | tf_op jit(solution)/shard_map/ppermute | solution.py:210
  58.5 7.8 %collective-permute-start.9 = (bf16[64,2048]{1,0:T(8,128)(2,1)S(1)}, bf16[64,2048]{1,0:T(8,128)(2,1)S(1)}, u32[]{:S(2)}, u32[]{:S(2)}) collective-permute-start(bf16[64,2048]{1,0:T(8,128)(2,1)S(1)} %get-tuple-element.38), channel_id=1, source_target_pairs={{0,1},{1,0},{2,3},{3,2},{4,5},{5,4},{6,7},{7,6},{8,9},{9,8},{10,11... | collective-permute-start | bytes 786440 | tf_op jit(solution)/shard_map/ppermute | solution.py:210
  64.1 6.4 %collective-permute-start.24 = (bf16[32,2048]{1,0:T(8,128)(2,1)S(1)}, bf16[32,2048]{1,0:T(8,128)(2,1)S(1)}, u32[]{:S(2)}, u32[]{:S(2)}) collective-permute-start(bf16[32,2048]{1,0:T(8,128)(2,1)S(1)} %slice.60), channel_id=1, source_target_pairs={{0,2},{1,3},{2,0},{3,1},{4,6},{5,7},{6,4},{7,5},{8,10},{9,11},{10,... | collective-permute-start | bytes 393224 | tf_op jit(solution)/shard_map/ppermute | solution.py:210
  65.7 7.5 %collective-permute-start.17 = (bf16[32,2048]{1,0:T(8,128)(2,1)S(1)}, bf16[32,2048]{1,0:T(8,128)(2,1)S(1)}, u32[]{:S(2)}, u32[]{:S(2)}) collective-permute-start(bf16[32,2048]{1,0:T(8,128)(2,1)S(1)} %slice.61), channel_id=1, source_target_pairs={{0,2},{1,3},{2,0},{3,1},{4,6},{5,7},{6,4},{7,5},{8,10},{9,11},{10,... | collective-permute-start | bytes 393224 | tf_op jit(solution)/shard_map/ppermute | solution.py:210
  66.4 9.2 %collective-permute-start.10 = (bf16[32,2048]{1,0:T(8,128)(2,1)S(1)}, bf16[32,2048]{1,0:T(8,128)(2,1)S(1)}, u32[]{:S(2)}, u32[]{:S(2)}) collective-permute-start(bf16[32,2048]{1,0:T(8,128)(2,1)S(1)} %slice.62), channel_id=1, source_target_pairs={{0,2},{1,3},{2,0},{3,1},{4,6},{5,7},{6,4},{7,5},{8,10},{9,11},{10,... | collective-permute-start | bytes 393224 | tf_op jit(solution)/shard_map/ppermute | solution.py:210
  70.5 8.1 %collective-permute-start.25 = (bf16[32,2048]{1,0:T(8,128)(2,1)S(1)}, bf16[32,2048]{1,0:T(8,128)(2,1)S(1)}, u32[]{:S(2)}, u32[]{:S(2)}) collective-permute-start(bf16[32,2048]{1,0:T(8,128)(2,1)S(1)} %fusion), channel_id=1, source_target_pairs={{0,12},{4,8},{8,4},{12,0},{1,13},{5,9},{9,5},{13,1},{2,14},{6,10},... | collective-permute-start | bytes 393224 | tf_op jit(solution)/shard_map/ppermute | solution.py:207
  73.3 9.3 %collective-permute-start.18 = (bf16[32,2048]{1,0:T(8,128)(2,1)S(1)}, bf16[32,2048]{1,0:T(8,128)(2,1)S(1)}, u32[]{:S(2)}, u32[]{:S(2)}) collective-permute-start(bf16[32,2048]{1,0:T(8,128)(2,1)S(1)} %fusion.1), channel_id=1, source_target_pairs={{0,8},{4,12},{8,0},{12,4},{1,9},{5,13},{9,1},{13,5},{2,10},{6,14},... | collective-permute-start | bytes 393224 | tf_op jit(solution)/shard_map/ppermute | solution.py:207
  75.6 8.3 %collective-permute-start.11 = (bf16[32,2048]{1,0:T(8,128)(2,1)S(1)}, bf16[32,2048]{1,0:T(8,128)(2,1)S(1)}, u32[]{:S(2)}, u32[]{:S(2)}) collective-permute-start(bf16[32,2048]{1,0:T(8,128)(2,1)S(1)} %fusion.2), channel_id=1, source_target_pairs={{0,4},{4,0},{8,12},{12,8},{1,5},{5,1},{9,13},{13,9},{2,6},{6,2},{1... | collective-permute-start | bytes 393224 | tf_op jit(solution)/shard_map/ppermute | solution.py:207
  (3 other events, 2.7 us)

commit v2 on v1

v2 whole, which is shorter than its diff:
```python
import functools

import jax
import jax.numpy as jnp
from jax import lax
from jax.experimental import pallas as pl
from jax.experimental.pallas import tpu as pltpu
from jax.sharding import PartitionSpec as P

BF16 = jnp.bfloat16
F32 = jnp.float32
GROUPS = 4
VMEM = pl.BlockSpec(memory_space=pltpu.VMEM)
ANY = pl.BlockSpec(memory_space=pl.ANY)
HBM = pl.BlockSpec(memory_space=pltpu.HBM)
NT = (((1,), (1,)), ((), ()))
TN = (((0,), (0,)), ((), ()))
PIECES = [[(0, 0, 2), (1, 0, 2), (3, 0, 2)], [(2, 0, 2)]]
RETURNS = [[(3, 0, 2)], [(0, 0, 2), (1, 0, 2)], [(2, 0, 2)]]
PARTS = 2
CUTS = (1, 1)
GATED = True


def params(mib):
    return pltpu.CompilerParams(vmem_limit_bytes=mib * 1024 * 1024)


def cost(flops, moved):
    return pl.CostEstimate(flops=flops, bytes_accessed=moved, transcendentals=0)


def in_hbm(a):
    return pltpu.with_memory_space_constraint(a, pltpu.HBM)


def pass_kernel(*refs):
    del refs


def after(a, *others):
    return pl.pallas_call(
        pass_kernel,
        out_shape=jax.ShapeDtypeStruct(a.shape, a.dtype),
        in_specs=[ANY] * (1 + len(others)),
        out_specs=ANY,
        input_output_aliases={0: 0},
        compiler_params=params(1),
        cost_estimate=cost(0, 0),
        name="after",
    )(a, *others)


def select_kernel(slot_cap, spans, tokens, grad_out, routes, order, *refs):
    sends, back = refs[: len(spans)], refs[len(spans)]
    xs, ys, route_in, order_in, sems = refs[len(spans) + 1 :]
    small = [
        pltpu.make_async_copy(routes, route_in, sems.at[0]),
        pltpu.make_async_copy(order, order_in, sems.at[1]),
    ]
    large = [
        pltpu.make_async_copy(tokens, xs, sems.at[2]),
        pltpu.make_async_copy(grad_out, ys, sems.at[3]),
    ]
    for copy in small + large:
        copy.start()
    count, width = tokens.shape
    rows = lax.broadcasted_iota(jnp.int32, (count, count), 0)
    lanes = lax.broadcasted_iota(jnp.int32, (count, count), 1)
    eye = rows == lanes
    me = lax.axis_index("expert")
    for copy in small:
        copy.wait()
    route_row = route_in[...]
    order_row = order_in[...]
    route_col = jnp.sum(jnp.where(eye, route_row, 0), axis=1, keepdims=True)
    order_col = jnp.sum(jnp.where(eye, order_row, 0), axis=1, keepdims=True)
    ahead = (route_col == route_row) & (order_col < order_row)
    rank = jnp.sum(ahead.astype(jnp.int32), axis=0, keepdims=True)
    place = jnp.bitwise_xor(route_row, me) * slot_cap + rank
    place = jnp.where(rank < slot_cap, place, -1)
    select = (rows == place).astype(F32).astype(BF16)
    place_col = jnp.sum(jnp.where(eye, place, 0), axis=1, keepdims=True)
    back[...] = (lanes == place_col).astype(F32).astype(BF16)
    for half, copy in enumerate(large):
        copy.wait()
        moved = jnp.dot(select, (xs, ys)[half][...], preferred_element_type=F32).astype(BF16)
        for send, (low, high) in zip(sends, spans):
            send[:, half * width : (half + 1) * width] = moved[low:high]


def select_rows(tokens, grad_out, routes, order, slot_cap, spans):
    count, width = tokens.shape
    return pl.pallas_call(
        functools.partial(select_kernel, slot_cap, spans),
        out_shape=[jax.ShapeDtypeStruct((high - low, 2 * width), BF16) for low, high in spans]
        + [jax.ShapeDtypeStruct((count, count), BF16)],
        in_specs=[HBM] * 4,
        out_specs=[VMEM] * (len(spans) + 1),
        scratch_shapes=[pltpu.VMEM((count, width), BF16)] * 2
        + [pltpu.VMEM((1, count), jnp.int32)] * 2
        + [pltpu.SemaphoreType.DMA((4,))],
        compiler_params=params(16),
        cost_estimate=cost(4 * count * count * width, 8 * count * width),
        name="select_rows",
    )(*map(in_hbm, (tokens, grad_out, routes.reshape(1, count), order)))


def load_kernel(n, *refs):
    sources, targets, sems = refs[:n], refs[n + 1 : 2 * n + 1], refs[-1]
    copies = [pltpu.make_async_copy(s, t, sems.at[i]) for i, (s, t) in enumerate(zip(sources, targets))]
    for copy in copies:
        copy.start()
    for copy in copies:
        copy.wait()


def load_weights(weights, passed):
    n = len(weights)
    return pl.pallas_call(
        functools.partial(load_kernel, n),
        out_shape=[jax.ShapeDtypeStruct(a.shape, a.dtype) for a in (*weights, passed)],
        in_specs=[HBM] * n + [ANY],
        out_specs=[VMEM] * n + [ANY],
        scratch_shapes=[pltpu.SemaphoreType.DMA((n,))],
        input_output_aliases={n: n},
        compiler_params=params(2),
        cost_estimate=cost(0, 0),
        name="load_weights",
    )(*map(in_hbm, weights), passed)


def sides(blocks, width):
    left, right, parts = [], [], []
    for block in blocks:
        step = block.shape[1]
        if step == 2 * width:
            left.append(block[:, :width])
            right.append(block[:, width:])
            continue
        parts.append(block[...])
        if len(parts) * step == width:
            side = left if len(left) == len(right) else right
            side.append(parts[0] if len(parts) == 1 else jnp.concatenate(parts, axis=1))
            parts = []
    return left, right


def chunk_kernel(n, *refs):
    blocks = refs[:n]
    gate_w, up_w, down_w = refs[n : n + 3]
    hidden_out, pair_out, away_out, keep_out = refs[-4:]
    width = gate_w.shape[0]
    units = gate_w.shape[1]
    count = keep_out.shape[0]
    inputs, cotangent = (jnp.concatenate(side, axis=0) for side in sides(blocks, width))
    gate = jnp.dot(inputs, gate_w[...], preferred_element_type=F32)
    upper = jnp.dot(inputs, up_w[...], preferred_element_type=F32)
    sig = jax.nn.sigmoid(gate)
    active = gate * sig
    slope = sig * (1.0 + gate * (1.0 - sig))
    hidden_out[...] = (active * upper).astype(BF16)
    grad_hidden = lax.dot_general(cotangent, down_w[...], NT, preferred_element_type=F32)
    grad_upper = (grad_hidden * active).astype(BF16)
    grad_gated = (grad_hidden * upper * slope).astype(BF16)
    pair_out[:, :units] = grad_gated
    pair_out[:, units:] = grad_upper
    back = lax.dot_general(grad_gated, gate_w[...], NT, preferred_element_type=F32)
    back = back + lax.dot_general(grad_upper, up_w[...], NT, preferred_element_type=F32)
    keep_out[...] = back[:count]
    away_out[...] = back[count:].astype(BF16)


def chunk_backward(blocks, gate_w, up_w, down_w, *before):
    width, units = gate_w.shape
    count = sum(block.size for block in blocks) // (4 * width)
    return pl.pallas_call(
        functools.partial(chunk_kernel, len(blocks)),
        out_shape=[
            jax.ShapeDtypeStruct((2 * count, units), BF16),
            jax.ShapeDtypeStruct((2 * count, 2 * units), BF16),
            jax.ShapeDtypeStruct((count, width), BF16),
            jax.ShapeDtypeStruct((count, width), F32),
        ],
        in_specs=[VMEM] * (len(blocks) + 3) + [ANY] * len(before),
        out_specs=[VMEM] * 4,
        compiler_params=params(24),
        cost_estimate=cost(20 * count * width * units, 6 * width * units),
        name="chunk_backward",
    )(*blocks, gate_w, up_w, down_w, *before)


def gather_pieces(values, scratch):
    at = 0
    for value in values:
        scratch[at : at + value.shape[0]] = value
        at += value.shape[0]


def pair_kernel(n, *refs):
    blocks, pairs = refs[: -5 - n], refs[-5 - n : -5]
    gate_out, up_out, xs, ps = refs[-4:]
    step = pl.program_id(0)
    units = gate_out.shape[1]

    @pl.when(step == 0)
    def _():
        gather_pieces(sides(blocks, xs.shape[1])[0], xs)
        gather_pieces([pair[...] for pair in pairs], ps)

    part = gate_out.shape[0]
    inputs = xs[:, pl.ds(pl.multiple_of(step * part, part), part)]
    both = lax.dot_general(inputs, ps[...], TN, preferred_element_type=F32).astype(BF16)
    gate_out[...] = both[:, :units]
    up_out[...] = both[:, units:]


def down_kernel(n, *refs):
    blocks, hidden = refs[: -5 - n], refs[-5 - n : -5]
    down_out, mark, ys, hs = refs[-4:]
    step = pl.program_id(0)

    @pl.when(step == 0)
    def _():
        gather_pieces(sides(blocks, ys.shape[1])[1], ys)
        gather_pieces([part[...] for part in hidden], hs)
        mark[...] = jnp.zeros_like(mark)

    part = down_out.shape[1]
    cotangent = ys[:, pl.ds(pl.multiple_of(step * part, part), part)]
    down_out[...] = lax.dot_general(hs[...], cotangent, TN, preferred_element_type=F32).astype(BF16)


def whole(a):
    return pl.BlockSpec(a.shape, lambda i: (0, 0))


def pair_grads(blocks, pairs, width, units, before):
    total = sum(a.size for a in blocks) // (2 * width)
    steps = 4
    return pl.pallas_call(
        functools.partial(pair_kernel, len(pairs)),
        grid=(steps,),
        out_shape=[jax.ShapeDtypeStruct((width, units), BF16)] * 2,
        in_specs=[whole(a) for a in (*blocks, *pairs)] + [ANY],
        out_specs=[pl.BlockSpec((width // steps, units), lambda i: (i, 0))] * 2,
        scratch_shapes=[pltpu.VMEM((total, width), BF16), pltpu.VMEM((total, 2 * units), BF16)],
        compiler_params=params(32),
        cost_estimate=cost(4 * total * width * units, 4 * width * units),
        name="pair_grads",
    )(*blocks, *pairs, before)


def down_grads(blocks, hidden, width, units, before):
    total = sum(a.size for a in blocks) // (2 * width)
    steps = 4
    return pl.pallas_call(
        functools.partial(down_kernel, len(hidden)),
        grid=(steps,),
        out_shape=[jax.ShapeDtypeStruct((units, width), BF16), jax.ShapeDtypeStruct((8, 128), F32)],
        in_specs=[whole(a) for a in (*blocks, *hidden)] + [ANY],
        out_specs=[
            pl.BlockSpec((units, width // steps), lambda i: (0, i)),
            pl.BlockSpec((8, 128), lambda i: (0, 0)),
        ],
        scratch_shapes=[pltpu.VMEM((total, width), BF16), pltpu.VMEM((total, units), BF16)],
        compiler_params=params(32),
        cost_estimate=cost(2 * total * width * units, 2 * width * units),
        name="down_grads",
    )(*blocks, *hidden, before)


def place_kernel(back, *refs):
    units, out = refs[:-1], refs[-1]
    rows = jnp.concatenate([unit[...] for unit in units], axis=0)
    out[...] = jnp.dot(back[...], rows, preferred_element_type=F32).astype(BF16)


def place_rows(back, units):
    count, width = back.shape[0], units[0].shape[1]
    return pl.pallas_call(
        place_kernel,
        out_shape=jax.ShapeDtypeStruct((count, width), BF16),
        in_specs=[VMEM] * (1 + len(units)),
        out_specs=VMEM,
        compiler_params=params(16),
        cost_estimate=cost(2 * count * count * width, 4 * count * width),
        name="place_rows",
    )(back, *units)


def on_device(tokens, grad_out, routes, order, w_gate, w_up, w_down):
    experts = lax.axis_size("expert")
    shards = lax.axis_size("et")
    local_tokens, width = tokens.shape
    slot_cap = local_tokens // experts
    rows = local_tokens // GROUPS

    def over_expert(a, k):
        if k == 0:
            return a
        return lax.ppermute(a, "expert", [(i, i ^ k) for i in range(experts)])

    def over_et(a, m):
        return lax.ppermute(a, "et", [(i, i ^ m) for i in range(shards)])

    def span(unit):
        group, first, parts = unit
        low = group * rows + first * rows // PARTS
        return low, low + parts * rows // PARTS

    def exchange(a, unit):
        low, high = span(unit)
        pieces = []
        at = low
        while at < high:
            k = at // slot_cap
            end = min(high, (k + 1) * slot_cap)
            whole_unit = (at, end) == (low, high)
            pieces.append(over_expert(a if whole_unit else a[at - low : end - low], k))
            at = end
        return pieces[0] if len(pieces) == 1 else jnp.concatenate(pieces, axis=0)

    units = [unit for piece in PIECES for unit in piece]
    spans = [span(unit) for unit in units]
    *sends, back = select_rows(tokens, grad_out, routes, order, slot_cap, spans)
    sends = dict(zip(units, sends))

    arrived = {}
    for unit in units:
        arrived[unit] = exchange(sends[unit], unit)

    hidden_units = w_gate.shape[2]
    weights = None
    blocks, hidden, pairs, kept, returned = [], [], [], {}, {}
    before = []
    for step, piece in enumerate(PIECES):
        last = step == len(PIECES) - 1
        near, far = [], []
        for unit in piece:
            mine = [arrived[unit]]
            for m in range(2, shards, 2):
                mine.append(over_et(arrived[unit], m))
            if weights is None:
                *weights, mine[-1] = load_weights([w_gate[0], w_up[0], w_down[0]], mine[-1])
            if GATED and last:
                mine[-1] = after(mine[-1], *before)
            near += mine
        size = 2 * width // CUTS[step]
        far = [over_et(a[:, at : at + size], 1) for a in near for at in range(0, 2 * width, size)]
        h, pair, away, keep = chunk_backward(near + far, *weights, *before)
        before = [away]
        blocks += near + far
        hidden.append(h)
        pairs.append(pair)
        many = keep.shape[0] // len(piece)
        for i, unit in enumerate(piece):
            kept[unit] = keep[i * many : (i + 1) * many], away[i * many : (i + 1) * many]
    for group in RETURNS:
        last = group is RETURNS[-1]
        ways = shards // 2
        away = [kept[unit][1] for unit in group]
        got = over_et(away[0] if len(away) == 1 else jnp.concatenate(away, axis=0), 1).astype(F32)
        own, sent = [], [[] for _ in range(ways - 1)]
        at = 0
        for unit in group:
            keep = kept[unit][0]
            summed = keep + got[at : at + keep.shape[0]]
            at += keep.shape[0]
            many = keep.shape[0] // ways
            own.append(summed[:many])
            for w in range(1, ways):
                sent[w - 1].append(summed[w * many : (w + 1) * many].astype(BF16))
        own = jnp.concatenate(own, axis=0)
        for w, part in enumerate(sent, 1):
            part = jnp.concatenate(part, axis=0)
            own = own + over_et(part, 2 * w).astype(F32)
        own = own.astype(BF16)
        if last:
            down_grad, mark = down_grads(blocks, hidden, width, hidden_units, part)
            own = after(own, mark)
            gate_grad, up_grad = pair_grads(blocks, pairs, width, hidden_units, mark)
        at = 0
        for unit in group:
            low, high = span(unit)
            returned[unit] = exchange(own if len(group) == 1 else own[at : at + high - low], unit)
            at += high - low
    grad_tokens = place_rows(back, [returned[unit] for unit in sorted(units)])
    return grad_tokens, gate_grad[None], up_grad[None], down_grad[None]


def solution(mesh):
    return jax.shard_map(
        on_device,
        mesh=mesh,
        in_specs=(
            P(("groups", "expert", "et"), None),
            P(("groups", "expert", "et"), None),
            P(("groups", "expert", "et"), None),
            P(("groups", "expert", "et"), None),
            P("expert", None, "et"),
            P("expert", None, "et"),
            P("expert", "et", None),
        ),
        out_specs=(
            P(("groups", "expert", "et"), None),
            P(("groups", "expert"), None, "et"),
            P(("groups", "expert"), None, "et"),
            P(("groups", "expert"), "et", None),
        ),
        check_vma=False,
    )
```

time: 85.4 us -> 68.2 us (0.80)
  waiting for transfers between devices: 38.6 us -> 21.5 us
  local copies, waits for them, and re-layouts: 8.34 us -> 0.18 us
  starting transfers between devices: 18.8 us -> 25 us
  Pallas kernels: 18.2 us -> 20.2 us
    ppermute x6, waiting for transfers between devices: 26.9 us -> 15.4 us  [over_expert(): return lax.ppermute(a, 'expert', [(i, i ^ k) for i in range(experts)])]
    unnamed x19 -> x0, local copies, waits for them, and re-layouts: 8.28 us -> none
    ppermute x6, starting transfers between devices: 6.97 us -> 12.7 us  [over_expert(): return lax.ppermute(a, 'expert', [(i, i ^ k) for i in range(experts)])]
    ppermute x20 -> x18, waiting for transfers between devices: 11.7 us -> 6.08 us  [over_et(): return lax.ppermute(a, 'et', [(i, i ^ m) for i in range(shards)])]
    pallas_call x6 -> x8, Pallas kernels: 17.1 us -> 19.1 us  [the longest x2 7.25 us: chunk_backward(): pl.pallas_call(functools.partial(chunk_kernel, len(blocks)), out_shape=[j...]
    ppermute x20 -> x18, starting transfers between devices: 11.9 us -> 12.2 us  [over_et(): return lax.ppermute(a, 'et', [(i, i ^ m) for i in range(shards)])]
  transfers between devices with their start and end apart: 26 -> 24, of which waited for: 12 -> 10; matrix products, arithmetic and copies ran while one was open for 0% -> 1% of each run, Pallas kernels for 19% -> 26%
where the time goes in v2:
time: 68.2 us; the launch traced here: 68.1 us
  starting transfers between devices  25 us (37%)
  waiting for transfers between devices  21.5 us (32%)
  Pallas kernels  20.2 us (30%)
  between operations  0.82 us (1%)
    ppermute x6, waiting for transfers between devices, over_expert(): return lax.ppermute(a, 'expert', [(i, i ^ k) for i in range(experts)])  15.4 us
    ppermute x6, starting transfers between devices, over_expert(): return lax.ppermute(a, 'expert', [(i, i ^ k) for i in range(experts)])  12.7 us
    ppermute x18, starting transfers between devices, over_et(): return lax.ppermute(a, 'et', [(i, i ^ m) for i in range(shards)])  12.2 us
    pallas_call x2, Pallas kernels, chunk_backward(): pl.pallas_call(functools.partial(chunk_kernel, len(blocks)), out_shape=[j...  7.25 us
    ppermute x18, waiting for transfers between devices, over_et(): return lax.ppermute(a, 'et', [(i, i ^ m) for i in range(shards)])  6.08 us
    pallas_call x1, Pallas kernels, pair_grads(): pl.pallas_call(functools.partial(pair_kernel, len(pairs)), grid=(steps,),...  4.07 us
    pallas_call x1, Pallas kernels, down_grads(): pl.pallas_call(functools.partial(down_kernel, len(hidden)), grid=(steps,)...  3.19 us
    pallas_call x1, Pallas kernels, load_weights(): pl.pallas_call(functools.partial(load_kernel, n), out_shape=[jax.ShapeDty...  2.88 us
  transfers between devices with their start and end apart: 24, of which 10 were waited for; matrix products, arithmetic and copies ran while one was open for 1% of the time, Pallas kernels for 26%

profile of v2, /device:TPU:0, one launch (start us, length us, event | category | flops | bytes accessed | tf_op | source)
XLA Modules:
  0.0 68.1 jit_solution(9136396822313494716)
XLA Ops:
  0.6 1.7 %select_rows.1 = (bf16[32,4096]{1,0:T(8,128)(2,1)S(1)}, bf16[32,4096]{1,0:T(8,128)(2,1)S(1)}, bf16[32,4096]{1,0:T(8,128)(2,1)S(1)}, bf16[32,4096]{1,0:T(8,128)(2,1)S(1)}, bf16[128,128]{1,0:T(8,128)(2,1)S(1)}) custom-call(bf16[128,2048]{1,0:T(8,128)(2,1)} %tokens.1, bf16[128,2048]{1,0:T(8,128)(2,1)} %grad_out.1, s32[1,128]{1,0:T(1,128)} %bitcast.10, ...), custom_call_target="tpu_custom_call" | custom-call | flops 134217728 | bytes 2097152 | tf_op jit(solution)/shard_map/select_rows/pallas_call | solution.py:94
  2.3 5.1 %collective-permute-start.3 = (bf16[32,4096]{1,0:T(8,128)(2,1)S(1)}, bf16[32,4096]{1,0:T(8,128)(2,1)S(1)}, u32[]{:S(2)}, u32[]{:S(2)}) collective-permute-start(bf16[32,4096]{1,0:T(8,128)(2,1)S(1)} %get-tuple-element.29), channel_id=1, source_target_pairs={{0,12},{4,8},{8,4},{12,0},{1,13},{5,9},{9,5},{13,1},{2,14},{6,10},... | collective-permute-start | bytes 786440 | tf_op jit(solution)/shard_map/ppermute | solution.py:302
  7.4 1.5 %collective-permute-start = (bf16[32,4096]{1,0:T(8,128)(2,1)S(1)}, bf16[32,4096]{1,0:T(8,128)(2,1)S(1)}, u32[]{:S(2)}, u32[]{:S(2)}) collective-permute-start(bf16[32,4096]{1,0:T(8,128)(2,1)S(1)} %get-tuple-element.26.refs_0_), channel_id=1, source_target_pairs={{0,2},{1,3},{2,0},{3,1},{4,6},{5,7},{6,4},{7,5},{8,10},{9,11},{10,... | collective-permute-start | bytes 786440 | tf_op jit(solution)/shard_map/ppermute | solution.py:305
  8.9 0.8 %collective-permute-start.14 = (bf16[32,4096]{1,0:T(8,128)(2,1)S(1)}, bf16[32,4096]{1,0:T(8,128)(2,1)S(1)}, u32[]{:S(2)}, u32[]{:S(2)}) collective-permute-start(bf16[32,4096]{1,0:T(8,128)(2,1)S(1)} %get-tuple-element.35), channel_id=1, source_target_pairs={{0,8},{4,12},{8,0},{12,4},{1,9},{5,13},{9,1},{13,5},{2,10},{6,14},... | collective-permute-start | bytes 786440 | tf_op jit(solution)/shard_map/ppermute | solution.py:302
  9.7 4.9 %collective-permute-done.3.refs_4_ = bf16[32,4096]{1,0:T(8,128)(2,1)S(1)} collective-permute-done((bf16[32,4096]{1,0:T(8,128)(2,1)S(1)}, bf16[32,4096]{1,0:T(8,128)(2,1)S(1)}, u32[]{:S(2)}, u32[]{:S(2)}) %collective-permute-start.3) | collective-permute-done | bytes 262176 | tf_op jit(solution)/shard_map/ppermute | solution.py:302
  14.7 1.7 %collective-permute-start.4 = (bf16[32,4096]{1,0:T(8,128)(2,1)S(1)}, bf16[32,4096]{1,0:T(8,128)(2,1)S(1)}, u32[]{:S(2)}, u32[]{:S(2)}) collective-permute-start(bf16[32,4096]{1,0:T(8,128)(2,1)S(1)} %collective-permute-done.3.refs_4_), channel_id=1, source_target_pairs={{0,2},{1,3},{2,0},{3,1},{4,6},{5,7},{6,4},{7,5},{8,10},{9,11},{10,... | collective-permute-start | bytes 786440 | tf_op jit(solution)/shard_map/ppermute | solution.py:305
  16.4 4.1 %collective-permute-done.1.refs_2_ = bf16[32,4096]{1,0:T(8,128)(2,1)S(1)} collective-permute-done((bf16[32,4096]{1,0:T(8,128)(2,1)S(1)}, bf16[32,4096]{1,0:T(8,128)(2,1)S(1)}, u32[]{:S(2)}, u32[]{:S(2)}) %collective-permute-start.1) | collective-permute-done | bytes 262176 | tf_op jit(solution)/shard_map/ppermute | solution.py:302
  20.5 1.4 %collective-permute-start.2 = (bf16[32,4096]{1,0:T(8,128)(2,1)S(1)}, bf16[32,4096]{1,0:T(8,128)(2,1)S(1)}, u32[]{:S(2)}, u32[]{:S(2)}) collective-permute-start(bf16[32,4096]{1,0:T(8,128)(2,1)S(1)} %collective-permute-done.1.refs_2_), channel_id=1, source_target_pairs={{0,2},{1,3},{2,0},{3,1},{4,6},{5,7},{6,4},{7,5},{8,10},{9,11},{10,... | collective-permute-start | bytes 786440 | tf_op jit(solution)/shard_map/ppermute | solution.py:305
  21.9 2.9 %load_weights.1 = (bf16[2048,512]{1,0:T(8,128)(2,1)S(1)}, bf16[2048,512]{1,0:T(8,128)(2,1)S(1)}, bf16[512,2048]{1,0:T(8,128)(2,1)S(1)}, bf16[32,4096]{1,0:T(8,128)(2,1)S(1)}) custom-call(bf16[2048,512]{1,0:T(8,128)(2,1)} %bitcast.7, bf16[2048,512]{1,0:T(8,128)(2,1)} %bitcast.8, bf16[512,2048]{1,0:T(8,128)(2,1)} %bitcast.9, ...), custom_call_target="tpu_custom_call", output_to_operand_aliasing={{3}: (3, {})} | custom-call | tf_op jit(solution)/shard_map/load_weights/pallas_call | solution.py:120
  24.8 0.5 collective-permute-start.7
  25.3 4.4 %collective-permute-done.14.refs_0_.refs_12_ = bf16[32,4096]{1,0:T(8,128)(2,1)S(1)} collective-permute-done((bf16[32,4096]{1,0:T(8,128)(2,1)S(1)}, bf16[32,4096]{1,0:T(8,128)(2,1)S(1)}, u32[]{:S(2)}, u32[]{:S(2)}) %collective-permute-start.14) | collective-permute-done | bytes 262176 | tf_op jit(solution)/shard_map/ppermute | solution.py:302
  29.7 0.5 collective-permute-start.10
  30.3 1.5 %collective-permute-start.15 = (bf16[32,4096]{1,0:T(8,128)(2,1)S(1)}, bf16[32,4096]{1,0:T(8,128)(2,1)S(1)}, u32[]{:S(2)}, u32[]{:S(2)}) collective-permute-start(bf16[32,4096]{1,0:T(8,128)(2,1)S(1)} %collective-permute-done.14.refs_0_.refs_12_), channel_id=1, source_target_pairs={{0,2},{1,3},{2,0},{3,1},{4,6},{5,7},{6,4},{7,5},{8,10},{9,11},{10,... | collective-permute-start | bytes 786440 | tf_op jit(solution)/shard_map/ppermute | solution.py:305
  32.0 4.4 %chunk_backward.2 = (bf16[384,512]{1,0:T(8,128)(2,1)S(1)}, bf16[384,1024]{1,0:T(8,128)(2,1)S(1)}, bf16[192,2048]{1,0:T(8,128)(2,1)S(1)}, f32[192,2048]{1,0:T(8,128)S(1)}) custom-call(bf16[32,4096]{1,0:T(8,128)(2,1)S(1)} %get-tuple-element.26.refs_0_, bf16[32,4096]{1,0:T(8,128)(2,1)S(1)} %get-tuple-element.27.refs_1_, ...), custom_call_target="tpu_custom_call" | custom-call | flops 4026531840 | bytes 6291456 | tf_op jit(solution)/shard_map/chunk_backward/pallas_call | solution.py:177
  36.7 0.4 collective-permute-start.16
  37.1 1.9 %collective-permute-done.15.refs_0_ = bf16[32,4096]{1,0:T(8,128)(2,1)S(1)} collective-permute-done((bf16[32,4096]{1,0:T(8,128)(2,1)S(1)}, bf16[32,4096]{1,0:T(8,128)(2,1)S(1)}, u32[]{:S(2)}, u32[]{:S(2)}) %collective-permute-start.15) | collective-permute-done | bytes 262176 | tf_op jit(solution)/shard_map/ppermute | solution.py:305
  39.0 0.6 collective-permute-start.21
  39.6 0.9 %collective-permute-done.17.refs_3_.refs_15_ = bf16[32,4096]{1,0:T(8,128)(2,1)S(1)} collective-permute-done((bf16[32,4096]{1,0:T(8,128)(2,1)S(1)}, bf16[32,4096]{1,0:T(8,128)(2,1)S(1)}, u32[]{:S(2)}, u32[]{:S(2)}) %collective-permute-start.17) | collective-permute-done | bytes 262176 | tf_op jit(solution)/shard_map/ppermute | solution.py:305
  40.5 2.8 %chunk_backward.3 = (bf16[128,512]{1,0:T(8,128)(2,1)S(1)}, bf16[128,1024]{1,0:T(8,128)(2,1)S(1)}, bf16[64,2048]{1,0:T(8,128)(2,1)S(1)}, f32[64,2048]{1,0:T(8,128)S(1)}) custom-call(bf16[32,4096]{1,0:T(8,128)(2,1)S(1)} %collective-permute-done.14.refs_0_.refs_12_, bf16[32,4096]{1,0:T(8,128)(2,1)S(1)} %after.2.refs_1_.refs_13_, ...), custom_call_target="tpu_custom_call" | custom-call | flops 1342177280 | bytes 6291456 | tf_op jit(solution)/shard_map/chunk_backward/pallas_call | solution.py:177
  44.0 1.0 %collective-permute-done.18 = bf16[64,2048]{1,0:T(8,128)(2,1)S(1)} collective-permute-done((bf16[64,2048]{1,0:T(8,128)(2,1)S(1)}, bf16[64,2048]{1,0:T(8,128)(2,1)S(1)}, u32[]{:S(2)}, u32[]{:S(2)}) %collective-permute-start.18) | collective-permute-done | bytes 262176 | tf_op jit(solution)/shard_map/ppermute | solution.py:305
  45.0 1.6 %collective-permute-start.22 = (bf16[32,2048]{1,0:T(8,128)(2,1)S(1)}, bf16[32,2048]{1,0:T(8,128)(2,1)S(1)}, u32[]{:S(2)}, u32[]{:S(2)}) collective-permute-start(bf16[32,2048]{1,0:T(8,128)(2,1)S(1)} %slice.98), channel_id=1, source_target_pairs={{0,2},{1,3},{2,0},{3,1},{4,6},{5,7},{6,4},{7,5},{8,10},{9,11},{10,... | collective-permute-start | bytes 393224 | tf_op jit(solution)/shard_map/ppermute | solution.py:305
  46.6 0.5 collective-permute-start.19
  47.2 1.6 %collective-permute-start.12 = (bf16[64,2048]{1,0:T(8,128)(2,1)S(1)}, bf16[64,2048]{1,0:T(8,128)(2,1)S(1)}, u32[]{:S(2)}, u32[]{:S(2)}) collective-permute-start(bf16[64,2048]{1,0:T(8,128)(2,1)S(1)} %pad_maximum_fusion), channel_id=1, source_target_pairs={{0,2},{1,3},{2,0},{3,1},{4,6},{5,7},{6,4},{7,5},{8,10},{9,11},{10,... | collective-permute-start | bytes 786440 | tf_op jit(solution)/shard_map/ppermute | solution.py:305
  48.7 3.2 %down_grads.1 = (bf16[512,2048]{1,0:T(8,128)(2,1)}, f32[8,128]{1,0:T(8,128)S(1)}) custom-call(bf16[32,4096]{1,0:T(8,128)(2,1)S(1)} %get-tuple-element.26.refs_0_, bf16[32,4096]{1,0:T(8,128)(2,1)S(1)} %get-tuple-element.27.refs_1_, bf16[32,4096]{1,0:T(8,128)(2,1)S(1)} %collective-permute-done.1.refs_2_, bf16[32,4096]{1,0:T(8,128)(2,1)S(1)} %collective-permute-done.2.refs_3_, ...), custom_call_target="tpu_custom_call" | custom-call | flops 1073741824 | bytes 2097152 | tf_op jit(solution)/shard_map/down_grads/pallas_call | solution.py:257
  52.0 2.5 %collective-permute-start.23 = (bf16[32,2048]{1,0:T(8,128)(2,1)S(1)}, bf16[32,2048]{1,0:T(8,128)(2,1)S(1)}, u32[]{:S(2)}, u32[]{:S(2)}) collective-permute-start(bf16[32,2048]{1,0:T(8,128)(2,1)S(1)} %fusion.1), channel_id=1, source_target_pairs={{0,12},{4,8},{8,4},{12,0},{1,13},{5,9},{9,5},{13,1},{2,14},{6,10},... | collective-permute-start | bytes 393224 | tf_op jit(solution)/shard_map/ppermute | solution.py:302
  54.5 2.5 %collective-permute-start.20 = (bf16[32,2048]{1,0:T(8,128)(2,1)S(1)}, bf16[32,2048]{1,0:T(8,128)(2,1)S(1)}, u32[]{:S(2)}, u32[]{:S(2)}) collective-permute-start(bf16[32,2048]{1,0:T(8,128)(2,1)S(1)} %after.3), channel_id=1, source_target_pairs={{0,8},{4,12},{8,0},{12,4},{1,9},{5,13},{9,1},{13,5},{2,10},{6,14},... | collective-permute-start | bytes 393224 | tf_op jit(solution)/shard_map/ppermute | solution.py:302
  57.0 2.1 %collective-permute-done.12 = bf16[64,2048]{1,0:T(8,128)(2,1)S(1)} collective-permute-done((bf16[64,2048]{1,0:T(8,128)(2,1)S(1)}, bf16[64,2048]{1,0:T(8,128)(2,1)S(1)}, u32[]{:S(2)}, u32[]{:S(2)}) %collective-permute-start.12) | collective-permute-done | bytes 262176 | tf_op jit(solution)/shard_map/ppermute | solution.py:305
  59.2 1.9 %collective-permute-start.13 = (bf16[32,2048]{1,0:T(8,128)(2,1)S(1)}, bf16[32,2048]{1,0:T(8,128)(2,1)S(1)}, u32[]{:S(2)}, u32[]{:S(2)}) collective-permute-start(bf16[32,2048]{1,0:T(8,128)(2,1)S(1)} %get-tuple-element.49), channel_id=1, source_target_pairs={{0,4},{4,0},{8,12},{12,8},{1,5},{5,1},{9,13},{13,9},{2,6},{6,2},{1... | collective-permute-start | bytes 393224 | tf_op jit(solution)/shard_map/ppermute | solution.py:302
  61.0 4.1 %pair_grads.1 = (bf16[2048,512]{1,0:T(8,128)(2,1)}, bf16[2048,512]{1,0:T(8,128)(2,1)}) custom-call(bf16[32,4096]{1,0:T(8,128)(2,1)S(1)} %get-tuple-element.26.refs_0_, bf16[32,4096]{1,0:T(8,128)(2,1)S(1)} %get-tuple-element.27.refs_1_, bf16[32,4096]{1,0:T(8,128)(2,1)S(1)} %collective-permute-done.1.refs_2_, ...), custom_call_target="tpu_custom_call" | custom-call | flops 2147483648 | bytes 4194304 | tf_op jit(solution)/shard_map/pair_grads/pallas_call | solution.py:241
  65.1 1.4 %collective-permute-done.20.refs_2_ = bf16[32,2048]{1,0:T(8,128)(2,1)S(1)} collective-permute-done((bf16[32,2048]{1,0:T(8,128)(2,1)S(1)}, bf16[32,2048]{1,0:T(8,128)(2,1)S(1)}, u32[]{:S(2)}, u32[]{:S(2)}) %collective-permute-start.20) | collective-permute-done | bytes 131104 | tf_op jit(solution)/shard_map/ppermute | solution.py:302
  66.5 0.5 collective-permute-done.13.refs_1_
  67.0 1.1 %place_rows.1 = bf16[128,2048]{1,0:T(8,128)(2,1)} custom-call(bf16[128,128]{1,0:T(8,128)(2,1)S(1)} %get-tuple-element.25.back, bf16[32,2048]{1,0:T(8,128)(2,1)S(1)} %get-tuple-element.50.refs_0_, bf16[32,2048]{1,0:T(8,128)(2,1)S(1)} %collective-permute-done.13.refs_1_, bf16[32,2048]{1,0:T(8,128)(2,1)S(1)} %collective-permute-done.20.refs_2_, ...), custom_call_target="tpu_custom_call" | custom-call | flops 67108864 | bytes 1048576 | tf_op jit(solution)/shard_map/place_rows/pallas_call | solution.py:281
  (41 shorter events, 1.5 us)
Async XLA Ops:
  2.3 12.3 %collective-permute-start.3 = (bf16[32,4096]{1,0:T(8,128)(2,1)S(1)}, bf16[32,4096]{1,0:T(8,128)(2,1)S(1)}, u32[]{:S(2)}, u32[]{:S(2)}) collective-permute-start(bf16[32,4096]{1,0:T(8,128)(2,1)S(1)} %get-tuple-element.29), channel_id=1, source_target_pairs={{0,12},{4,8},{8,4},{12,0},{1,13},{5,9},{9,5},{13,1},{2,14},{6,10},... | collective-permute-start | bytes 786440 | tf_op jit(solution)/shard_map/ppermute | solution.py:302
  7.4 13.1 %collective-permute-start.1 = (bf16[32,4096]{1,0:T(8,128)(2,1)S(1)}, bf16[32,4096]{1,0:T(8,128)(2,1)S(1)}, u32[]{:S(2)}, u32[]{:S(2)}) collective-permute-start(bf16[32,4096]{1,0:T(8,128)(2,1)S(1)} %get-tuple-element.28), channel_id=1, source_target_pairs={{0,4},{4,0},{8,12},{12,8},{1,5},{5,1},{9,13},{13,9},{2,6},{6,2},{1... | collective-permute-start | bytes 786440 | tf_op jit(solution)/shard_map/ppermute | solution.py:302
  7.4 14.4 %collective-permute-start = (bf16[32,4096]{1,0:T(8,128)(2,1)S(1)}, bf16[32,4096]{1,0:T(8,128)(2,1)S(1)}, u32[]{:S(2)}, u32[]{:S(2)}) collective-permute-start(bf16[32,4096]{1,0:T(8,128)(2,1)S(1)} %get-tuple-element.26.refs_0_), channel_id=1, source_target_pairs={{0,2},{1,3},{2,0},{3,1},{4,6},{5,7},{6,4},{7,5},{8,10},{9,11},{10,... | collective-permute-start | bytes 786440 | tf_op jit(solution)/shard_map/ppermute | solution.py:305
  8.9 15.9 %collective-permute-start.5 = (bf16[32,4096]{1,0:T(8,128)(2,1)S(1)}, bf16[32,4096]{1,0:T(8,128)(2,1)S(1)}, u32[]{:S(2)}, u32[]{:S(2)}) collective-permute-start(bf16[32,4096]{1,0:T(8,128)(2,1)S(1)} %get-tuple-element.26.refs_0_), channel_id=1, source_target_pairs={{0,1},{1,0},{2,3},{3,2},{4,5},{5,4},{6,7},{7,6},{8,9},{9,8},{10,11... | collective-permute-start | bytes 786440 | tf_op jit(solution)/shard_map/ppermute | solution.py:305
  8.9 20.8 %collective-permute-start.14 = (bf16[32,4096]{1,0:T(8,128)(2,1)S(1)}, bf16[32,4096]{1,0:T(8,128)(2,1)S(1)}, u32[]{:S(2)}, u32[]{:S(2)}) collective-permute-start(bf16[32,4096]{1,0:T(8,128)(2,1)S(1)} %get-tuple-element.35), channel_id=1, source_target_pairs={{0,8},{4,12},{8,0},{12,4},{1,9},{5,13},{9,1},{13,5},{2,10},{6,14},... | collective-permute-start | bytes 786440 | tf_op jit(solution)/shard_map/ppermute | solution.py:302
  14.7 15.1 %collective-permute-start.4 = (bf16[32,4096]{1,0:T(8,128)(2,1)S(1)}, bf16[32,4096]{1,0:T(8,128)(2,1)S(1)}, u32[]{:S(2)}, u32[]{:S(2)}) collective-permute-start(bf16[32,4096]{1,0:T(8,128)(2,1)S(1)} %collective-permute-done.3.refs_4_), channel_id=1, source_target_pairs={{0,2},{1,3},{2,0},{3,1},{4,6},{5,7},{6,4},{7,5},{8,10},{9,11},{10,... | collective-permute-start | bytes 786440 | tf_op jit(solution)/shard_map/ppermute | solution.py:305
  20.5 9.8 %collective-permute-start.2 = (bf16[32,4096]{1,0:T(8,128)(2,1)S(1)}, bf16[32,4096]{1,0:T(8,128)(2,1)S(1)}, u32[]{:S(2)}, u32[]{:S(2)}) collective-permute-start(bf16[32,4096]{1,0:T(8,128)(2,1)S(1)} %collective-permute-done.1.refs_2_), channel_id=1, source_target_pairs={{0,2},{1,3},{2,0},{3,1},{4,6},{5,7},{6,4},{7,5},{8,10},{9,11},{10,... | collective-permute-start | bytes 786440 | tf_op jit(solution)/shard_map/ppermute | solution.py:305
  24.8 5.6 %collective-permute-start.6 = (bf16[32,4096]{1,0:T(8,128)(2,1)S(1)}, bf16[32,4096]{1,0:T(8,128)(2,1)S(1)}, u32[]{:S(2)}, u32[]{:S(2)}) collective-permute-start(bf16[32,4096]{1,0:T(8,128)(2,1)S(1)} %get-tuple-element.27.refs_1_), channel_id=1, source_target_pairs={{0,1},{1,0},{2,3},{3,2},{4,5},{5,4},{6,7},{7,6},{8,9},{9,8},{10,11... | collective-permute-start | bytes 786440 | tf_op jit(solution)/shard_map/ppermute | solution.py:305
  24.8 7.0 %collective-permute-start.7 = (bf16[32,4096]{1,0:T(8,128)(2,1)S(1)}, bf16[32,4096]{1,0:T(8,128)(2,1)S(1)}, u32[]{:S(2)}, u32[]{:S(2)}) collective-permute-start(bf16[32,4096]{1,0:T(8,128)(2,1)S(1)} %collective-permute-done.1.refs_2_), channel_id=1, source_target_pairs={{0,1},{1,0},{2,3},{3,2},{4,5},{5,4},{6,7},{7,6},{8,9},{9,8},{10,11... | collective-permute-start | bytes 786440 | tf_op jit(solution)/shard_map/ppermute | solution.py:305
  29.7 2.1 %collective-permute-start.9 = (bf16[32,4096]{1,0:T(8,128)(2,1)S(1)}, bf16[32,4096]{1,0:T(8,128)(2,1)S(1)}, u32[]{:S(2)}, u32[]{:S(2)}) collective-permute-start(bf16[32,4096]{1,0:T(8,128)(2,1)S(1)} %collective-permute-done.3.refs_4_), channel_id=1, source_target_pairs={{0,1},{1,0},{2,3},{3,2},{4,5},{5,4},{6,7},{7,6},{8,9},{9,8},{10,11... | collective-permute-start | bytes 786440 | tf_op jit(solution)/shard_map/ppermute | solution.py:305
  29.7 2.1 %collective-permute-start.10 = (bf16[32,4096]{1,0:T(8,128)(2,1)S(1)}, bf16[32,4096]{1,0:T(8,128)(2,1)S(1)}, u32[]{:S(2)}, u32[]{:S(2)}) collective-permute-start(bf16[32,4096]{1,0:T(8,128)(2,1)S(1)} %collective-permute-done.4.refs_5_), channel_id=1, source_target_pairs={{0,1},{1,0},{2,3},{3,2},{4,5},{5,4},{6,7},{7,6},{8,9},{9,8},{10,11... | collective-permute-start | bytes 786440 | tf_op jit(solution)/shard_map/ppermute | solution.py:305
  30.3 1.8 %collective-permute-start.8 = (bf16[32,4096]{1,0:T(8,128)(2,1)S(1)}, bf16[32,4096]{1,0:T(8,128)(2,1)S(1)}, u32[]{:S(2)}, u32[]{:S(2)}) collective-permute-start(bf16[32,4096]{1,0:T(8,128)(2,1)S(1)} %collective-permute-done.2.refs_3_), channel_id=1, source_target_pairs={{0,1},{1,0},{2,3},{3,2},{4,5},{5,4},{6,7},{7,6},{8,9},{9,8},{10,11... | collective-permute-start | bytes 786440 | tf_op jit(solution)/shard_map/ppermute | solution.py:305
  30.3 8.7 %collective-permute-start.15 = (bf16[32,4096]{1,0:T(8,128)(2,1)S(1)}, bf16[32,4096]{1,0:T(8,128)(2,1)S(1)}, u32[]{:S(2)}, u32[]{:S(2)}) collective-permute-start(bf16[32,4096]{1,0:T(8,128)(2,1)S(1)} %collective-permute-done.14.refs_0_.refs_12_), channel_id=1, source_target_pairs={{0,2},{1,3},{2,0},{3,1},{4,6},{5,7},{6,4},{7,5},{8,10},{9,11},{10,... | collective-permute-start | bytes 786440 | tf_op jit(solution)/shard_map/ppermute | solution.py:305
  36.5 7.0 %collective-permute-start.11 = (bf16[128,2048]{1,0:T(8,128)(2,1)S(1)}, bf16[128,2048]{1,0:T(8,128)(2,1)S(1)}, u32[]{:S(2)}, u32[]{:S(2)}) collective-permute-start(bf16[128,2048]{1,0:T(8,128)(2,1)S(1)} %concatenate.9), channel_id=1, source_target_pairs={{0,1},{1,0},{2,3},{3,2},{4,5},{5,4},{6,7},{7,6},{8,9},{9,8},{10,11... | collective-permute-start | bytes 1572872 | tf_op jit(solution)/shard_map/ppermute | solution.py:305
  36.7 2.9 %collective-permute-start.16 = (bf16[32,4096]{1,0:T(8,128)(2,1)S(1)}, bf16[32,4096]{1,0:T(8,128)(2,1)S(1)}, u32[]{:S(2)}, u32[]{:S(2)}) collective-permute-start(bf16[32,4096]{1,0:T(8,128)(2,1)S(1)} %collective-permute-done.14.refs_0_.refs_12_), channel_id=1, source_target_pairs={{0,1},{1,0},{2,3},{3,2},{4,5},{5,4},{6,7},{7,6},{8,9},{9,8},{10,11... | collective-permute-start | bytes 786440 | tf_op jit(solution)/shard_map/ppermute | solution.py:305
  39.0 1.5 %collective-permute-start.17 = (bf16[32,4096]{1,0:T(8,128)(2,1)S(1)}, bf16[32,4096]{1,0:T(8,128)(2,1)S(1)}, u32[]{:S(2)}, u32[]{:S(2)}) collective-permute-start(bf16[32,4096]{1,0:T(8,128)(2,1)S(1)} %after.2.refs_1_.refs_13_), channel_id=1, source_target_pairs={{0,1},{1,0},{2,3},{3,2},{4,5},{5,4},{6,7},{7,6},{8,9},{9,8},{10,11... | collective-permute-start | bytes 786440 | tf_op jit(solution)/shard_map/ppermute | solution.py:305
  39.0 4.6 %collective-permute-start.21 = (bf16[64,2048]{1,0:T(8,128)(2,1)S(1)}, bf16[64,2048]{1,0:T(8,128)(2,1)S(1)}, u32[]{:S(2)}, u32[]{:S(2)}) collective-permute-start(bf16[64,2048]{1,0:T(8,128)(2,1)S(1)} %slice.68), channel_id=1, source_target_pairs={{0,1},{1,0},{2,3},{3,2},{4,5},{5,4},{6,7},{7,6},{8,9},{9,8},{10,11... | collective-permute-start | bytes 786440 | tf_op jit(solution)/shard_map/ppermute | solution.py:305
  43.3 1.6 %collective-permute-start.18 = (bf16[64,2048]{1,0:T(8,128)(2,1)S(1)}, bf16[64,2048]{1,0:T(8,128)(2,1)S(1)}, u32[]{:S(2)}, u32[]{:S(2)}) collective-permute-start(bf16[64,2048]{1,0:T(8,128)(2,1)S(1)} %get-tuple-element.37), channel_id=1, source_target_pairs={{0,1},{1,0},{2,3},{3,2},{4,5},{5,4},{6,7},{7,6},{8,9},{9,8},{10,11... | collective-permute-start | bytes 786440 | tf_op jit(solution)/shard_map/ppermute | solution.py:305
  45.0 6.9 %collective-permute-start.22 = (bf16[32,2048]{1,0:T(8,128)(2,1)S(1)}, bf16[32,2048]{1,0:T(8,128)(2,1)S(1)}, u32[]{:S(2)}, u32[]{:S(2)}) collective-permute-start(bf16[32,2048]{1,0:T(8,128)(2,1)S(1)} %slice.98), channel_id=1, source_target_pairs={{0,2},{1,3},{2,0},{3,1},{4,6},{5,7},{6,4},{7,5},{8,10},{9,11},{10,... | collective-permute-start | bytes 393224 | tf_op jit(solution)/shard_map/ppermute | solution.py:305
  46.6 7.9 %collective-permute-start.19 = (bf16[32,2048]{1,0:T(8,128)(2,1)S(1)}, bf16[32,2048]{1,0:T(8,128)(2,1)S(1)}, u32[]{:S(2)}, u32[]{:S(2)}) collective-permute-start(bf16[32,2048]{1,0:T(8,128)(2,1)S(1)} %slice.99.refs_18_), channel_id=1, source_target_pairs={{0,2},{1,3},{2,0},{3,1},{4,6},{5,7},{6,4},{7,5},{8,10},{9,11},{10,... | collective-permute-start | bytes 393224 | tf_op jit(solution)/shard_map/ppermute | solution.py:305
  47.2 11.9 %collective-permute-start.12 = (bf16[64,2048]{1,0:T(8,128)(2,1)S(1)}, bf16[64,2048]{1,0:T(8,128)(2,1)S(1)}, u32[]{:S(2)}, u32[]{:S(2)}) collective-permute-start(bf16[64,2048]{1,0:T(8,128)(2,1)S(1)} %pad_maximum_fusion), channel_id=1, source_target_pairs={{0,2},{1,3},{2,0},{3,1},{4,6},{5,7},{6,4},{7,5},{8,10},{9,11},{10,... | collective-permute-start | bytes 786440 | tf_op jit(solution)/shard_map/ppermute | solution.py:305
  52.0 13.1 %collective-permute-start.23 = (bf16[32,2048]{1,0:T(8,128)(2,1)S(1)}, bf16[32,2048]{1,0:T(8,128)(2,1)S(1)}, u32[]{:S(2)}, u32[]{:S(2)}) collective-permute-start(bf16[32,2048]{1,0:T(8,128)(2,1)S(1)} %fusion.1), channel_id=1, source_target_pairs={{0,12},{4,8},{8,4},{12,0},{1,13},{5,9},{9,5},{13,1},{2,14},{6,10},... | collective-permute-start | bytes 393224 | tf_op jit(solution)/shard_map/ppermute | solution.py:302
  54.5 11.9 %collective-permute-start.20 = (bf16[32,2048]{1,0:T(8,128)(2,1)S(1)}, bf16[32,2048]{1,0:T(8,128)(2,1)S(1)}, u32[]{:S(2)}, u32[]{:S(2)}) collective-permute-start(bf16[32,2048]{1,0:T(8,128)(2,1)S(1)} %after.3), channel_id=1, source_target_pairs={{0,8},{4,12},{8,0},{12,4},{1,9},{5,13},{9,1},{13,5},{2,10},{6,14},... | collective-permute-start | bytes 393224 | tf_op jit(solution)/shard_map/ppermute | solution.py:302
  59.2 7.8 %collective-permute-start.13 = (bf16[32,2048]{1,0:T(8,128)(2,1)S(1)}, bf16[32,2048]{1,0:T(8,128)(2,1)S(1)}, u32[]{:S(2)}, u32[]{:S(2)}) collective-permute-start(bf16[32,2048]{1,0:T(8,128)(2,1)S(1)} %get-tuple-element.49), channel_id=1, source_target_pairs={{0,4},{4,0},{8,12},{12,8},{1,5},{5,1},{9,13},{13,9},{2,6},{6,2},{1... | collective-permute-start | bytes 393224 | tf_op jit(solution)/shard_map/ppermute | solution.py:302

commit v3 on v2

v3 whole, which is shorter than its diff:
```python
import functools

import jax
import jax.numpy as jnp
from jax import lax
from jax.experimental import pallas as pl
from jax.experimental.pallas import tpu as pltpu
from jax.sharding import PartitionSpec as P

BF16 = jnp.bfloat16
F32 = jnp.float32
GROUPS = 4
VMEM = pl.BlockSpec(memory_space=pltpu.VMEM)
ANY = pl.BlockSpec(memory_space=pl.ANY)
HBM = pl.BlockSpec(memory_space=pltpu.HBM)
TN = (((0,), (0,)), ((), ()))
PIECES = [[(0, 0, 2), (3, 0, 2), (1, 0, 2)], [(2, 0, 2)]]
PARTS = 2
TILES = 4
RETURNS = [[[(3, 0, 2)], [(1, 0, 2)], [(0, 0, 2)]], [[(2, 0, 2)]]]


def params(mib):
    return pltpu.CompilerParams(vmem_limit_bytes=mib * 1024 * 1024)


def cost(flops, moved):
    return pl.CostEstimate(flops=flops, bytes_accessed=moved, transcendentals=0)


def in_hbm(a):
    return pltpu.with_memory_space_constraint(a, pltpu.HBM)


def pass_kernel(*refs):
    del refs


def after(a, *others):
    return pl.pallas_call(
        pass_kernel,
        out_shape=jax.ShapeDtypeStruct(a.shape, a.dtype),
        in_specs=[ANY] * (1 + len(others)),
        out_specs=ANY,
        input_output_aliases={0: 0},
        compiler_params=params(1),
        cost_estimate=cost(0, 0),
        name="after",
    )(a, *others)


def select_kernel(slot_cap, spans, tokens, grad_out, routes, order, *refs):
    sends, back = refs[: len(spans)], refs[len(spans)]
    xs, ys, route_in, order_in, sems = refs[len(spans) + 1 :]
    small = [
        pltpu.make_async_copy(routes, route_in, sems.at[0]),
        pltpu.make_async_copy(order, order_in, sems.at[1]),
    ]
    large = [
        pltpu.make_async_copy(tokens, xs, sems.at[2]),
        pltpu.make_async_copy(grad_out, ys, sems.at[3]),
    ]
    for copy in small + large:
        copy.start()
    count, width = tokens.shape
    rows = lax.broadcasted_iota(jnp.int32, (count, count), 0)
    lanes = lax.broadcasted_iota(jnp.int32, (count, count), 1)
    eye = rows == lanes
    me = lax.axis_index("expert")
    for copy in small:
        copy.wait()
    route_row = route_in[...]
    order_row = order_in[...]
    route_col = jnp.sum(jnp.where(eye, route_row, 0), axis=1, keepdims=True)
    order_col = jnp.sum(jnp.where(eye, order_row, 0), axis=1, keepdims=True)
    ahead = (route_col == route_row) & (order_col < order_row)
    rank = jnp.sum(ahead.astype(jnp.int32), axis=0, keepdims=True)
    place = jnp.bitwise_xor(route_row, me) * slot_cap + rank
    place = jnp.where(rank < slot_cap, place, -1)
    select = (rows == place).astype(F32).astype(BF16)
    place_col = jnp.sum(jnp.where(eye, place, 0), axis=1, keepdims=True)
    back[...] = (lanes == place_col).astype(F32).astype(BF16)
    for half, copy in enumerate(large):
        copy.wait()
        moved = jnp.dot(select, (xs, ys)[half][...], preferred_element_type=F32).astype(BF16)
        for send, (low, high) in zip(sends, spans):
            send[:, half * width : (half + 1) * width] = moved[low:high]


def select_rows(tokens, grad_out, routes, order, slot_cap, spans):
    count, width = tokens.shape
    return pl.pallas_call(
        functools.partial(select_kernel, slot_cap, spans),
        out_shape=[jax.ShapeDtypeStruct((high - low, 2 * width), BF16) for low, high in spans]
        + [jax.ShapeDtypeStruct((count, count), BF16)],
        in_specs=[HBM] * 4,
        out_specs=[VMEM] * (len(spans) + 1),
        scratch_shapes=[pltpu.VMEM((count, width), BF16)] * 2
        + [pltpu.VMEM((1, count), jnp.int32)] * 2
        + [pltpu.SemaphoreType.DMA((4,))],
        compiler_params=params(16),
        cost_estimate=cost(4 * count * count * width, 8 * count * width),
        name="select_rows",
    )(*map(in_hbm, (tokens, grad_out, routes.reshape(1, count), order)))


def load_kernel(gate_w, up_w, down_w, passed, pair_w, pair_t, down_t, passed_out, down_in, sems):
    del passed, passed_out
    width, units = gate_w.shape
    copies = [
        pltpu.make_async_copy(down_w, down_in, sems.at[0]),
        pltpu.make_async_copy(gate_w, pair_w.at[:, pl.ds(0, units)], sems.at[1]),
        pltpu.make_async_copy(up_w, pair_w.at[:, pl.ds(units, units)], sems.at[2]),
    ]
    for copy in copies:
        copy.start()
    tiles = width // units
    copies[0].wait()
    for t in range(tiles):
        part = slice(t * units, (t + 1) * units)
        down_t[part] = down_in[:, part].T
    for half in range(2):
        copies[1 + half].wait()
        side = slice(half * units, (half + 1) * units)
        for t in range(tiles):
            part = slice(t * units, (t + 1) * units)
            pair_t[side, part] = pair_w[part, side].T


def load_weights(gate_w, up_w, down_w, passed):
    width, units = gate_w.shape
    return pl.pallas_call(
        load_kernel,
        out_shape=[
            jax.ShapeDtypeStruct((width, 2 * units), BF16),
            jax.ShapeDtypeStruct((2 * units, width), BF16),
            jax.ShapeDtypeStruct((width, units), BF16),
            jax.ShapeDtypeStruct(passed.shape, passed.dtype),
        ],
        in_specs=[HBM] * 3 + [ANY],
        out_specs=[VMEM] * 3 + [ANY],
        scratch_shapes=[pltpu.VMEM((units, width), BF16), pltpu.SemaphoreType.DMA((3,))],
        input_output_aliases={3: 3},
        compiler_params=params(12),
        cost_estimate=cost(0, 0),
        name="load_weights",
    )(*map(in_hbm, (gate_w, up_w, down_w)), passed)


def chunk_kernel(n, first, *refs):
    blocks = refs[:n]
    pair_w, pair_t, down_t = refs[n : n + 3]
    xs, ys, hs, ps, away_out, keep_out = refs[-6:]
    width = pair_w.shape[0]
    units = down_t.shape[1]
    count = keep_out.shape[0]
    at = first
    for block in blocks:
        rows = block.shape[0]
        xs[at : at + rows] = block[:, :width]
        ys[at : at + rows] = block[:, width:]
        at += rows
    mine = slice(first, at)
    both = jnp.dot(xs[mine], pair_w[...], preferred_element_type=F32)
    gate, upper = both[:, :units], both[:, units:]
    sig = jax.nn.sigmoid(gate)
    active = gate * sig
    slope = sig * (1.0 + gate * (1.0 - sig))
    hs[mine] = (active * upper).astype(BF16)
    grad_hidden = jnp.dot(ys[mine], down_t[...], preferred_element_type=F32)
    ps[mine, :units] = (grad_hidden * upper * slope).astype(BF16)
    ps[mine, units:] = (grad_hidden * active).astype(BF16)
    back = jnp.dot(ps[mine], pair_t[...], preferred_element_type=F32)
    keep_out[...] = back[:count]
    away_out[...] = back[count:].astype(BF16)


def chunk_backward(blocks, weights, first, total, earlier, gates):
    n = len(blocks)
    width, units = weights[2].shape
    count = sum(block.shape[0] for block in blocks) // 2
    aliases = {n + 3 + i: i for i in range(len(earlier))}
    return pl.pallas_call(
        functools.partial(chunk_kernel, n, first),
        out_shape=[
            jax.ShapeDtypeStruct((total, width), BF16),
            jax.ShapeDtypeStruct((total, width), BF16),
            jax.ShapeDtypeStruct((total, units), BF16),
            jax.ShapeDtypeStruct((total, 2 * units), BF16),
            jax.ShapeDtypeStruct((count, width), BF16),
            jax.ShapeDtypeStruct((count, width), F32),
        ],
        in_specs=[VMEM] * (n + 3 + len(earlier)) + [ANY] * len(gates),
        out_specs=[VMEM] * 6,
        input_output_aliases=aliases,
        compiler_params=params(16),
        cost_estimate=cost(20 * count * width * units, 6 * width * units),
        name="chunk_backward",
    )(*blocks, *weights, *earlier, *gates)


def pair_kernel(xs, ps, before, gate_out, up_out, results, sems):
    del before
    units = gate_out.shape[1]
    part = xs.shape[1] // TILES
    copies = []
    for t in range(TILES):
        rows = slice(t * part, (t + 1) * part)
        both = lax.dot_general(xs[:, rows], ps[...], TN, preferred_element_type=F32)
        results[rows] = both.astype(BF16)
        for i, out in enumerate((gate_out, up_out)):
            source = results.at[pl.ds(t * part, part), pl.ds(i * units, units)]
            copies.append(pltpu.make_async_copy(source, out.at[pl.ds(t * part, part)], sems.at[t, i]))
            copies[-1].start()
    for copy in copies:
        copy.wait()


def down_kernel(ys, hs, before, down_out, mark, results, sems):
    del before
    mark[...] = jnp.zeros_like(mark)
    part = ys.shape[1] // TILES
    copies = []
    for t in range(TILES):
        columns = slice(t * part, (t + 1) * part)
        tile = lax.dot_general(hs[...], ys[:, columns], TN, preferred_element_type=F32)
        results[:, columns] = tile.astype(BF16)
        place = pl.ds(t * part, part)
        copies.append(pltpu.make_async_copy(results.at[:, place], down_out.at[:, place], sems.at[t]))
        copies[-1].start()
    for copy in copies:
        copy.wait()


def pair_grads(xs, ps, before):
    total, width = xs.shape
    units = ps.shape[1] // 2
    return pl.pallas_call(
        pair_kernel,
        out_shape=[jax.ShapeDtypeStruct((width, units), BF16)] * 2,
        in_specs=[VMEM, VMEM, ANY],
        out_specs=[HBM] * 2,
        scratch_shapes=[pltpu.VMEM((width, 2 * units), BF16), pltpu.SemaphoreType.DMA((TILES, 2))],
        compiler_params=params(16),
        cost_estimate=cost(4 * total * width * units, 4 * width * units),
        name="pair_grads",
    )(xs, ps, before)


def down_grads(ys, hs, before):
    total, width = ys.shape
    units = hs.shape[1]
    return pl.pallas_call(
        down_kernel,
        out_shape=[jax.ShapeDtypeStruct((units, width), BF16), jax.ShapeDtypeStruct((8, 128), F32)],
        in_specs=[VMEM, VMEM, ANY],
        out_specs=[HBM, VMEM],
        scratch_shapes=[pltpu.VMEM((units, width), BF16), pltpu.SemaphoreType.DMA((TILES,))],
        compiler_params=params(12),
        cost_estimate=cost(2 * total * width * units, 2 * width * units),
        name="down_grads",
    )(ys, hs, before)


def place_kernel(back, *refs):
    units, out = refs[:-1], refs[-1]
    rows = jnp.concatenate([unit[...] for unit in units], axis=0)
    out[...] = jnp.dot(back[...], rows, preferred_element_type=F32).astype(BF16)


def place_rows(back, units):
    count, width = back.shape[0], units[0].shape[1]
    return pl.pallas_call(
        place_kernel,
        out_shape=jax.ShapeDtypeStruct((count, width), BF16),
        in_specs=[VMEM] * (1 + len(units)),
        out_specs=VMEM,
        compiler_params=params(16),
        cost_estimate=cost(2 * count * count * width, 4 * count * width),
        name="place_rows",
    )(back, *units)


def on_device(tokens, grad_out, routes, order, w_gate, w_up, w_down):
    experts = lax.axis_size("expert")
    shards = lax.axis_size("et")
    local_tokens, width = tokens.shape
    slot_cap = local_tokens // experts
    rows = local_tokens // GROUPS

    def over_expert(a, k):
        if k == 0:
            return a
        return lax.ppermute(a, "expert", [(i, i ^ k) for i in range(experts)])

    def over_et(a, m):
        return lax.ppermute(a, "et", [(i, i ^ m) for i in range(shards)])

    def span(unit):
        group, first, parts = unit
        low = group * rows + first * rows // PARTS
        return low, low + parts * rows // PARTS

    def exchange(a, unit):
        low, high = span(unit)
        pieces = []
        at = low
        while at < high:
            k = at // slot_cap
            end = min(high, (k + 1) * slot_cap)
            whole_unit = (at, end) == (low, high)
            pieces.append(over_expert(a if whole_unit else a[at - low : end - low], k))
            at = end
        return pieces[0] if len(pieces) == 1 else jnp.concatenate(pieces, axis=0)

    units = [unit for piece in PIECES for unit in piece]
    spans = [span(unit) for unit in units]
    *sends, back = select_rows(tokens, grad_out, routes, order, slot_cap, spans)
    sends = dict(zip(units, sends))

    arrived = {}
    for unit in units:
        arrived[unit] = exchange(sends[unit], unit)

    weights = None
    ways = shards // 2
    kept, returned = {}, {}
    before, gates, returns = [], [], []
    everything, first = [], 0
    for step, piece in enumerate(PIECES):
        last = step == len(PIECES) - 1
        near = []
        for unit in piece:
            mine = [arrived[unit]]
            for m in range(2, shards, 2):
                mine.append(over_et(arrived[unit], m))
            if weights is None:
                *weights, mine[-1] = load_weights(w_gate[0], w_up[0], w_down[0], mine[-1])
            if last:
                mine[-1] = after(mine[-1], *before)
            near += mine
        far = [over_et(a, 1) for a in near]
        *everything, away, keep = chunk_backward(
            near + far, weights, first, shards * local_tokens, everything, before + gates
        )
        first += 2 * keep.shape[0]
        before = [away]
        many = keep.shape[0] // len(piece)
        for i, unit in enumerate(piece):
            kept[unit] = keep[i * many : (i + 1) * many], away[i * many : (i + 1) * many]
        for group in RETURNS[step]:
            own, sent = [], [[] for _ in range(ways - 1)]
            for unit in group:
                keep, away = kept[unit]
                summed = keep + over_et(away, 1).astype(F32)
                many = keep.shape[0] // ways
                own.append(summed[:many])
                for w in range(1, ways):
                    sent[w - 1].append(summed[w * many : (w + 1) * many].astype(BF16))
            own = jnp.concatenate(own, axis=0)
            sent = [jnp.concatenate(part, axis=0) for part in sent]
            if not gates:
                gates.append(sent[-1])
            returns.append((group, own, sent))
    xs, ys, hs, ps = everything
    down_grad, mark = down_grads(ys, hs, returns[-1][2][-1])
    part = returns[-1][2][-1]
    done = {}
    group, own, sent = returns[0]
    for w, piece in enumerate(sent, 1):
        own = own + over_et(piece, 2 * w).astype(F32)
    own = own.astype(BF16)
    done[0] = own
    at = 0
    for unit in group:
        low, high = span(unit)
        returned[unit] = exchange(own if len(group) == 1 else own[at : at + high - low], unit)
        at += high - low
    group, own, sent = returns[3]
    for w, piece in enumerate(sent, 1):
        own = own + over_et(piece, 2 * w).astype(F32)
    own = own.astype(BF16)
    own = after(own, mark)
    done[3] = own
    at = 0
    for unit in group:
        low, high = span(unit)
        returned[unit] = exchange(own if len(group) == 1 else own[at : at + high - low], unit)
        at += high - low
    group, own, sent = returns[1]
    for w, piece in enumerate(sent, 1):
        own = own + over_et(piece, 2 * w).astype(F32)
    own = own.astype(BF16)
    own = after(own, done[3])
    done[1] = own
    at = 0
    for unit in group:
        low, high = span(unit)
        returned[unit] = exchange(own if len(group) == 1 else own[at : at + high - low], unit)
        at += high - low
    group, own, sent = returns[2]
    sent = [after(piece, done[3]) for piece in sent]
    for w, piece in enumerate(sent, 1):
        own = own + over_et(piece, 2 * w).astype(F32)
    own = own.astype(BF16)
    done[2] = own
    at = 0
    for unit in group:
        low, high = span(unit)
        returned[unit] = exchange(own if len(group) == 1 else own[at : at + high - low], unit)
        at += high - low
    gate_grad, up_grad = pair_grads(xs, ps, done[3])
    grad_tokens = place_rows(back, [returned[unit] for unit in sorted(units)])
    return grad_tokens, gate_grad[None], up_grad[None], down_grad[None]


def solution(mesh):
    return jax.shard_map(
        on_device,
        mesh=mesh,
        in_specs=(
            P(("groups", "expert", "et"), None),
            P(("groups", "expert", "et"), None),
            P(("groups", "expert", "et"), None),
            P(("groups", "expert", "et"), None),
            P("expert", None, "et"),
            P("expert", None, "et"),
            P("expert", "et", None),
        ),
        out_specs=(
            P(("groups", "expert", "et"), None),
            P(("groups", "expert"), None, "et"),
            P(("groups", "expert"), None, "et"),
            P(("groups", "expert"), "et", None),
        ),
        check_vma=False,
    )
```

time: 68.2 us -> 63 us (0.924)
  Pallas kernels: 20.2 us -> 18.1 us
  waiting for transfers between devices: 21.5 us -> 19.7 us
  starting transfers between devices: 25 us -> 23.7 us
    ppermute x6, starting transfers between devices: 12.7 us -> 10.3 us  [over_expert(): return lax.ppermute(a, 'expert', [(i, i ^ k) for i in range(experts)])]
    pallas_call x5, Pallas kernels: 17.4 us -> 15.3 us  [the longest x2 6.26 us: chunk_backward(): pl.pallas_call(functools.partial(chunk_kernel, n, first), out_shape=[jax....]
    ppermute x6, waiting for transfers between devices: 15.4 us -> 14.1 us  [over_expert(): return lax.ppermute(a, 'expert', [(i, i ^ k) for i in range(experts)])]
    ppermute x18 -> x20, starting transfers between devices: 12.2 us -> 13.4 us  [over_et(): return lax.ppermute(a, 'et', [(i, i ^ m) for i in range(shards)])]
    ppermute x18 -> x20, waiting for transfers between devices: 6.08 us -> 5.56 us  [over_et(): return lax.ppermute(a, 'et', [(i, i ^ m) for i in range(shards)])]
  transfers between devices with their start and end apart: 24 -> 26, of which waited for: 10 -> 9; matrix products, arithmetic and copies ran while one was open for 1% -> 1% of each run, Pallas kernels for 26% -> 24%
where the time goes in v3:
time: 63 us; the launch traced here: 62.9 us
  starting transfers between devices  23.7 us (38%)
  waiting for transfers between devices  19.7 us (31%)
  Pallas kernels  18.1 us (29%)
  between operations  0.84 us (1%)
    ppermute x6, waiting for transfers between devices, over_expert(): return lax.ppermute(a, 'expert', [(i, i ^ k) for i in range(experts)])  14.1 us
    ppermute x20, starting transfers between devices, over_et(): return lax.ppermute(a, 'et', [(i, i ^ m) for i in range(shards)])  13.4 us
    ppermute x6, starting transfers between devices, over_expert(): return lax.ppermute(a, 'expert', [(i, i ^ k) for i in range(experts)])  10.3 us
    pallas_call x2, Pallas kernels, chunk_backward(): pl.pallas_call(functools.partial(chunk_kernel, n, first), out_shape=[jax....  6.26 us
    ppermute x20, waiting for transfers between devices, over_et(): return lax.ppermute(a, 'et', [(i, i ^ m) for i in range(shards)])  5.56 us
    pallas_call x1, Pallas kernels, load_weights(): pl.pallas_call(load_kernel, out_shape=[jax.ShapeDtypeStruct((width, 2 * u...  3.53 us
    pallas_call x1, Pallas kernels, pair_grads(): pl.pallas_call(pair_kernel, out_shape=[jax.ShapeDtypeStruct((width, units...  3.42 us
    pallas_call x1, Pallas kernels, down_grads(): pl.pallas_call(down_kernel, out_shape=[jax.ShapeDtypeStruct((units, width...  2.12 us
  transfers between devices with their start and end apart: 26, of which 9 were waited for; matrix products, arithmetic and copies ran while one was open for 1% of the time, Pallas kernels for 24%

profile of v3, /device:TPU:0, one launch (start us, length us, event | category | flops | bytes accessed | tf_op | source)
XLA Modules:
  0.0 62.9 jit_solution(5778418909099071841)
XLA Ops:
  0.6 1.7 %select_rows.1 = (bf16[32,4096]{1,0:T(8,128)(2,1)S(1)}, bf16[32,4096]{1,0:T(8,128)(2,1)S(1)}, bf16[32,4096]{1,0:T(8,128)(2,1)S(1)}, bf16[32,4096]{1,0:T(8,128)(2,1)S(1)}, bf16[128,128]{1,0:T(8,128)(2,1)S(1)}) custom-call(bf16[128,2048]{1,0:T(8,128)(2,1)} %tokens.1, bf16[128,2048]{1,0:T(8,128)(2,1)} %grad_out.1, s32[1,128]{1,0:T(1,128)} %bitcast.10, ...), custom_call_target="tpu_custom_call" | custom-call | flops 134217728 | bytes 2097152 | tf_op jit(solution)/shard_map/select_rows/pallas_call | solution.py:92
  2.3 5.1 %collective-permute-start.1 = (bf16[32,4096]{1,0:T(8,128)(2,1)S(1)}, bf16[32,4096]{1,0:T(8,128)(2,1)S(1)}, u32[]{:S(2)}, u32[]{:S(2)}) collective-permute-start(bf16[32,4096]{1,0:T(8,128)(2,1)S(1)} %get-tuple-element.32), channel_id=1, source_target_pairs={{0,12},{4,8},{8,4},{12,0},{1,13},{5,9},{9,5},{13,1},{2,14},{6,10},... | collective-permute-start | bytes 786440 | tf_op jit(solution)/shard_map/ppermute | solution.py:294
  7.4 1.5 %collective-permute-start = (bf16[32,4096]{1,0:T(8,128)(2,1)S(1)}, bf16[32,4096]{1,0:T(8,128)(2,1)S(1)}, u32[]{:S(2)}, u32[]{:S(2)}) collective-permute-start(bf16[32,4096]{1,0:T(8,128)(2,1)S(1)} %get-tuple-element.30.refs_0_), channel_id=1, source_target_pairs={{0,2},{1,3},{2,0},{3,1},{4,6},{5,7},{6,4},{7,5},{8,10},{9,11},{10,... | collective-permute-start | bytes 786440 | tf_op jit(solution)/shard_map/ppermute | solution.py:297
  8.9 0.8 %collective-permute-start.12 = (bf16[32,4096]{1,0:T(8,128)(2,1)S(1)}, bf16[32,4096]{1,0:T(8,128)(2,1)S(1)}, u32[]{:S(2)}, u32[]{:S(2)}) collective-permute-start(bf16[32,4096]{1,0:T(8,128)(2,1)S(1)} %get-tuple-element.39), channel_id=1, source_target_pairs={{0,8},{4,12},{8,0},{12,4},{1,9},{5,13},{9,1},{13,5},{2,10},{6,14},... | collective-permute-start | bytes 786440 | tf_op jit(solution)/shard_map/ppermute | solution.py:294
  9.7 4.9 %collective-permute-done.1.refs_2_ = bf16[32,4096]{1,0:T(8,128)(2,1)S(1)} collective-permute-done((bf16[32,4096]{1,0:T(8,128)(2,1)S(1)}, bf16[32,4096]{1,0:T(8,128)(2,1)S(1)}, u32[]{:S(2)}, u32[]{:S(2)}) %collective-permute-start.1) | collective-permute-done | bytes 262176 | tf_op jit(solution)/shard_map/ppermute | solution.py:294
  14.7 1.7 %collective-permute-start.2 = (bf16[32,4096]{1,0:T(8,128)(2,1)S(1)}, bf16[32,4096]{1,0:T(8,128)(2,1)S(1)}, u32[]{:S(2)}, u32[]{:S(2)}) collective-permute-start(bf16[32,4096]{1,0:T(8,128)(2,1)S(1)} %collective-permute-done.1.refs_2_), channel_id=1, source_target_pairs={{0,2},{1,3},{2,0},{3,1},{4,6},{5,7},{6,4},{7,5},{8,10},{9,11},{10,... | collective-permute-start | bytes 786440 | tf_op jit(solution)/shard_map/ppermute | solution.py:297
  16.4 4.1 %collective-permute-done.3.refs_4_ = bf16[32,4096]{1,0:T(8,128)(2,1)S(1)} collective-permute-done((bf16[32,4096]{1,0:T(8,128)(2,1)S(1)}, bf16[32,4096]{1,0:T(8,128)(2,1)S(1)}, u32[]{:S(2)}, u32[]{:S(2)}) %collective-permute-start.3) | collective-permute-done | bytes 262176 | tf_op jit(solution)/shard_map/ppermute | solution.py:294
  20.5 1.4 %collective-permute-start.4 = (bf16[32,4096]{1,0:T(8,128)(2,1)S(1)}, bf16[32,4096]{1,0:T(8,128)(2,1)S(1)}, u32[]{:S(2)}, u32[]{:S(2)}) collective-permute-start(bf16[32,4096]{1,0:T(8,128)(2,1)S(1)} %collective-permute-done.3.refs_4_), channel_id=1, source_target_pairs={{0,2},{1,3},{2,0},{3,1},{4,6},{5,7},{6,4},{7,5},{8,10},{9,11},{10,... | collective-permute-start | bytes 786440 | tf_op jit(solution)/shard_map/ppermute | solution.py:297
  21.9 3.5 %load_weights.1 = (bf16[2048,1024]{1,0:T(8,128)(2,1)S(1)}, bf16[1024,2048]{1,0:T(8,128)(2,1)S(1)}, bf16[2048,512]{1,0:T(8,128)(2,1)S(1)}, bf16[32,4096]{1,0:T(8,128)(2,1)S(1)}) custom-call(bf16[2048,512]{1,0:T(8,128)(2,1)} %bitcast.7, bf16[2048,512]{1,0:T(8,128)(2,1)} %bitcast.8, bf16[512,2048]{1,0:T(8,128)(2,1)} %bitcast.9, ...), custom_call_target="tpu_custom_call", output_to_operand_aliasing={{3}: (3, {})} | custom-call | tf_op jit(solution)/shard_map/load_weights/pallas_call | solution.py:132
  25.5 4.3 %collective-permute-done.12.refs_0_ = bf16[32,4096]{1,0:T(8,128)(2,1)S(1)} collective-permute-done((bf16[32,4096]{1,0:T(8,128)(2,1)S(1)}, bf16[32,4096]{1,0:T(8,128)(2,1)S(1)}, u32[]{:S(2)}, u32[]{:S(2)}) %collective-permute-start.12) | collective-permute-done | bytes 262176 | tf_op jit(solution)/shard_map/ppermute | solution.py:294
  29.7 0.5 collective-permute-start.9
  30.3 0.4 collective-permute-start.10
  30.8 0.5 collective-permute-done.7.refs_8_
  31.3 1.5 %collective-permute-start.13 = (bf16[32,4096]{1,0:T(8,128)(2,1)S(1)}, bf16[32,4096]{1,0:T(8,128)(2,1)S(1)}, u32[]{:S(2)}, u32[]{:S(2)}) collective-permute-start(bf16[32,4096]{1,0:T(8,128)(2,1)S(1)} %collective-permute-done.12.refs_0_), channel_id=1, source_target_pairs={{0,2},{1,3},{2,0},{3,1},{4,6},{5,7},{6,4},{7,5},{8,10},{9,11},{10,... | collective-permute-start | bytes 786440 | tf_op jit(solution)/shard_map/ppermute | solution.py:297
  32.8 4.5 %chunk_backward.2 = (bf16[512,2048]{1,0:T(8,128)(2,1)S(1)}, bf16[512,2048]{1,0:T(8,128)(2,1)S(1)}, bf16[512,512]{1,0:T(8,128)(2,1)S(1)}, bf16[512,1024]{1,0:T(8,...) custom-call(bf16[32,4096]{1,0:T(8,128)(2,1)S(1)} %get-tuple-element.30.refs_0_, ...), custom_call_target="tpu_custom_call" | custom-call | flops 4026531840 | bytes 6291456 | tf_op jit(solution)/shard_map/chunk_backward/pallas_call | solution.py:183
  37.5 0.5 collective-permute-start.16
  38.1 0.4 collective-permute-start.14
  38.5 1.1 %collective-permute-done.13.refs_0_ = bf16[32,4096]{1,0:T(8,128)(2,1)S(1)} collective-permute-done((bf16[32,4096]{1,0:T(8,128)(2,1)S(1)}, bf16[32,4096]{1,0:T(8,128)(2,1)S(1)}, u32[]{:S(2)}, u32[]{:S(2)}) %collective-permute-start.13) | collective-permute-done | bytes 262176 | tf_op jit(solution)/shard_map/ppermute | solution.py:297
  39.8 0.2 convert_add_fusion
  40.0 1.5 %collective-permute-start.24 = (bf16[32,2048]{1,0:T(8,128)(2,1)S(1)}, bf16[32,2048]{1,0:T(8,128)(2,1)S(1)}, u32[]{:S(2)}, u32[]{:S(2)}) collective-permute-start(bf16[32,2048]{1,0:T(8,128)(2,1)S(1)} %slice.89.refs_12_), channel_id=1, source_target_pairs={{0,2},{1,3},{2,0},{3,1},{4,6},{5,7},{6,4},{7,5},{8,10},{9,11},{10,... | collective-permute-start | bytes 393224 | tf_op jit(solution)/shard_map/ppermute | solution.py:297
  41.5 0.7 %collective-permute-start.21 = (bf16[32,2048]{1,0:T(8,128)(2,1)S(1)}, bf16[32,2048]{1,0:T(8,128)(2,1)S(1)}, u32[]{:S(2)}, u32[]{:S(2)}) collective-permute-start(bf16[32,2048]{1,0:T(8,128)(2,1)S(1)} %slice.87), channel_id=1, source_target_pairs={{0,2},{1,3},{2,0},{3,1},{4,6},{5,7},{6,4},{7,5},{8,10},{9,11},{10,... | collective-permute-start | bytes 393224 | tf_op jit(solution)/shard_map/ppermute | solution.py:297
  42.2 1.7 %chunk_backward.3 = (bf16[512,2048]{1,0:T(8,128)(2,1)S(1)}, bf16[512,2048]{1,0:T(8,128)(2,1)S(1)}, bf16[512,512]{1,0:T(8,128)(2,1)S(1)}, bf16[512,1024]{1,0:T(8,...) custom-call(bf16[32,4096]{1,0:T(8,128)(2,1)S(1)} %collective-permute, ...), custom_call_target="tpu_custom_call", output_to_operand_aliasing={{0}: (7, {}), {1}: (8, {}), {2}: (9, {}), {3}: (10, {})} | custom-call | flops 1342177280 | bytes 6291456 | tf_op jit(solution)/shard_map/chunk_backward/pallas_call | solution.py:183
  44.0 2.3 %collective-permute-done.24 = bf16[32,2048]{1,0:T(8,128)(2,1)S(1)} collective-permute-done((bf16[32,2048]{1,0:T(8,128)(2,1)S(1)}, bf16[32,2048]{1,0:T(8,128)(2,1)S(1)}, u32[]{:S(2)}, u32[]{:S(2)}) %collective-permute-start.24) | collective-permute-done | bytes 131104 | tf_op jit(solution)/shard_map/ppermute | solution.py:297
  46.4 2.5 %collective-permute-start.25 = (bf16[32,2048]{1,0:T(8,128)(2,1)S(1)}, bf16[32,2048]{1,0:T(8,128)(2,1)S(1)}, u32[]{:S(2)}, u32[]{:S(2)}) collective-permute-start(bf16[32,2048]{1,0:T(8,128)(2,1)S(1)} %fusion), channel_id=1, source_target_pairs={{0,12},{4,8},{8,4},{12,0},{1,13},{5,9},{9,5},{13,1},{2,14},{6,10},... | collective-permute-start | bytes 393224 | tf_op jit(solution)/shard_map/ppermute | solution.py:294
  49.0 1.4 %collective-permute-start.18 = (bf16[32,2048]{1,0:T(8,128)(2,1)S(1)}, bf16[32,2048]{1,0:T(8,128)(2,1)S(1)}, u32[]{:S(2)}, u32[]{:S(2)}) collective-permute-start(bf16[32,2048]{1,0:T(8,128)(2,1)S(1)} %slice.88.before), channel_id=1, source_target_pairs={{0,2},{1,3},{2,0},{3,1},{4,6},{5,7},{6,4},{7,5},{8,10},{9,11},{10,... | collective-permute-start | bytes 393224 | tf_op jit(solution)/shard_map/ppermute | solution.py:297
  50.5 2.1 %down_grads.1 = (bf16[512,2048]{1,0:T(8,128)(2,1)}, f32[8,128]{1,0:T(8,128)S(1)}) custom-call(bf16[512,2048]{1,0:T(8,128)(2,1)S(1)} %get-tuple-element.46.ys, bf16[512,512]{1,0:T(8,128)(2,1)S(1)} %get-tuple-element.47.hs, bf16[32,2048]{1,0:T(8,128)(2,1)S(1)} %slice.88.before), custom_call_target="tpu_custom_call" | custom-call | flops 1073741824 | bytes 2097152 | tf_op jit(solution)/shard_map/down_grads/pallas_call | solution.py:253
  52.6 1.4 %collective-permute-done.18 = bf16[32,2048]{1,0:T(8,128)(2,1)S(1)} collective-permute-done((bf16[32,2048]{1,0:T(8,128)(2,1)S(1)}, bf16[32,2048]{1,0:T(8,128)(2,1)S(1)}, u32[]{:S(2)}, u32[]{:S(2)}) %collective-permute-start.18) | collective-permute-done | bytes 131104 | tf_op jit(solution)/shard_map/ppermute | solution.py:297
  54.2 1.5 %collective-permute-start.19 = (bf16[32,2048]{1,0:T(8,128)(2,1)S(1)}, bf16[32,2048]{1,0:T(8,128)(2,1)S(1)}, u32[]{:S(2)}, u32[]{:S(2)}) collective-permute-start(bf16[32,2048]{1,0:T(8,128)(2,1)S(1)} %after.6), channel_id=1, source_target_pairs={{0,2},{1,3},{2,0},{3,1},{4,6},{5,7},{6,4},{7,5},{8,10},{9,11},{10,... | collective-permute-start | bytes 393224 | tf_op jit(solution)/shard_map/ppermute | solution.py:297
  55.7 1.8 %collective-permute-start.22 = (bf16[32,2048]{1,0:T(8,128)(2,1)S(1)}, bf16[32,2048]{1,0:T(8,128)(2,1)S(1)}, u32[]{:S(2)}, u32[]{:S(2)}) collective-permute-start(bf16[32,2048]{1,0:T(8,128)(2,1)S(1)} %after.7), channel_id=1, source_target_pairs={{0,4},{4,0},{8,12},{12,8},{1,5},{5,1},{9,13},{13,9},{2,6},{6,2},{1... | collective-permute-start | bytes 393224 | tf_op jit(solution)/shard_map/ppermute | solution.py:294
  57.5 3.4 %pair_grads.1 = (bf16[2048,512]{1,0:T(8,128)(2,1)}, bf16[2048,512]{1,0:T(8,128)(2,1)}) custom-call(bf16[512,2048]{1,0:T(8,128)(2,1)S(1)} %get-tuple-element.49.xs, bf16[512,1024]{1,0:T(8,128)(2,1)S(1)} %get-tuple-element.50.ps, bf16[32,2048]{1,0:T(8,128)(2,1)S(1)} %after.5.refs_1_.before), custom_call_target="tpu_custom_call" | custom-call | flops 2147483648 | bytes 4194304 | tf_op jit(solution)/shard_map/pair_grads/pallas_call | solution.py:238
  61.0 0.8 %collective-permute-done.22.refs_1_ = bf16[32,2048]{1,0:T(8,128)(2,1)S(1)} collective-permute-done((bf16[32,2048]{1,0:T(8,128)(2,1)S(1)}, bf16[32,2048]{1,0:T(8,128)(2,1)S(1)}, u32[]{:S(2)}, u32[]{:S(2)}) %collective-permute-start.22) | collective-permute-done | bytes 131104 | tf_op jit(solution)/shard_map/ppermute | solution.py:294
  61.8 1.1 %place_rows.1 = bf16[128,2048]{1,0:T(8,128)(2,1)} custom-call(bf16[128,128]{1,0:T(8,128)(2,1)S(1)} %get-tuple-element.29.back, bf16[32,2048]{1,0:T(8,128)(2,1)S(1)} %fusion.3.refs_0_, bf16[32,2048]{1,0:T(8,128)(2,1)S(1)} %collective-permute-done.22.refs_1_, bf16[32,2048]{1,0:T(8,128)(2,1)S(1)} %collective-permute-done.23.refs_2_, ...), custom_call_target="tpu_custom_call" | custom-call | flops 67108864 | bytes 1048576 | tf_op jit(solution)/shard_map/place_rows/pallas_call | solution.py:273
  (42 shorter events, 0.9 us)
Async XLA Ops:
  2.3 12.3 %collective-permute-start.1 = (bf16[32,4096]{1,0:T(8,128)(2,1)S(1)}, bf16[32,4096]{1,0:T(8,128)(2,1)S(1)}, u32[]{:S(2)}, u32[]{:S(2)}) collective-permute-start(bf16[32,4096]{1,0:T(8,128)(2,1)S(1)} %get-tuple-element.32), channel_id=1, source_target_pairs={{0,12},{4,8},{8,4},{12,0},{1,13},{5,9},{9,5},{13,1},{2,14},{6,10},... | collective-permute-start | bytes 786440 | tf_op jit(solution)/shard_map/ppermute | solution.py:294
  7.4 13.1 %collective-permute-start.3 = (bf16[32,4096]{1,0:T(8,128)(2,1)S(1)}, bf16[32,4096]{1,0:T(8,128)(2,1)S(1)}, u32[]{:S(2)}, u32[]{:S(2)}) collective-permute-start(bf16[32,4096]{1,0:T(8,128)(2,1)S(1)} %get-tuple-element.33), channel_id=1, source_target_pairs={{0,4},{4,0},{8,12},{12,8},{1,5},{5,1},{9,13},{13,9},{2,6},{6,2},{1... | collective-permute-start | bytes 786440 | tf_op jit(solution)/shard_map/ppermute | solution.py:294
  7.4 14.4 %collective-permute-start = (bf16[32,4096]{1,0:T(8,128)(2,1)S(1)}, bf16[32,4096]{1,0:T(8,128)(2,1)S(1)}, u32[]{:S(2)}, u32[]{:S(2)}) collective-permute-start(bf16[32,4096]{1,0:T(8,128)(2,1)S(1)} %get-tuple-element.30.refs_0_), channel_id=1, source_target_pairs={{0,2},{1,3},{2,0},{3,1},{4,6},{5,7},{6,4},{7,5},{8,10},{9,11},{10,... | collective-permute-start | bytes 786440 | tf_op jit(solution)/shard_map/ppermute | solution.py:297
  8.9 20.8 %collective-permute-start.12 = (bf16[32,4096]{1,0:T(8,128)(2,1)S(1)}, bf16[32,4096]{1,0:T(8,128)(2,1)S(1)}, u32[]{:S(2)}, u32[]{:S(2)}) collective-permute-start(bf16[32,4096]{1,0:T(8,128)(2,1)S(1)} %get-tuple-element.39), channel_id=1, source_target_pairs={{0,8},{4,12},{8,0},{12,4},{1,9},{5,13},{9,1},{13,5},{2,10},{6,14},... | collective-permute-start | bytes 786440 | tf_op jit(solution)/shard_map/ppermute | solution.py:294
  9.7 20.0 %collective-permute-start.5 = (bf16[32,4096]{1,0:T(8,128)(2,1)S(1)}, bf16[32,4096]{1,0:T(8,128)(2,1)S(1)}, u32[]{:S(2)}, u32[]{:S(2)}) collective-permute-start(bf16[32,4096]{1,0:T(8,128)(2,1)S(1)} %get-tuple-element.30.refs_0_), channel_id=1, source_target_pairs={{0,1},{1,0},{2,3},{3,2},{4,5},{5,4},{6,7},{7,6},{8,9},{9,8},{10,11... | collective-permute-start | bytes 786440 | tf_op jit(solution)/shard_map/ppermute | solution.py:297
  14.7 15.6 %collective-permute-start.2 = (bf16[32,4096]{1,0:T(8,128)(2,1)S(1)}, bf16[32,4096]{1,0:T(8,128)(2,1)S(1)}, u32[]{:S(2)}, u32[]{:S(2)}) collective-permute-start(bf16[32,4096]{1,0:T(8,128)(2,1)S(1)} %collective-permute-done.1.refs_2_), channel_id=1, source_target_pairs={{0,2},{1,3},{2,0},{3,1},{4,6},{5,7},{6,4},{7,5},{8,10},{9,11},{10,... | collective-permute-start | bytes 786440 | tf_op jit(solution)/shard_map/ppermute | solution.py:297
  20.5 9.8 %collective-permute-start.4 = (bf16[32,4096]{1,0:T(8,128)(2,1)S(1)}, bf16[32,4096]{1,0:T(8,128)(2,1)S(1)}, u32[]{:S(2)}, u32[]{:S(2)}) collective-permute-start(bf16[32,4096]{1,0:T(8,128)(2,1)S(1)} %collective-permute-done.3.refs_4_), channel_id=1, source_target_pairs={{0,2},{1,3},{2,0},{3,1},{4,6},{5,7},{6,4},{7,5},{8,10},{9,11},{10,... | collective-permute-start | bytes 786440 | tf_op jit(solution)/shard_map/ppermute | solution.py:297
  25.4 7.4 %collective-permute-start.6 = (bf16[32,4096]{1,0:T(8,128)(2,1)S(1)}, bf16[32,4096]{1,0:T(8,128)(2,1)S(1)}, u32[]{:S(2)}, u32[]{:S(2)}) collective-permute-start(bf16[32,4096]{1,0:T(8,128)(2,1)S(1)} %get-tuple-element.31.refs_1_), channel_id=1, source_target_pairs={{0,1},{1,0},{2,3},{3,2},{4,5},{5,4},{6,7},{7,6},{8,9},{9,8},{10,11... | collective-permute-start | bytes 786440 | tf_op jit(solution)/shard_map/ppermute | solution.py:297
  29.7 1.5 %collective-permute-start.7 = (bf16[32,4096]{1,0:T(8,128)(2,1)S(1)}, bf16[32,4096]{1,0:T(8,128)(2,1)S(1)}, u32[]{:S(2)}, u32[]{:S(2)}) collective-permute-start(bf16[32,4096]{1,0:T(8,128)(2,1)S(1)} %collective-permute-done.1.refs_2_), channel_id=1, source_target_pairs={{0,1},{1,0},{2,3},{3,2},{4,5},{5,4},{6,7},{7,6},{8,9},{9,8},{10,11... | collective-permute-start | bytes 786440 | tf_op jit(solution)/shard_map/ppermute | solution.py:297
  29.7 3.0 %collective-permute-start.9 = (bf16[32,4096]{1,0:T(8,128)(2,1)S(1)}, bf16[32,4096]{1,0:T(8,128)(2,1)S(1)}, u32[]{:S(2)}, u32[]{:S(2)}) collective-permute-start(bf16[32,4096]{1,0:T(8,128)(2,1)S(1)} %collective-permute-done.3.refs_4_), channel_id=1, source_target_pairs={{0,1},{1,0},{2,3},{3,2},{4,5},{5,4},{6,7},{7,6},{8,9},{9,8},{10,11... | collective-permute-start | bytes 786440 | tf_op jit(solution)/shard_map/ppermute | solution.py:297
  30.3 2.5 %collective-permute-start.8 = (bf16[32,4096]{1,0:T(8,128)(2,1)S(1)}, bf16[32,4096]{1,0:T(8,128)(2,1)S(1)}, u32[]{:S(2)}, u32[]{:S(2)}) collective-permute-start(bf16[32,4096]{1,0:T(8,128)(2,1)S(1)} %collective-permute-done.2.refs_3_), channel_id=1, source_target_pairs={{0,1},{1,0},{2,3},{3,2},{4,5},{5,4},{6,7},{7,6},{8,9},{9,8},{10,11... | collective-permute-start | bytes 786440 | tf_op jit(solution)/shard_map/ppermute | solution.py:297
  30.3 2.5 %collective-permute-start.10 = (bf16[32,4096]{1,0:T(8,128)(2,1)S(1)}, bf16[32,4096]{1,0:T(8,128)(2,1)S(1)}, u32[]{:S(2)}, u32[]{:S(2)}) collective-permute-start(bf16[32,4096]{1,0:T(8,128)(2,1)S(1)} %collective-permute-done.4.refs_5_), channel_id=1, source_target_pairs={{0,1},{1,0},{2,3},{3,2},{4,5},{5,4},{6,7},{7,6},{8,9},{9,8},{10,11... | collective-permute-start | bytes 786440 | tf_op jit(solution)/shard_map/ppermute | solution.py:297
  31.3 8.3 %collective-permute-start.13 = (bf16[32,4096]{1,0:T(8,128)(2,1)S(1)}, bf16[32,4096]{1,0:T(8,128)(2,1)S(1)}, u32[]{:S(2)}, u32[]{:S(2)}) collective-permute-start(bf16[32,4096]{1,0:T(8,128)(2,1)S(1)} %collective-permute-done.12.refs_0_), channel_id=1, source_target_pairs={{0,2},{1,3},{2,0},{3,1},{4,6},{5,7},{6,4},{7,5},{8,10},{9,11},{10,... | collective-permute-start | bytes 786440 | tf_op jit(solution)/shard_map/ppermute | solution.py:297
  37.4 2.2 %collective-permute-start.20 = (bf16[64,2048]{1,0:T(8,128)(2,1)S(1)}, bf16[64,2048]{1,0:T(8,128)(2,1)S(1)}, u32[]{:S(2)}, u32[]{:S(2)}) collective-permute-start(bf16[64,2048]{1,0:T(8,128)(2,1)S(1)} %get-tuple-element.57), channel_id=1, source_target_pairs={{0,1},{1,0},{2,3},{3,2},{4,5},{5,4},{6,7},{7,6},{8,9},{9,8},{10,11... | collective-permute-start | bytes 786440 | tf_op jit(solution)/shard_map/ppermute | solution.py:297
  37.5 2.2 %collective-permute-start.16 = (bf16[64,2048]{1,0:T(8,128)(2,1)S(1)}, bf16[64,2048]{1,0:T(8,128)(2,1)S(1)}, u32[]{:S(2)}, u32[]{:S(2)}) collective-permute-start(bf16[64,2048]{1,0:T(8,128)(2,1)S(1)} %get-tuple-element.58), channel_id=1, source_target_pairs={{0,1},{1,0},{2,3},{3,2},{4,5},{5,4},{6,7},{7,6},{8,9},{9,8},{10,11... | collective-permute-start | bytes 786440 | tf_op jit(solution)/shard_map/ppermute | solution.py:297
  38.0 1.8 %collective-permute-start.11 = (bf16[64,2048]{1,0:T(8,128)(2,1)S(1)}, bf16[64,2048]{1,0:T(8,128)(2,1)S(1)}, u32[]{:S(2)}, u32[]{:S(2)}) collective-permute-start(bf16[64,2048]{1,0:T(8,128)(2,1)S(1)} %get-tuple-element.59), channel_id=1, source_target_pairs={{0,1},{1,0},{2,3},{3,2},{4,5},{5,4},{6,7},{7,6},{8,9},{9,8},{10,11... | collective-permute-start | bytes 786440 | tf_op jit(solution)/shard_map/ppermute | solution.py:297
  38.1 4.2 %collective-permute-start.14 = (bf16[32,4096]{1,0:T(8,128)(2,1)S(1)}, bf16[32,4096]{1,0:T(8,128)(2,1)S(1)}, u32[]{:S(2)}, u32[]{:S(2)}) collective-permute-start(bf16[32,4096]{1,0:T(8,128)(2,1)S(1)} %collective-permute-done.12.refs_0_), channel_id=1, source_target_pairs={{0,1},{1,0},{2,3},{3,2},{4,5},{5,4},{6,7},{7,6},{8,9},{9,8},{10,11... | collective-permute-start | bytes 786440 | tf_op jit(solution)/shard_map/ppermute | solution.py:297
  39.6 2.6 %collective-permute-start.15 = (bf16[32,4096]{1,0:T(8,128)(2,1)S(1)}, bf16[32,4096]{1,0:T(8,128)(2,1)S(1)}, u32[]{:S(2)}, u32[]{:S(2)}) collective-permute-start(bf16[32,4096]{1,0:T(8,128)(2,1)S(1)} %after.4.refs_1_), channel_id=1, source_target_pairs={{0,1},{1,0},{2,3},{3,2},{4,5},{5,4},{6,7},{7,6},{8,9},{9,8},{10,11... | collective-permute-start | bytes 786440 | tf_op jit(solution)/shard_map/ppermute | solution.py:297
  40.0 6.4 %collective-permute-start.24 = (bf16[32,2048]{1,0:T(8,128)(2,1)S(1)}, bf16[32,2048]{1,0:T(8,128)(2,1)S(1)}, u32[]{:S(2)}, u32[]{:S(2)}) collective-permute-start(bf16[32,2048]{1,0:T(8,128)(2,1)S(1)} %slice.89.refs_12_), channel_id=1, source_target_pairs={{0,2},{1,3},{2,0},{3,1},{4,6},{5,7},{6,4},{7,5},{8,10},{9,11},{10,... | collective-permute-start | bytes 393224 | tf_op jit(solution)/shard_map/ppermute | solution.py:297
  41.5 9.0 %collective-permute-start.21 = (bf16[32,2048]{1,0:T(8,128)(2,1)S(1)}, bf16[32,2048]{1,0:T(8,128)(2,1)S(1)}, u32[]{:S(2)}, u32[]{:S(2)}) collective-permute-start(bf16[32,2048]{1,0:T(8,128)(2,1)S(1)} %slice.87), channel_id=1, source_target_pairs={{0,2},{1,3},{2,0},{3,1},{4,6},{5,7},{6,4},{7,5},{8,10},{9,11},{10,... | collective-permute-start | bytes 393224 | tf_op jit(solution)/shard_map/ppermute | solution.py:297
  44.0 5.0 %collective-permute-start.17 = (bf16[64,2048]{1,0:T(8,128)(2,1)S(1)}, bf16[64,2048]{1,0:T(8,128)(2,1)S(1)}, u32[]{:S(2)}, u32[]{:S(2)}) collective-permute-start(bf16[64,2048]{1,0:T(8,128)(2,1)S(1)} %get-tuple-element.45), channel_id=1, source_target_pairs={{0,1},{1,0},{2,3},{3,2},{4,5},{5,4},{6,7},{7,6},{8,9},{9,8},{10,11... | collective-permute-start | bytes 786440 | tf_op jit(solution)/shard_map/ppermute | solution.py:297
  46.4 14.6 %collective-permute-start.25 = (bf16[32,2048]{1,0:T(8,128)(2,1)S(1)}, bf16[32,2048]{1,0:T(8,128)(2,1)S(1)}, u32[]{:S(2)}, u32[]{:S(2)}) collective-permute-start(bf16[32,2048]{1,0:T(8,128)(2,1)S(1)} %fusion), channel_id=1, source_target_pairs={{0,12},{4,8},{8,4},{12,0},{1,13},{5,9},{9,5},{13,1},{2,14},{6,10},... | collective-permute-start | bytes 393224 | tf_op jit(solution)/shard_map/ppermute | solution.py:294
  49.0 5.0 %collective-permute-start.18 = (bf16[32,2048]{1,0:T(8,128)(2,1)S(1)}, bf16[32,2048]{1,0:T(8,128)(2,1)S(1)}, u32[]{:S(2)}, u32[]{:S(2)}) collective-permute-start(bf16[32,2048]{1,0:T(8,128)(2,1)S(1)} %slice.88.before), channel_id=1, source_target_pairs={{0,2},{1,3},{2,0},{3,1},{4,6},{5,7},{6,4},{7,5},{8,10},{9,11},{10,... | collective-permute-start | bytes 393224 | tf_op jit(solution)/shard_map/ppermute | solution.py:297
  54.1 7.7 %collective-permute-start.23 = (bf16[32,2048]{1,0:T(8,128)(2,1)S(1)}, bf16[32,2048]{1,0:T(8,128)(2,1)S(1)}, u32[]{:S(2)}, u32[]{:S(2)}) collective-permute-start(bf16[32,2048]{1,0:T(8,128)(2,1)S(1)} %after.5.refs_1_.before), channel_id=1, source_target_pairs={{0,8},{4,12},{8,0},{12,4},{1,9},{5,13},{9,1},{13,5},{2,10},{6,14},... | collective-permute-start | bytes 393224 | tf_op jit(solution)/shard_map/ppermute | solution.py:294
  54.2 6.7 %collective-permute-start.19 = (bf16[32,2048]{1,0:T(8,128)(2,1)S(1)}, bf16[32,2048]{1,0:T(8,128)(2,1)S(1)}, u32[]{:S(2)}, u32[]{:S(2)}) collective-permute-start(bf16[32,2048]{1,0:T(8,128)(2,1)S(1)} %after.6), channel_id=1, source_target_pairs={{0,2},{1,3},{2,0},{3,1},{4,6},{5,7},{6,4},{7,5},{8,10},{9,11},{10,... | collective-permute-start | bytes 393224 | tf_op jit(solution)/shard_map/ppermute | solution.py:297
  55.7 6.1 %collective-permute-start.22 = (bf16[32,2048]{1,0:T(8,128)(2,1)S(1)}, bf16[32,2048]{1,0:T(8,128)(2,1)S(1)}, u32[]{:S(2)}, u32[]{:S(2)}) collective-permute-start(bf16[32,2048]{1,0:T(8,128)(2,1)S(1)} %after.7), channel_id=1, source_target_pairs={{0,4},{4,0},{8,12},{12,8},{1,5},{5,1},{9,13},{13,9},{2,6},{6,2},{1... | collective-permute-start | bytes 393224 | tf_op jit(solution)/shard_map/ppermute | solution.py:294

commit v4 on v3

--- a/solution.py
+++ b/solution.py
@@ -263,9 +263,17 @@
 
 
 def place_kernel(back, *refs):
-    units, out = refs[:-1], refs[-1]
-    rows = jnp.concatenate([unit[...] for unit in units], axis=0)
-    out[...] = jnp.dot(back[...], rows, preferred_element_type=F32).astype(BF16)
+    units, (out, results, sems) = refs[:-3], refs[-3:]
+    part = out.shape[1] // TILES
+    copies = []
+    for t in range(TILES):
+        columns = pl.ds(t * part, part)
+        rows = jnp.concatenate([unit[:, columns] for unit in units], axis=0)
+        results[:, columns] = jnp.dot(back[...], rows, preferred_element_type=F32).astype(BF16)
+        copies.append(pltpu.make_async_copy(results.at[:, columns], out.at[:, columns], sems.at[t]))
+        copies[-1].start()
+    for copy in copies:
+        copy.wait()
 
 
 def place_rows(back, units):
@@ -274,7 +282,8 @@
         place_kernel,
         out_shape=jax.ShapeDtypeStruct((count, width), BF16),
         in_specs=[VMEM] * (1 + len(units)),
-        out_specs=VMEM,
+        out_specs=HBM,
+        scratch_shapes=[pltpu.VMEM((count, width), BF16), pltpu.SemaphoreType.DMA((TILES,))],
         compiler_params=params(16),
         cost_estimate=cost(2 * count * count * width, 4 * count * width),
         name="place_rows",
@@ -364,51 +373,19 @@
             returns.append((group, own, sent))
     xs, ys, hs, ps = everything
     down_grad, mark = down_grads(ys, hs, returns[-1][2][-1])
-    part = returns[-1][2][-1]
     done = {}
-    group, own, sent = returns[0]
-    for w, piece in enumerate(sent, 1):
-        own = own + over_et(piece, 2 * w).astype(F32)
-    own = own.astype(BF16)
-    done[0] = own
-    at = 0
-    for unit in group:
-        low, high = span(unit)
-        returned[unit] = exchange(own if len(group) == 1 else own[at : at + high - low], unit)
-        at += high - low
-    group, own, sent = returns[3]
-    for w, piece in enumerate(sent, 1):
-        own = own + over_et(piece, 2 * w).astype(F32)
-    own = own.astype(BF16)
-    own = after(own, mark)
-    done[3] = own
-    at = 0
-    for unit in group:
-        low, high = span(unit)
-        returned[unit] = exchange(own if len(group) == 1 else own[at : at + high - low], unit)
-        at += high - low
-    group, own, sent = returns[1]
-    for w, piece in enumerate(sent, 1):
-        own = own + over_et(piece, 2 * w).astype(F32)
-    own = own.astype(BF16)
-    own = after(own, done[3])
-    done[1] = own
-    at = 0
-    for unit in group:
-        low, high = span(unit)
-        returned[unit] = exchange(own if len(group) == 1 else own[at : at + high - low], unit)
-        at += high - low
-    group, own, sent = returns[2]
-    sent = [after(piece, done[3]) for piece in sent]
-    for w, piece in enumerate(sent, 1):
-        own = own + over_et(piece, 2 * w).astype(F32)
-    own = own.astype(BF16)
-    done[2] = own
-    at = 0
-    for unit in group:
-        low, high = span(unit)
-        returned[unit] = exchange(own if len(group) == 1 else own[at : at + high - low], unit)
-        at += high - low
+    for k in (0, 3, 1, 2):
+        _, own, sent = returns[k]
+        if k == 2:
+            sent = [after(piece, mark) for piece in sent]
+        for w, piece in enumerate(sent, 1):
+            own = own + over_et(piece, 2 * w).astype(F32)
+        done[k] = own.astype(BF16)
+    for k, gate in ((0, None), (3, mark), (1, 3), (2, None)):
+        if gate is not None:
+            done[k] = after(done[k], done[gate] if k == 1 else gate)
+        (unit,) = returns[k][0]
+        returned[unit] = exchange(done[k], unit)
     gate_grad, up_grad = pair_grads(xs, ps, done[3])
     grad_tokens = place_rows(back, [returned[unit] for unit in sorted(units)])
     return grad_tokens, gate_grad[None], up_grad[None], down_grad[None]

time: 63 us -> 62.6 us (level)
  starting transfers between devices: 23.7 us -> 23 us
    ppermute x20, waiting for transfers between devices: 5.56 us -> 6.42 us  [over_et(): return lax.ppermute(a, 'et', [(i, i ^ m) for i in range(shards)])]
    ppermute x20, starting transfers between devices: 13.4 us -> 12.6 us  [over_et(): return lax.ppermute(a, 'et', [(i, i ^ m) for i in range(shards)])]
  transfers between devices with their start and end apart: 26 -> 26, of which waited for: 9 -> 10; matrix products, arithmetic and copies ran while one was open for 1% -> 1% of each run, Pallas kernels for 24% -> 25%
where the time goes in v4:
time: 62.6 us; the launch traced here: 62.4 us
  starting transfers between devices  23 us (37%)
  waiting for transfers between devices  20 us (32%)
  Pallas kernels  18 us (29%)
  between operations  0.83 us (1%)
    ppermute x6, waiting for transfers between devices, over_expert(): return lax.ppermute(a, 'expert', [(i, i ^ k) for i in range(experts)])  13.6 us
    ppermute x20, starting transfers between devices, over_et(): return lax.ppermute(a, 'et', [(i, i ^ m) for i in range(shards)])  12.6 us
    ppermute x6, starting transfers between devices, over_expert(): return lax.ppermute(a, 'expert', [(i, i ^ k) for i in range(experts)])  10.4 us
    ppermute x20, waiting for transfers between devices, over_et(): return lax.ppermute(a, 'et', [(i, i ^ m) for i in range(shards)])  6.42 us
    pallas_call x2, Pallas kernels, chunk_backward(): pl.pallas_call(functools.partial(chunk_kernel, n, first), out_shape=[jax....  6.26 us
    pallas_call x1, Pallas kernels, load_weights(): pl.pallas_call(load_kernel, out_shape=[jax.ShapeDtypeStruct((width, 2 * u...  3.53 us
    pallas_call x1, Pallas kernels, pair_grads(): pl.pallas_call(pair_kernel, out_shape=[jax.ShapeDtypeStruct((width, units...  3.42 us
    pallas_call x1, Pallas kernels, down_grads(): pl.pallas_call(down_kernel, out_shape=[jax.ShapeDtypeStruct((units, width...  2.12 us
  transfers between devices with their start and end apart: 26, of which 10 were waited for; matrix products, arithmetic and copies ran while one was open for 1% of the time, Pallas kernels for 25%

profile of v4, /device:TPU:0, one launch (start us, length us, event | category | flops | bytes accessed | tf_op | source)
XLA Modules:
  0.0 62.4 jit_solution(10664342571048123161)
XLA Ops:
  0.6 1.7 %select_rows.1 = (bf16[32,4096]{1,0:T(8,128)(2,1)S(1)}, bf16[32,4096]{1,0:T(8,128)(2,1)S(1)}, bf16[32,4096]{1,0:T(8,128)(2,1)S(1)}, bf16[32,4096]{1,0:T(8,128)(2,1)S(1)}, bf16[128,128]{1,0:T(8,128)(2,1)S(1)}) custom-call(bf16[128,2048]{1,0:T(8,128)(2,1)} %tokens.1, bf16[128,2048]{1,0:T(8,128)(2,1)} %grad_out.1, s32[1,128]{1,0:T(1,128)} %bitcast.10, ...), custom_call_target="tpu_custom_call" | custom-call | flops 134217728 | bytes 2097152 | tf_op jit(solution)/shard_map/select_rows/pallas_call | solution.py:92
  2.3 5.1 %collective-permute-start.1 = (bf16[32,4096]{1,0:T(8,128)(2,1)S(1)}, bf16[32,4096]{1,0:T(8,128)(2,1)S(1)}, u32[]{:S(2)}, u32[]{:S(2)}) collective-permute-start(bf16[32,4096]{1,0:T(8,128)(2,1)S(1)} %get-tuple-element.32), channel_id=1, source_target_pairs={{0,12},{4,8},{8,4},{12,0},{1,13},{5,9},{9,5},{13,1},{2,14},{6,10},... | collective-permute-start | bytes 786440 | tf_op jit(solution)/shard_map/ppermute | solution.py:303
  7.4 1.5 %collective-permute-start = (bf16[32,4096]{1,0:T(8,128)(2,1)S(1)}, bf16[32,4096]{1,0:T(8,128)(2,1)S(1)}, u32[]{:S(2)}, u32[]{:S(2)}) collective-permute-start(bf16[32,4096]{1,0:T(8,128)(2,1)S(1)} %get-tuple-element.30.refs_0_), channel_id=1, source_target_pairs={{0,2},{1,3},{2,0},{3,1},{4,6},{5,7},{6,4},{7,5},{8,10},{9,11},{10,... | collective-permute-start | bytes 786440 | tf_op jit(solution)/shard_map/ppermute | solution.py:306
  8.9 0.8 %collective-permute-start.12 = (bf16[32,4096]{1,0:T(8,128)(2,1)S(1)}, bf16[32,4096]{1,0:T(8,128)(2,1)S(1)}, u32[]{:S(2)}, u32[]{:S(2)}) collective-permute-start(bf16[32,4096]{1,0:T(8,128)(2,1)S(1)} %get-tuple-element.39), channel_id=1, source_target_pairs={{0,8},{4,12},{8,0},{12,4},{1,9},{5,13},{9,1},{13,5},{2,10},{6,14},... | collective-permute-start | bytes 786440 | tf_op jit(solution)/shard_map/ppermute | solution.py:303
  9.7 4.9 %collective-permute-done.1.refs_2_ = bf16[32,4096]{1,0:T(8,128)(2,1)S(1)} collective-permute-done((bf16[32,4096]{1,0:T(8,128)(2,1)S(1)}, bf16[32,4096]{1,0:T(8,128)(2,1)S(1)}, u32[]{:S(2)}, u32[]{:S(2)}) %collective-permute-start.1) | collective-permute-done | bytes 262176 | tf_op jit(solution)/shard_map/ppermute | solution.py:303
  14.7 1.7 %collective-permute-start.2 = (bf16[32,4096]{1,0:T(8,128)(2,1)S(1)}, bf16[32,4096]{1,0:T(8,128)(2,1)S(1)}, u32[]{:S(2)}, u32[]{:S(2)}) collective-permute-start(bf16[32,4096]{1,0:T(8,128)(2,1)S(1)} %collective-permute-done.1.refs_2_), channel_id=1, source_target_pairs={{0,2},{1,3},{2,0},{3,1},{4,6},{5,7},{6,4},{7,5},{8,10},{9,11},{10,... | collective-permute-start | bytes 786440 | tf_op jit(solution)/shard_map/ppermute | solution.py:306
  16.4 4.1 %collective-permute-done.3.refs_4_ = bf16[32,4096]{1,0:T(8,128)(2,1)S(1)} collective-permute-done((bf16[32,4096]{1,0:T(8,128)(2,1)S(1)}, bf16[32,4096]{1,0:T(8,128)(2,1)S(1)}, u32[]{:S(2)}, u32[]{:S(2)}) %collective-permute-start.3) | collective-permute-done | bytes 262176 | tf_op jit(solution)/shard_map/ppermute | solution.py:303
  20.5 1.4 %collective-permute-start.4 = (bf16[32,4096]{1,0:T(8,128)(2,1)S(1)}, bf16[32,4096]{1,0:T(8,128)(2,1)S(1)}, u32[]{:S(2)}, u32[]{:S(2)}) collective-permute-start(bf16[32,4096]{1,0:T(8,128)(2,1)S(1)} %collective-permute-done.3.refs_4_), channel_id=1, source_target_pairs={{0,2},{1,3},{2,0},{3,1},{4,6},{5,7},{6,4},{7,5},{8,10},{9,11},{10,... | collective-permute-start | bytes 786440 | tf_op jit(solution)/shard_map/ppermute | solution.py:306
  21.9 3.5 %load_weights.1 = (bf16[2048,1024]{1,0:T(8,128)(2,1)S(1)}, bf16[1024,2048]{1,0:T(8,128)(2,1)S(1)}, bf16[2048,512]{1,0:T(8,128)(2,1)S(1)}, bf16[32,4096]{1,0:T(8,128)(2,1)S(1)}) custom-call(bf16[2048,512]{1,0:T(8,128)(2,1)} %bitcast.7, bf16[2048,512]{1,0:T(8,128)(2,1)} %bitcast.8, bf16[512,2048]{1,0:T(8,128)(2,1)} %bitcast.9, ...), custom_call_target="tpu_custom_call", output_to_operand_aliasing={{3}: (3, {})} | custom-call | tf_op jit(solution)/shard_map/load_weights/pallas_call | solution.py:132
  25.5 4.3 %collective-permute-done.12.refs_0_ = bf16[32,4096]{1,0:T(8,128)(2,1)S(1)} collective-permute-done((bf16[32,4096]{1,0:T(8,128)(2,1)S(1)}, bf16[32,4096]{1,0:T(8,128)(2,1)S(1)}, u32[]{:S(2)}, u32[]{:S(2)}) %collective-permute-start.12) | collective-permute-done | bytes 262176 | tf_op jit(solution)/shard_map/ppermute | solution.py:303
  29.7 0.5 collective-permute-start.9
  30.3 0.4 collective-permute-start.10
  30.8 0.5 collective-permute-done.7.refs_8_
  31.3 1.5 %collective-permute-start.13 = (bf16[32,4096]{1,0:T(8,128)(2,1)S(1)}, bf16[32,4096]{1,0:T(8,128)(2,1)S(1)}, u32[]{:S(2)}, u32[]{:S(2)}) collective-permute-start(bf16[32,4096]{1,0:T(8,128)(2,1)S(1)} %collective-permute-done.12.refs_0_), channel_id=1, source_target_pairs={{0,2},{1,3},{2,0},{3,1},{4,6},{5,7},{6,4},{7,5},{8,10},{9,11},{10,... | collective-permute-start | bytes 786440 | tf_op jit(solution)/shard_map/ppermute | solution.py:306
  32.8 4.5 %chunk_backward.2 = (bf16[512,2048]{1,0:T(8,128)(2,1)S(1)}, bf16[512,2048]{1,0:T(8,128)(2,1)S(1)}, bf16[512,512]{1,0:T(8,128)(2,1)S(1)}, bf16[512,1024]{1,0:T(8,...) custom-call(bf16[32,4096]{1,0:T(8,128)(2,1)S(1)} %get-tuple-element.30.refs_0_, ...), custom_call_target="tpu_custom_call" | custom-call | flops 4026531840 | bytes 6291456 | tf_op jit(solution)/shard_map/chunk_backward/pallas_call | solution.py:183
  37.5 0.5 collective-permute-start.16
  38.1 0.4 collective-permute-start.14
  38.5 1.1 %collective-permute-done.13.refs_0_ = bf16[32,4096]{1,0:T(8,128)(2,1)S(1)} collective-permute-done((bf16[32,4096]{1,0:T(8,128)(2,1)S(1)}, bf16[32,4096]{1,0:T(8,128)(2,1)S(1)}, u32[]{:S(2)}, u32[]{:S(2)}) %collective-permute-start.13) | collective-permute-done | bytes 262176 | tf_op jit(solution)/shard_map/ppermute | solution.py:306
  40.0 1.5 %collective-permute-start.24 = (bf16[32,2048]{1,0:T(8,128)(2,1)S(1)}, bf16[32,2048]{1,0:T(8,128)(2,1)S(1)}, u32[]{:S(2)}, u32[]{:S(2)}) collective-permute-start(bf16[32,2048]{1,0:T(8,128)(2,1)S(1)} %slice.89.refs_12_), channel_id=1, source_target_pairs={{0,2},{1,3},{2,0},{3,1},{4,6},{5,7},{6,4},{7,5},{8,10},{9,11},{10,... | collective-permute-start | bytes 393224 | tf_op jit(solution)/shard_map/ppermute | solution.py:306
  41.5 0.7 %collective-permute-start.20 = (bf16[32,2048]{1,0:T(8,128)(2,1)S(1)}, bf16[32,2048]{1,0:T(8,128)(2,1)S(1)}, u32[]{:S(2)}, u32[]{:S(2)}) collective-permute-start(bf16[32,2048]{1,0:T(8,128)(2,1)S(1)} %slice.87), channel_id=1, source_target_pairs={{0,2},{1,3},{2,0},{3,1},{4,6},{5,7},{6,4},{7,5},{8,10},{9,11},{10,... | collective-permute-start | bytes 393224 | tf_op jit(solution)/shard_map/ppermute | solution.py:306
  42.2 1.7 %chunk_backward.3 = (bf16[512,2048]{1,0:T(8,128)(2,1)S(1)}, bf16[512,2048]{1,0:T(8,128)(2,1)S(1)}, bf16[512,512]{1,0:T(8,128)(2,1)S(1)}, bf16[512,1024]{1,0:T(8,...) custom-call(bf16[32,4096]{1,0:T(8,128)(2,1)S(1)} %collective-permute, ...), custom_call_target="tpu_custom_call", output_to_operand_aliasing={{0}: (7, {}), {1}: (8, {}), {2}: (9, {}), {3}: (10, {})} | custom-call | flops 1342177280 | bytes 6291456 | tf_op jit(solution)/shard_map/chunk_backward/pallas_call | solution.py:183
  44.0 2.3 %collective-permute-done.24 = bf16[32,2048]{1,0:T(8,128)(2,1)S(1)} collective-permute-done((bf16[32,2048]{1,0:T(8,128)(2,1)S(1)}, bf16[32,2048]{1,0:T(8,128)(2,1)S(1)}, u32[]{:S(2)}, u32[]{:S(2)}) %collective-permute-start.24) | collective-permute-done | bytes 131104 | tf_op jit(solution)/shard_map/ppermute | solution.py:306
  46.4 2.5 %collective-permute-start.25 = (bf16[32,2048]{1,0:T(8,128)(2,1)S(1)}, bf16[32,2048]{1,0:T(8,128)(2,1)S(1)}, u32[]{:S(2)}, u32[]{:S(2)}) collective-permute-start(bf16[32,2048]{1,0:T(8,128)(2,1)S(1)} %fusion), channel_id=1, source_target_pairs={{0,12},{4,8},{8,4},{12,0},{1,13},{5,9},{9,5},{13,1},{2,14},{6,10},... | collective-permute-start | bytes 393224 | tf_op jit(solution)/shard_map/ppermute | solution.py:303
  49.0 1.4 %collective-permute-start.21 = (bf16[32,2048]{1,0:T(8,128)(2,1)S(1)}, bf16[32,2048]{1,0:T(8,128)(2,1)S(1)}, u32[]{:S(2)}, u32[]{:S(2)}) collective-permute-start(bf16[32,2048]{1,0:T(8,128)(2,1)S(1)} %slice.88.before), channel_id=1, source_target_pairs={{0,2},{1,3},{2,0},{3,1},{4,6},{5,7},{6,4},{7,5},{8,10},{9,11},{10,... | collective-permute-start | bytes 393224 | tf_op jit(solution)/shard_map/ppermute | solution.py:306
  50.5 2.1 %down_grads.1 = (bf16[512,2048]{1,0:T(8,128)(2,1)}, f32[8,128]{1,0:T(8,128)S(1)}) custom-call(bf16[512,2048]{1,0:T(8,128)(2,1)S(1)} %get-tuple-element.44.ys, bf16[512,512]{1,0:T(8,128)(2,1)S(1)} %get-tuple-element.45.hs, bf16[32,2048]{1,0:T(8,128)(2,1)S(1)} %slice.88.before), custom_call_target="tpu_custom_call" | custom-call | flops 1073741824 | bytes 2097152 | tf_op jit(solution)/shard_map/down_grads/pallas_call | solution.py:253
  52.7 0.7 %collective-permute-start.18 = (bf16[32,2048]{1,0:T(8,128)(2,1)S(1)}, bf16[32,2048]{1,0:T(8,128)(2,1)S(1)}, u32[]{:S(2)}, u32[]{:S(2)}) collective-permute-start(bf16[32,2048]{1,0:T(8,128)(2,1)S(1)} %after.5), channel_id=1, source_target_pairs={{0,2},{1,3},{2,0},{3,1},{4,6},{5,7},{6,4},{7,5},{8,10},{9,11},{10,... | collective-permute-start | bytes 393224 | tf_op jit(solution)/shard_map/ppermute | solution.py:306
  53.4 0.7 %collective-permute-done.21 = bf16[32,2048]{1,0:T(8,128)(2,1)S(1)} collective-permute-done((bf16[32,2048]{1,0:T(8,128)(2,1)S(1)}, bf16[32,2048]{1,0:T(8,128)(2,1)S(1)}, u32[]{:S(2)}, u32[]{:S(2)}) %collective-permute-start.21) | collective-permute-done | bytes 131104 | tf_op jit(solution)/shard_map/ppermute | solution.py:306
  54.1 0.4 collective-permute-start.23
  54.5 1.6 %collective-permute-start.22 = (bf16[32,2048]{1,0:T(8,128)(2,1)S(1)}, bf16[32,2048]{1,0:T(8,128)(2,1)S(1)}, u32[]{:S(2)}, u32[]{:S(2)}) collective-permute-start(bf16[32,2048]{1,0:T(8,128)(2,1)S(1)} %after.7), channel_id=1, source_target_pairs={{0,4},{4,0},{8,12},{12,8},{1,5},{5,1},{9,13},{13,9},{2,6},{6,2},{1... | collective-permute-start | bytes 393224 | tf_op jit(solution)/shard_map/ppermute | solution.py:303
  56.1 1.6 %collective-permute-done.18 = bf16[32,2048]{1,0:T(8,128)(2,1)S(1)} collective-permute-done((bf16[32,2048]{1,0:T(8,128)(2,1)S(1)}, bf16[32,2048]{1,0:T(8,128)(2,1)S(1)}, u32[]{:S(2)}, u32[]{:S(2)}) %collective-permute-start.18) | collective-permute-done | bytes 131104 | tf_op jit(solution)/shard_map/ppermute | solution.py:306
  57.7 3.4 %pair_grads.1 = (bf16[2048,512]{1,0:T(8,128)(2,1)}, bf16[2048,512]{1,0:T(8,128)(2,1)}) custom-call(bf16[512,2048]{1,0:T(8,128)(2,1)S(1)} %get-tuple-element.49.xs, bf16[512,1024]{1,0:T(8,128)(2,1)S(1)} %get-tuple-element.50.ps, bf16[32,2048]{1,0:T(8,128)(2,1)S(1)} %after.6.refs_1_.before), custom_call_target="tpu_custom_call" | custom-call | flops 2147483648 | bytes 4194304 | tf_op jit(solution)/shard_map/pair_grads/pallas_call | solution.py:238
  61.4 1.0 %place_rows.1 = bf16[128,2048]{1,0:T(8,128)(2,1)} custom-call(bf16[128,128]{1,0:T(8,128)(2,1)S(1)} %get-tuple-element.29.back, bf16[32,2048]{1,0:T(8,128)(2,1)S(1)} %fusion.3.refs_0_, bf16[32,2048]{1,0:T(8,128)(2,1)S(1)} %collective-permute-done.22.refs_1_, bf16[32,2048]{1,0:T(8,128)(2,1)S(1)} %collective-permute-done.23.refs_2_, ...), custom_call_target="tpu_custom_call" | custom-call | flops 67108864 | bytes 1048576 | tf_op jit(solution)/shard_map/place_rows/pallas_call | solution.py:281
  (42 shorter events, 1.3 us)
Async XLA Ops:
  2.3 12.3 %collective-permute-start.1 = (bf16[32,4096]{1,0:T(8,128)(2,1)S(1)}, bf16[32,4096]{1,0:T(8,128)(2,1)S(1)}, u32[]{:S(2)}, u32[]{:S(2)}) collective-permute-start(bf16[32,4096]{1,0:T(8,128)(2,1)S(1)} %get-tuple-element.32), channel_id=1, source_target_pairs={{0,12},{4,8},{8,4},{12,0},{1,13},{5,9},{9,5},{13,1},{2,14},{6,10},... | collective-permute-start | bytes 786440 | tf_op jit(solution)/shard_map/ppermute | solution.py:303
  7.4 13.1 %collective-permute-start.3 = (bf16[32,4096]{1,0:T(8,128)(2,1)S(1)}, bf16[32,4096]{1,0:T(8,128)(2,1)S(1)}, u32[]{:S(2)}, u32[]{:S(2)}) collective-permute-start(bf16[32,4096]{1,0:T(8,128)(2,1)S(1)} %get-tuple-element.33), channel_id=1, source_target_pairs={{0,4},{4,0},{8,12},{12,8},{1,5},{5,1},{9,13},{13,9},{2,6},{6,2},{1... | collective-permute-start | bytes 786440 | tf_op jit(solution)/shard_map/ppermute | solution.py:303
  7.4 14.4 %collective-permute-start = (bf16[32,4096]{1,0:T(8,128)(2,1)S(1)}, bf16[32,4096]{1,0:T(8,128)(2,1)S(1)}, u32[]{:S(2)}, u32[]{:S(2)}) collective-permute-start(bf16[32,4096]{1,0:T(8,128)(2,1)S(1)} %get-tuple-element.30.refs_0_), channel_id=1, source_target_pairs={{0,2},{1,3},{2,0},{3,1},{4,6},{5,7},{6,4},{7,5},{8,10},{9,11},{10,... | collective-permute-start | bytes 786440 | tf_op jit(solution)/shard_map/ppermute | solution.py:306
  8.9 20.8 %collective-permute-start.12 = (bf16[32,4096]{1,0:T(8,128)(2,1)S(1)}, bf16[32,4096]{1,0:T(8,128)(2,1)S(1)}, u32[]{:S(2)}, u32[]{:S(2)}) collective-permute-start(bf16[32,4096]{1,0:T(8,128)(2,1)S(1)} %get-tuple-element.39), channel_id=1, source_target_pairs={{0,8},{4,12},{8,0},{12,4},{1,9},{5,13},{9,1},{13,5},{2,10},{6,14},... | collective-permute-start | bytes 786440 | tf_op jit(solution)/shard_map/ppermute | solution.py:303
  9.7 20.0 %collective-permute-start.5 = (bf16[32,4096]{1,0:T(8,128)(2,1)S(1)}, bf16[32,4096]{1,0:T(8,128)(2,1)S(1)}, u32[]{:S(2)}, u32[]{:S(2)}) collective-permute-start(bf16[32,4096]{1,0:T(8,128)(2,1)S(1)} %get-tuple-element.30.refs_0_), channel_id=1, source_target_pairs={{0,1},{1,0},{2,3},{3,2},{4,5},{5,4},{6,7},{7,6},{8,9},{9,8},{10,11... | collective-permute-start | bytes 786440 | tf_op jit(solution)/shard_map/ppermute | solution.py:306
  14.7 15.6 %collective-permute-start.2 = (bf16[32,4096]{1,0:T(8,128)(2,1)S(1)}, bf16[32,4096]{1,0:T(8,128)(2,1)S(1)}, u32[]{:S(2)}, u32[]{:S(2)}) collective-permute-start(bf16[32,4096]{1,0:T(8,128)(2,1)S(1)} %collective-permute-done.1.refs_2_), channel_id=1, source_target_pairs={{0,2},{1,3},{2,0},{3,1},{4,6},{5,7},{6,4},{7,5},{8,10},{9,11},{10,... | collective-permute-start | bytes 786440 | tf_op jit(solution)/shard_map/ppermute | solution.py:306
  20.5 9.8 %collective-permute-start.4 = (bf16[32,4096]{1,0:T(8,128)(2,1)S(1)}, bf16[32,4096]{1,0:T(8,128)(2,1)S(1)}, u32[]{:S(2)}, u32[]{:S(2)}) collective-permute-start(bf16[32,4096]{1,0:T(8,128)(2,1)S(1)} %collective-permute-done.3.refs_4_), channel_id=1, source_target_pairs={{0,2},{1,3},{2,0},{3,1},{4,6},{5,7},{6,4},{7,5},{8,10},{9,11},{10,... | collective-permute-start | bytes 786440 | tf_op jit(solution)/shard_map/ppermute | solution.py:306
  25.4 7.4 %collective-permute-start.6 = (bf16[32,4096]{1,0:T(8,128)(2,1)S(1)}, bf16[32,4096]{1,0:T(8,128)(2,1)S(1)}, u32[]{:S(2)}, u32[]{:S(2)}) collective-permute-start(bf16[32,4096]{1,0:T(8,128)(2,1)S(1)} %get-tuple-element.31.refs_1_), channel_id=1, source_target_pairs={{0,1},{1,0},{2,3},{3,2},{4,5},{5,4},{6,7},{7,6},{8,9},{9,8},{10,11... | collective-permute-start | bytes 786440 | tf_op jit(solution)/shard_map/ppermute | solution.py:306
  29.7 1.5 %collective-permute-start.7 = (bf16[32,4096]{1,0:T(8,128)(2,1)S(1)}, bf16[32,4096]{1,0:T(8,128)(2,1)S(1)}, u32[]{:S(2)}, u32[]{:S(2)}) collective-permute-start(bf16[32,4096]{1,0:T(8,128)(2,1)S(1)} %collective-permute-done.1.refs_2_), channel_id=1, source_target_pairs={{0,1},{1,0},{2,3},{3,2},{4,5},{5,4},{6,7},{7,6},{8,9},{9,8},{10,11... | collective-permute-start | bytes 786440 | tf_op jit(solution)/shard_map/ppermute | solution.py:306
  29.7 3.0 %collective-permute-start.9 = (bf16[32,4096]{1,0:T(8,128)(2,1)S(1)}, bf16[32,4096]{1,0:T(8,128)(2,1)S(1)}, u32[]{:S(2)}, u32[]{:S(2)}) collective-permute-start(bf16[32,4096]{1,0:T(8,128)(2,1)S(1)} %collective-permute-done.3.refs_4_), channel_id=1, source_target_pairs={{0,1},{1,0},{2,3},{3,2},{4,5},{5,4},{6,7},{7,6},{8,9},{9,8},{10,11... | collective-permute-start | bytes 786440 | tf_op jit(solution)/shard_map/ppermute | solution.py:306
  30.3 2.5 %collective-permute-start.8 = (bf16[32,4096]{1,0:T(8,128)(2,1)S(1)}, bf16[32,4096]{1,0:T(8,128)(2,1)S(1)}, u32[]{:S(2)}, u32[]{:S(2)}) collective-permute-start(bf16[32,4096]{1,0:T(8,128)(2,1)S(1)} %collective-permute-done.2.refs_3_), channel_id=1, source_target_pairs={{0,1},{1,0},{2,3},{3,2},{4,5},{5,4},{6,7},{7,6},{8,9},{9,8},{10,11... | collective-permute-start | bytes 786440 | tf_op jit(solution)/shard_map/ppermute | solution.py:306
  30.3 2.5 %collective-permute-start.10 = (bf16[32,4096]{1,0:T(8,128)(2,1)S(1)}, bf16[32,4096]{1,0:T(8,128)(2,1)S(1)}, u32[]{:S(2)}, u32[]{:S(2)}) collective-permute-start(bf16[32,4096]{1,0:T(8,128)(2,1)S(1)} %collective-permute-done.4.refs_5_), channel_id=1, source_target_pairs={{0,1},{1,0},{2,3},{3,2},{4,5},{5,4},{6,7},{7,6},{8,9},{9,8},{10,11... | collective-permute-start | bytes 786440 | tf_op jit(solution)/shard_map/ppermute | solution.py:306
  31.3 8.3 %collective-permute-start.13 = (bf16[32,4096]{1,0:T(8,128)(2,1)S(1)}, bf16[32,4096]{1,0:T(8,128)(2,1)S(1)}, u32[]{:S(2)}, u32[]{:S(2)}) collective-permute-start(bf16[32,4096]{1,0:T(8,128)(2,1)S(1)} %collective-permute-done.12.refs_0_), channel_id=1, source_target_pairs={{0,2},{1,3},{2,0},{3,1},{4,6},{5,7},{6,4},{7,5},{8,10},{9,11},{10,... | collective-permute-start | bytes 786440 | tf_op jit(solution)/shard_map/ppermute | solution.py:306
  37.4 2.2 %collective-permute-start.19 = (bf16[64,2048]{1,0:T(8,128)(2,1)S(1)}, bf16[64,2048]{1,0:T(8,128)(2,1)S(1)}, u32[]{:S(2)}, u32[]{:S(2)}) collective-permute-start(bf16[64,2048]{1,0:T(8,128)(2,1)S(1)} %get-tuple-element.57), channel_id=1, source_target_pairs={{0,1},{1,0},{2,3},{3,2},{4,5},{5,4},{6,7},{7,6},{8,9},{9,8},{10,11... | collective-permute-start | bytes 786440 | tf_op jit(solution)/shard_map/ppermute | solution.py:306
  37.5 2.2 %collective-permute-start.16 = (bf16[64,2048]{1,0:T(8,128)(2,1)S(1)}, bf16[64,2048]{1,0:T(8,128)(2,1)S(1)}, u32[]{:S(2)}, u32[]{:S(2)}) collective-permute-start(bf16[64,2048]{1,0:T(8,128)(2,1)S(1)} %get-tuple-element.58), channel_id=1, source_target_pairs={{0,1},{1,0},{2,3},{3,2},{4,5},{5,4},{6,7},{7,6},{8,9},{9,8},{10,11... | collective-permute-start | bytes 786440 | tf_op jit(solution)/shard_map/ppermute | solution.py:306
  38.0 1.8 %collective-permute-start.11 = (bf16[64,2048]{1,0:T(8,128)(2,1)S(1)}, bf16[64,2048]{1,0:T(8,128)(2,1)S(1)}, u32[]{:S(2)}, u32[]{:S(2)}) collective-permute-start(bf16[64,2048]{1,0:T(8,128)(2,1)S(1)} %get-tuple-element.59), channel_id=1, source_target_pairs={{0,1},{1,0},{2,3},{3,2},{4,5},{5,4},{6,7},{7,6},{8,9},{9,8},{10,11... | collective-permute-start | bytes 786440 | tf_op jit(solution)/shard_map/ppermute | solution.py:306
  38.1 4.2 %collective-permute-start.14 = (bf16[32,4096]{1,0:T(8,128)(2,1)S(1)}, bf16[32,4096]{1,0:T(8,128)(2,1)S(1)}, u32[]{:S(2)}, u32[]{:S(2)}) collective-permute-start(bf16[32,4096]{1,0:T(8,128)(2,1)S(1)} %collective-permute-done.12.refs_0_), channel_id=1, source_target_pairs={{0,1},{1,0},{2,3},{3,2},{4,5},{5,4},{6,7},{7,6},{8,9},{9,8},{10,11... | collective-permute-start | bytes 786440 | tf_op jit(solution)/shard_map/ppermute | solution.py:306
  39.6 2.6 %collective-permute-start.15 = (bf16[32,4096]{1,0:T(8,128)(2,1)S(1)}, bf16[32,4096]{1,0:T(8,128)(2,1)S(1)}, u32[]{:S(2)}, u32[]{:S(2)}) collective-permute-start(bf16[32,4096]{1,0:T(8,128)(2,1)S(1)} %after.4.refs_1_), channel_id=1, source_target_pairs={{0,1},{1,0},{2,3},{3,2},{4,5},{5,4},{6,7},{7,6},{8,9},{9,8},{10,11... | collective-permute-start | bytes 786440 | tf_op jit(solution)/shard_map/ppermute | solution.py:306
  40.0 6.4 %collective-permute-start.24 = (bf16[32,2048]{1,0:T(8,128)(2,1)S(1)}, bf16[32,2048]{1,0:T(8,128)(2,1)S(1)}, u32[]{:S(2)}, u32[]{:S(2)}) collective-permute-start(bf16[32,2048]{1,0:T(8,128)(2,1)S(1)} %slice.89.refs_12_), channel_id=1, source_target_pairs={{0,2},{1,3},{2,0},{3,1},{4,6},{5,7},{6,4},{7,5},{8,10},{9,11},{10,... | collective-permute-start | bytes 393224 | tf_op jit(solution)/shard_map/ppermute | solution.py:306
  41.5 9.0 %collective-permute-start.20 = (bf16[32,2048]{1,0:T(8,128)(2,1)S(1)}, bf16[32,2048]{1,0:T(8,128)(2,1)S(1)}, u32[]{:S(2)}, u32[]{:S(2)}) collective-permute-start(bf16[32,2048]{1,0:T(8,128)(2,1)S(1)} %slice.87), channel_id=1, source_target_pairs={{0,2},{1,3},{2,0},{3,1},{4,6},{5,7},{6,4},{7,5},{8,10},{9,11},{10,... | collective-permute-start | bytes 393224 | tf_op jit(solution)/shard_map/ppermute | solution.py:306
  44.0 5.0 %collective-permute-start.17 = (bf16[64,2048]{1,0:T(8,128)(2,1)S(1)}, bf16[64,2048]{1,0:T(8,128)(2,1)S(1)}, u32[]{:S(2)}, u32[]{:S(2)}) collective-permute-start(bf16[64,2048]{1,0:T(8,128)(2,1)S(1)} %get-tuple-element.47), channel_id=1, source_target_pairs={{0,1},{1,0},{2,3},{3,2},{4,5},{5,4},{6,7},{7,6},{8,9},{9,8},{10,11... | collective-permute-start | bytes 786440 | tf_op jit(solution)/shard_map/ppermute | solution.py:306
  46.4 14.7 %collective-permute-start.25 = (bf16[32,2048]{1,0:T(8,128)(2,1)S(1)}, bf16[32,2048]{1,0:T(8,128)(2,1)S(1)}, u32[]{:S(2)}, u32[]{:S(2)}) collective-permute-start(bf16[32,2048]{1,0:T(8,128)(2,1)S(1)} %fusion), channel_id=1, source_target_pairs={{0,12},{4,8},{8,4},{12,0},{1,13},{5,9},{9,5},{13,1},{2,14},{6,10},... | collective-permute-start | bytes 393224 | tf_op jit(solution)/shard_map/ppermute | solution.py:303
  49.0 5.0 %collective-permute-start.21 = (bf16[32,2048]{1,0:T(8,128)(2,1)S(1)}, bf16[32,2048]{1,0:T(8,128)(2,1)S(1)}, u32[]{:S(2)}, u32[]{:S(2)}) collective-permute-start(bf16[32,2048]{1,0:T(8,128)(2,1)S(1)} %slice.88.before), channel_id=1, source_target_pairs={{0,2},{1,3},{2,0},{3,1},{4,6},{5,7},{6,4},{7,5},{8,10},{9,11},{10,... | collective-permute-start | bytes 393224 | tf_op jit(solution)/shard_map/ppermute | solution.py:306
  52.7 5.0 %collective-permute-start.18 = (bf16[32,2048]{1,0:T(8,128)(2,1)S(1)}, bf16[32,2048]{1,0:T(8,128)(2,1)S(1)}, u32[]{:S(2)}, u32[]{:S(2)}) collective-permute-start(bf16[32,2048]{1,0:T(8,128)(2,1)S(1)} %after.5), channel_id=1, source_target_pairs={{0,2},{1,3},{2,0},{3,1},{4,6},{5,7},{6,4},{7,5},{8,10},{9,11},{10,... | collective-permute-start | bytes 393224 | tf_op jit(solution)/shard_map/ppermute | solution.py:306
  54.1 7.3 %collective-permute-start.23 = (bf16[32,2048]{1,0:T(8,128)(2,1)S(1)}, bf16[32,2048]{1,0:T(8,128)(2,1)S(1)}, u32[]{:S(2)}, u32[]{:S(2)}) collective-permute-start(bf16[32,2048]{1,0:T(8,128)(2,1)S(1)} %after.6.refs_1_.before), channel_id=1, source_target_pairs={{0,8},{4,12},{8,0},{12,4},{1,9},{5,13},{9,1},{13,5},{2,10},{6,14},... | collective-permute-start | bytes 393224 | tf_op jit(solution)/shard_map/ppermute | solution.py:303
  54.5 6.7 %collective-permute-start.22 = (bf16[32,2048]{1,0:T(8,128)(2,1)S(1)}, bf16[32,2048]{1,0:T(8,128)(2,1)S(1)}, u32[]{:S(2)}, u32[]{:S(2)}) collective-permute-start(bf16[32,2048]{1,0:T(8,128)(2,1)S(1)} %after.7), channel_id=1, source_target_pairs={{0,4},{4,0},{8,12},{12,8},{1,5},{5,1},{9,13},{13,9},{2,6},{6,2},{1... | collective-permute-start | bytes 393224 | tf_op jit(solution)/shard_map/ppermute | solution.py:303

commit v5 on v4

--- a/solution.py
+++ b/solution.py
@@ -17,6 +17,7 @@
 PIECES = [[(0, 0, 2), (3, 0, 2), (1, 0, 2)], [(2, 0, 2)]]
 PARTS = 2
 TILES = 4
+PAIR_TILES = 8
 RETURNS = [[[(3, 0, 2)], [(1, 0, 2)], [(0, 0, 2)]], [[(2, 0, 2)]]]
 
 
@@ -202,9 +203,9 @@
 def pair_kernel(xs, ps, before, gate_out, up_out, results, sems):
     del before
     units = gate_out.shape[1]
-    part = xs.shape[1] // TILES
+    part = xs.shape[1] // PAIR_TILES
     copies = []
-    for t in range(TILES):
+    for t in range(PAIR_TILES):
         rows = slice(t * part, (t + 1) * part)
         both = lax.dot_general(xs[:, rows], ps[...], TN, preferred_element_type=F32)
         results[rows] = both.astype(BF16)
@@ -240,7 +241,7 @@
         out_shape=[jax.ShapeDtypeStruct((width, units), BF16)] * 2,
         in_specs=[VMEM, VMEM, ANY],
         out_specs=[HBM] * 2,
-        scratch_shapes=[pltpu.VMEM((width, 2 * units), BF16), pltpu.SemaphoreType.DMA((TILES, 2))],
+        scratch_shapes=[pltpu.VMEM((width, 2 * units), BF16), pltpu.SemaphoreType.DMA((PAIR_TILES, 2))],
         compiler_params=params(16),
         cost_estimate=cost(4 * total * width * units, 4 * width * units),
         name="pair_grads",

time: 62.6 us -> 62.6 us (level)
  transfers between devices with their start and end apart: 26 -> 26, of which waited for: 10 -> 10; matrix products, arithmetic and copies ran while one was open for 1% -> 1% of each run, Pallas kernels for 25% -> 24%
where the time goes in v5:
time: 62.6 us; the launch traced here: 62.4 us
  starting transfers between devices  23 us (37%)
  waiting for transfers between devices  20.1 us (32%)
  Pallas kernels  17.9 us (29%)
  between operations  0.83 us (1%)
    ppermute x6, waiting for transfers between devices, over_expert(): return lax.ppermute(a, 'expert', [(i, i ^ k) for i in range(experts)])  13.7 us
    ppermute x20, starting transfers between devices, over_et(): return lax.ppermute(a, 'et', [(i, i ^ m) for i in range(shards)])  12.6 us
    ppermute x6, starting transfers between devices, over_expert(): return lax.ppermute(a, 'expert', [(i, i ^ k) for i in range(experts)])  10.4 us
    ppermute x20, waiting for transfers between devices, over_et(): return lax.ppermute(a, 'et', [(i, i ^ m) for i in range(shards)])  6.42 us
    pallas_call x2, Pallas kernels, chunk_backward(): pl.pallas_call(functools.partial(chunk_kernel, n, first), out_shape=[jax....  6.26 us
    pallas_call x1, Pallas kernels, load_weights(): pl.pallas_call(load_kernel, out_shape=[jax.ShapeDtypeStruct((width, 2 * u...  3.53 us
    pallas_call x1, Pallas kernels, pair_grads(): pl.pallas_call(pair_kernel, out_shape=[jax.ShapeDtypeStruct((width, units...  3.31 us
    pallas_call x1, Pallas kernels, down_grads(): pl.pallas_call(down_kernel, out_shape=[jax.ShapeDtypeStruct((units, width...  2.12 us
  transfers between devices with their start and end apart: 26, of which 10 were waited for; matrix products, arithmetic and copies ran while one was open for 1% of the time, Pallas kernels for 24%

profile of v5, /device:TPU:0, one launch (start us, length us, event | category | flops | bytes accessed | tf_op | source)
XLA Modules:
  0.0 62.4 jit_solution(4655957750609912373)
XLA Ops:
  0.6 1.7 %select_rows.1 = (bf16[32,4096]{1,0:T(8,128)(2,1)S(1)}, bf16[32,4096]{1,0:T(8,128)(2,1)S(1)}, bf16[32,4096]{1,0:T(8,128)(2,1)S(1)}, bf16[32,4096]{1,0:T(8,128)(2,1)S(1)}, bf16[128,128]{1,0:T(8,128)(2,1)S(1)}) custom-call(bf16[128,2048]{1,0:T(8,128)(2,1)} %tokens.1, bf16[128,2048]{1,0:T(8,128)(2,1)} %grad_out.1, s32[1,128]{1,0:T(1,128)} %bitcast.10, ...), custom_call_target="tpu_custom_call" | custom-call | flops 134217728 | bytes 2097152 | tf_op jit(solution)/shard_map/select_rows/pallas_call | solution.py:93
  2.3 5.1 %collective-permute-start.1 = (bf16[32,4096]{1,0:T(8,128)(2,1)S(1)}, bf16[32,4096]{1,0:T(8,128)(2,1)S(1)}, u32[]{:S(2)}, u32[]{:S(2)}) collective-permute-start(bf16[32,4096]{1,0:T(8,128)(2,1)S(1)} %get-tuple-element.32), channel_id=1, source_target_pairs={{0,12},{4,8},{8,4},{12,0},{1,13},{5,9},{9,5},{13,1},{2,14},{6,10},... | collective-permute-start | bytes 786440 | tf_op jit(solution)/shard_map/ppermute | solution.py:304
  7.4 1.5 %collective-permute-start = (bf16[32,4096]{1,0:T(8,128)(2,1)S(1)}, bf16[32,4096]{1,0:T(8,128)(2,1)S(1)}, u32[]{:S(2)}, u32[]{:S(2)}) collective-permute-start(bf16[32,4096]{1,0:T(8,128)(2,1)S(1)} %get-tuple-element.30.refs_0_), channel_id=1, source_target_pairs={{0,2},{1,3},{2,0},{3,1},{4,6},{5,7},{6,4},{7,5},{8,10},{9,11},{10,... | collective-permute-start | bytes 786440 | tf_op jit(solution)/shard_map/ppermute | solution.py:307
  8.9 0.8 %collective-permute-start.12 = (bf16[32,4096]{1,0:T(8,128)(2,1)S(1)}, bf16[32,4096]{1,0:T(8,128)(2,1)S(1)}, u32[]{:S(2)}, u32[]{:S(2)}) collective-permute-start(bf16[32,4096]{1,0:T(8,128)(2,1)S(1)} %get-tuple-element.39), channel_id=1, source_target_pairs={{0,8},{4,12},{8,0},{12,4},{1,9},{5,13},{9,1},{13,5},{2,10},{6,14},... | collective-permute-start | bytes 786440 | tf_op jit(solution)/shard_map/ppermute | solution.py:304
  9.7 4.9 %collective-permute-done.1.refs_2_ = bf16[32,4096]{1,0:T(8,128)(2,1)S(1)} collective-permute-done((bf16[32,4096]{1,0:T(8,128)(2,1)S(1)}, bf16[32,4096]{1,0:T(8,128)(2,1)S(1)}, u32[]{:S(2)}, u32[]{:S(2)}) %collective-permute-start.1) | collective-permute-done | bytes 262176 | tf_op jit(solution)/shard_map/ppermute | solution.py:304
  14.7 1.7 %collective-permute-start.2 = (bf16[32,4096]{1,0:T(8,128)(2,1)S(1)}, bf16[32,4096]{1,0:T(8,128)(2,1)S(1)}, u32[]{:S(2)}, u32[]{:S(2)}) collective-permute-start(bf16[32,4096]{1,0:T(8,128)(2,1)S(1)} %collective-permute-done.1.refs_2_), channel_id=1, source_target_pairs={{0,2},{1,3},{2,0},{3,1},{4,6},{5,7},{6,4},{7,5},{8,10},{9,11},{10,... | collective-permute-start | bytes 786440 | tf_op jit(solution)/shard_map/ppermute | solution.py:307
  16.4 4.1 %collective-permute-done.3.refs_4_ = bf16[32,4096]{1,0:T(8,128)(2,1)S(1)} collective-permute-done((bf16[32,4096]{1,0:T(8,128)(2,1)S(1)}, bf16[32,4096]{1,0:T(8,128)(2,1)S(1)}, u32[]{:S(2)}, u32[]{:S(2)}) %collective-permute-start.3) | collective-permute-done | bytes 262176 | tf_op jit(solution)/shard_map/ppermute | solution.py:304
  20.5 1.4 %collective-permute-start.4 = (bf16[32,4096]{1,0:T(8,128)(2,1)S(1)}, bf16[32,4096]{1,0:T(8,128)(2,1)S(1)}, u32[]{:S(2)}, u32[]{:S(2)}) collective-permute-start(bf16[32,4096]{1,0:T(8,128)(2,1)S(1)} %collective-permute-done.3.refs_4_), channel_id=1, source_target_pairs={{0,2},{1,3},{2,0},{3,1},{4,6},{5,7},{6,4},{7,5},{8,10},{9,11},{10,... | collective-permute-start | bytes 786440 | tf_op jit(solution)/shard_map/ppermute | solution.py:307
  21.9 3.5 %load_weights.1 = (bf16[2048,1024]{1,0:T(8,128)(2,1)S(1)}, bf16[1024,2048]{1,0:T(8,128)(2,1)S(1)}, bf16[2048,512]{1,0:T(8,128)(2,1)S(1)}, bf16[32,4096]{1,0:T(8,128)(2,1)S(1)}) custom-call(bf16[2048,512]{1,0:T(8,128)(2,1)} %bitcast.7, bf16[2048,512]{1,0:T(8,128)(2,1)} %bitcast.8, bf16[512,2048]{1,0:T(8,128)(2,1)} %bitcast.9, ...), custom_call_target="tpu_custom_call", output_to_operand_aliasing={{3}: (3, {})} | custom-call | tf_op jit(solution)/shard_map/load_weights/pallas_call | solution.py:133
  25.5 4.3 %collective-permute-done.12.refs_0_ = bf16[32,4096]{1,0:T(8,128)(2,1)S(1)} collective-permute-done((bf16[32,4096]{1,0:T(8,128)(2,1)S(1)}, bf16[32,4096]{1,0:T(8,128)(2,1)S(1)}, u32[]{:S(2)}, u32[]{:S(2)}) %collective-permute-start.12) | collective-permute-done | bytes 262176 | tf_op jit(solution)/shard_map/ppermute | solution.py:304
  29.7 0.5 collective-permute-start.9
  30.3 0.4 collective-permute-start.10
  30.8 0.5 collective-permute-done.7.refs_8_
  31.3 1.5 %collective-permute-start.13 = (bf16[32,4096]{1,0:T(8,128)(2,1)S(1)}, bf16[32,4096]{1,0:T(8,128)(2,1)S(1)}, u32[]{:S(2)}, u32[]{:S(2)}) collective-permute-start(bf16[32,4096]{1,0:T(8,128)(2,1)S(1)} %collective-permute-done.12.refs_0_), channel_id=1, source_target_pairs={{0,2},{1,3},{2,0},{3,1},{4,6},{5,7},{6,4},{7,5},{8,10},{9,11},{10,... | collective-permute-start | bytes 786440 | tf_op jit(solution)/shard_map/ppermute | solution.py:307
  32.8 4.5 %chunk_backward.2 = (bf16[512,2048]{1,0:T(8,128)(2,1)S(1)}, bf16[512,2048]{1,0:T(8,128)(2,1)S(1)}, bf16[512,512]{1,0:T(8,128)(2,1)S(1)}, bf16[512,1024]{1,0:T(8,...) custom-call(bf16[32,4096]{1,0:T(8,128)(2,1)S(1)} %get-tuple-element.30.refs_0_, ...), custom_call_target="tpu_custom_call" | custom-call | flops 4026531840 | bytes 6291456 | tf_op jit(solution)/shard_map/chunk_backward/pallas_call | solution.py:184
  37.5 0.5 collective-permute-start.16
  38.1 0.4 collective-permute-start.14
  38.5 1.1 %collective-permute-done.13.refs_0_ = bf16[32,4096]{1,0:T(8,128)(2,1)S(1)} collective-permute-done((bf16[32,4096]{1,0:T(8,128)(2,1)S(1)}, bf16[32,4096]{1,0:T(8,128)(2,1)S(1)}, u32[]{:S(2)}, u32[]{:S(2)}) %collective-permute-start.13) | collective-permute-done | bytes 262176 | tf_op jit(solution)/shard_map/ppermute | solution.py:307
  40.0 1.5 %collective-permute-start.24 = (bf16[32,2048]{1,0:T(8,128)(2,1)S(1)}, bf16[32,2048]{1,0:T(8,128)(2,1)S(1)}, u32[]{:S(2)}, u32[]{:S(2)}) collective-permute-start(bf16[32,2048]{1,0:T(8,128)(2,1)S(1)} %slice.89.refs_12_), channel_id=1, source_target_pairs={{0,2},{1,3},{2,0},{3,1},{4,6},{5,7},{6,4},{7,5},{8,10},{9,11},{10,... | collective-permute-start | bytes 393224 | tf_op jit(solution)/shard_map/ppermute | solution.py:307
  41.5 0.7 %collective-permute-start.20 = (bf16[32,2048]{1,0:T(8,128)(2,1)S(1)}, bf16[32,2048]{1,0:T(8,128)(2,1)S(1)}, u32[]{:S(2)}, u32[]{:S(2)}) collective-permute-start(bf16[32,2048]{1,0:T(8,128)(2,1)S(1)} %slice.87), channel_id=1, source_target_pairs={{0,2},{1,3},{2,0},{3,1},{4,6},{5,7},{6,4},{7,5},{8,10},{9,11},{10,... | collective-permute-start | bytes 393224 | tf_op jit(solution)/shard_map/ppermute | solution.py:307
  42.2 1.7 %chunk_backward.3 = (bf16[512,2048]{1,0:T(8,128)(2,1)S(1)}, bf16[512,2048]{1,0:T(8,128)(2,1)S(1)}, bf16[512,512]{1,0:T(8,128)(2,1)S(1)}, bf16[512,1024]{1,0:T(8,...) custom-call(bf16[32,4096]{1,0:T(8,128)(2,1)S(1)} %collective-permute, ...), custom_call_target="tpu_custom_call", output_to_operand_aliasing={{0}: (7, {}), {1}: (8, {}), {2}: (9, {}), {3}: (10, {})} | custom-call | flops 1342177280 | bytes 6291456 | tf_op jit(solution)/shard_map/chunk_backward/pallas_call | solution.py:184
  44.0 2.3 %collective-permute-done.24 = bf16[32,2048]{1,0:T(8,128)(2,1)S(1)} collective-permute-done((bf16[32,2048]{1,0:T(8,128)(2,1)S(1)}, bf16[32,2048]{1,0:T(8,128)(2,1)S(1)}, u32[]{:S(2)}, u32[]{:S(2)}) %collective-permute-start.24) | collective-permute-done | bytes 131104 | tf_op jit(solution)/shard_map/ppermute | solution.py:307
  46.4 2.5 %collective-permute-start.25 = (bf16[32,2048]{1,0:T(8,128)(2,1)S(1)}, bf16[32,2048]{1,0:T(8,128)(2,1)S(1)}, u32[]{:S(2)}, u32[]{:S(2)}) collective-permute-start(bf16[32,2048]{1,0:T(8,128)(2,1)S(1)} %fusion), channel_id=1, source_target_pairs={{0,12},{4,8},{8,4},{12,0},{1,13},{5,9},{9,5},{13,1},{2,14},{6,10},... | collective-permute-start | bytes 393224 | tf_op jit(solution)/shard_map/ppermute | solution.py:304
  49.0 1.4 %collective-permute-start.21 = (bf16[32,2048]{1,0:T(8,128)(2,1)S(1)}, bf16[32,2048]{1,0:T(8,128)(2,1)S(1)}, u32[]{:S(2)}, u32[]{:S(2)}) collective-permute-start(bf16[32,2048]{1,0:T(8,128)(2,1)S(1)} %slice.88.before), channel_id=1, source_target_pairs={{0,2},{1,3},{2,0},{3,1},{4,6},{5,7},{6,4},{7,5},{8,10},{9,11},{10,... | collective-permute-start | bytes 393224 | tf_op jit(solution)/shard_map/ppermute | solution.py:307
  50.5 2.1 %down_grads.1 = (bf16[512,2048]{1,0:T(8,128)(2,1)}, f32[8,128]{1,0:T(8,128)S(1)}) custom-call(bf16[512,2048]{1,0:T(8,128)(2,1)S(1)} %get-tuple-element.44.ys, bf16[512,512]{1,0:T(8,128)(2,1)S(1)} %get-tuple-element.45.hs, bf16[32,2048]{1,0:T(8,128)(2,1)S(1)} %slice.88.before), custom_call_target="tpu_custom_call" | custom-call | flops 1073741824 | bytes 2097152 | tf_op jit(solution)/shard_map/down_grads/pallas_call | solution.py:254
  52.7 0.7 %collective-permute-start.18 = (bf16[32,2048]{1,0:T(8,128)(2,1)S(1)}, bf16[32,2048]{1,0:T(8,128)(2,1)S(1)}, u32[]{:S(2)}, u32[]{:S(2)}) collective-permute-start(bf16[32,2048]{1,0:T(8,128)(2,1)S(1)} %after.5), channel_id=1, source_target_pairs={{0,2},{1,3},{2,0},{3,1},{4,6},{5,7},{6,4},{7,5},{8,10},{9,11},{10,... | collective-permute-start | bytes 393224 | tf_op jit(solution)/shard_map/ppermute | solution.py:307
  53.4 0.7 %collective-permute-done.21 = bf16[32,2048]{1,0:T(8,128)(2,1)S(1)} collective-permute-done((bf16[32,2048]{1,0:T(8,128)(2,1)S(1)}, bf16[32,2048]{1,0:T(8,128)(2,1)S(1)}, u32[]{:S(2)}, u32[]{:S(2)}) %collective-permute-start.21) | collective-permute-done | bytes 131104 | tf_op jit(solution)/shard_map/ppermute | solution.py:307
  54.1 0.4 collective-permute-start.23
  54.5 1.6 %collective-permute-start.22 = (bf16[32,2048]{1,0:T(8,128)(2,1)S(1)}, bf16[32,2048]{1,0:T(8,128)(2,1)S(1)}, u32[]{:S(2)}, u32[]{:S(2)}) collective-permute-start(bf16[32,2048]{1,0:T(8,128)(2,1)S(1)} %after.7), channel_id=1, source_target_pairs={{0,4},{4,0},{8,12},{12,8},{1,5},{5,1},{9,13},{13,9},{2,6},{6,2},{1... | collective-permute-start | bytes 393224 | tf_op jit(solution)/shard_map/ppermute | solution.py:304
  56.1 1.6 %collective-permute-done.18 = bf16[32,2048]{1,0:T(8,128)(2,1)S(1)} collective-permute-done((bf16[32,2048]{1,0:T(8,128)(2,1)S(1)}, bf16[32,2048]{1,0:T(8,128)(2,1)S(1)}, u32[]{:S(2)}, u32[]{:S(2)}) %collective-permute-start.18) | collective-permute-done | bytes 131104 | tf_op jit(solution)/shard_map/ppermute | solution.py:307
  57.7 3.3 %pair_grads.1 = (bf16[2048,512]{1,0:T(8,128)(2,1)}, bf16[2048,512]{1,0:T(8,128)(2,1)}) custom-call(bf16[512,2048]{1,0:T(8,128)(2,1)S(1)} %get-tuple-element.49.xs, bf16[512,1024]{1,0:T(8,128)(2,1)S(1)} %get-tuple-element.50.ps, bf16[32,2048]{1,0:T(8,128)(2,1)S(1)} %after.6.refs_1_.before), custom_call_target="tpu_custom_call" | custom-call | flops 2147483648 | bytes 4194304 | tf_op jit(solution)/shard_map/pair_grads/pallas_call | solution.py:239
  61.4 1.0 %place_rows.1 = bf16[128,2048]{1,0:T(8,128)(2,1)} custom-call(bf16[128,128]{1,0:T(8,128)(2,1)S(1)} %get-tuple-element.29.back, bf16[32,2048]{1,0:T(8,128)(2,1)S(1)} %fusion.3.refs_0_, bf16[32,2048]{1,0:T(8,128)(2,1)S(1)} %collective-permute-done.22.refs_1_, bf16[32,2048]{1,0:T(8,128)(2,1)S(1)} %collective-permute-done.23.refs_2_, ...), custom_call_target="tpu_custom_call" | custom-call | flops 67108864 | bytes 1048576 | tf_op jit(solution)/shard_map/place_rows/pallas_call | solution.py:282
  (42 shorter events, 1.4 us)
Async XLA Ops:
  2.3 12.3 %collective-permute-start.1 = (bf16[32,4096]{1,0:T(8,128)(2,1)S(1)}, bf16[32,4096]{1,0:T(8,128)(2,1)S(1)}, u32[]{:S(2)}, u32[]{:S(2)}) collective-permute-start(bf16[32,4096]{1,0:T(8,128)(2,1)S(1)} %get-tuple-element.32), channel_id=1, source_target_pairs={{0,12},{4,8},{8,4},{12,0},{1,13},{5,9},{9,5},{13,1},{2,14},{6,10},... | collective-permute-start | bytes 786440 | tf_op jit(solution)/shard_map/ppermute | solution.py:304
  7.4 13.1 %collective-permute-start.3 = (bf16[32,4096]{1,0:T(8,128)(2,1)S(1)}, bf16[32,4096]{1,0:T(8,128)(2,1)S(1)}, u32[]{:S(2)}, u32[]{:S(2)}) collective-permute-start(bf16[32,4096]{1,0:T(8,128)(2,1)S(1)} %get-tuple-element.33), channel_id=1, source_target_pairs={{0,4},{4,0},{8,12},{12,8},{1,5},{5,1},{9,13},{13,9},{2,6},{6,2},{1... | collective-permute-start | bytes 786440 | tf_op jit(solution)/shard_map/ppermute | solution.py:304
  7.4 14.4 %collective-permute-start = (bf16[32,4096]{1,0:T(8,128)(2,1)S(1)}, bf16[32,4096]{1,0:T(8,128)(2,1)S(1)}, u32[]{:S(2)}, u32[]{:S(2)}) collective-permute-start(bf16[32,4096]{1,0:T(8,128)(2,1)S(1)} %get-tuple-element.30.refs_0_), channel_id=1, source_target_pairs={{0,2},{1,3},{2,0},{3,1},{4,6},{5,7},{6,4},{7,5},{8,10},{9,11},{10,... | collective-permute-start | bytes 786440 | tf_op jit(solution)/shard_map/ppermute | solution.py:307
  8.9 20.8 %collective-permute-start.12 = (bf16[32,4096]{1,0:T(8,128)(2,1)S(1)}, bf16[32,4096]{1,0:T(8,128)(2,1)S(1)}, u32[]{:S(2)}, u32[]{:S(2)}) collective-permute-start(bf16[32,4096]{1,0:T(8,128)(2,1)S(1)} %get-tuple-element.39), channel_id=1, source_target_pairs={{0,8},{4,12},{8,0},{12,4},{1,9},{5,13},{9,1},{13,5},{2,10},{6,14},... | collective-permute-start | bytes 786440 | tf_op jit(solution)/shard_map/ppermute | solution.py:304
  9.7 20.0 %collective-permute-start.5 = (bf16[32,4096]{1,0:T(8,128)(2,1)S(1)}, bf16[32,4096]{1,0:T(8,128)(2,1)S(1)}, u32[]{:S(2)}, u32[]{:S(2)}) collective-permute-start(bf16[32,4096]{1,0:T(8,128)(2,1)S(1)} %get-tuple-element.30.refs_0_), channel_id=1, source_target_pairs={{0,1},{1,0},{2,3},{3,2},{4,5},{5,4},{6,7},{7,6},{8,9},{9,8},{10,11... | collective-permute-start | bytes 786440 | tf_op jit(solution)/shard_map/ppermute | solution.py:307
  14.7 15.6 %collective-permute-start.2 = (bf16[32,4096]{1,0:T(8,128)(2,1)S(1)}, bf16[32,4096]{1,0:T(8,128)(2,1)S(1)}, u32[]{:S(2)}, u32[]{:S(2)}) collective-permute-start(bf16[32,4096]{1,0:T(8,128)(2,1)S(1)} %collective-permute-done.1.refs_2_), channel_id=1, source_target_pairs={{0,2},{1,3},{2,0},{3,1},{4,6},{5,7},{6,4},{7,5},{8,10},{9,11},{10,... | collective-permute-start | bytes 786440 | tf_op jit(solution)/shard_map/ppermute | solution.py:307
  20.5 9.8 %collective-permute-start.4 = (bf16[32,4096]{1,0:T(8,128)(2,1)S(1)}, bf16[32,4096]{1,0:T(8,128)(2,1)S(1)}, u32[]{:S(2)}, u32[]{:S(2)}) collective-permute-start(bf16[32,4096]{1,0:T(8,128)(2,1)S(1)} %collective-permute-done.3.refs_4_), channel_id=1, source_target_pairs={{0,2},{1,3},{2,0},{3,1},{4,6},{5,7},{6,4},{7,5},{8,10},{9,11},{10,... | collective-permute-start | bytes 786440 | tf_op jit(solution)/shard_map/ppermute | solution.py:307
  25.4 7.4 %collective-permute-start.6 = (bf16[32,4096]{1,0:T(8,128)(2,1)S(1)}, bf16[32,4096]{1,0:T(8,128)(2,1)S(1)}, u32[]{:S(2)}, u32[]{:S(2)}) collective-permute-start(bf16[32,4096]{1,0:T(8,128)(2,1)S(1)} %get-tuple-element.31.refs_1_), channel_id=1, source_target_pairs={{0,1},{1,0},{2,3},{3,2},{4,5},{5,4},{6,7},{7,6},{8,9},{9,8},{10,11... | collective-permute-start | bytes 786440 | tf_op jit(solution)/shard_map/ppermute | solution.py:307
  29.7 1.5 %collective-permute-start.7 = (bf16[32,4096]{1,0:T(8,128)(2,1)S(1)}, bf16[32,4096]{1,0:T(8,128)(2,1)S(1)}, u32[]{:S(2)}, u32[]{:S(2)}) collective-permute-start(bf16[32,4096]{1,0:T(8,128)(2,1)S(1)} %collective-permute-done.1.refs_2_), channel_id=1, source_target_pairs={{0,1},{1,0},{2,3},{3,2},{4,5},{5,4},{6,7},{7,6},{8,9},{9,8},{10,11... | collective-permute-start | bytes 786440 | tf_op jit(solution)/shard_map/ppermute | solution.py:307
  29.7 3.0 %collective-permute-start.9 = (bf16[32,4096]{1,0:T(8,128)(2,1)S(1)}, bf16[32,4096]{1,0:T(8,128)(2,1)S(1)}, u32[]{:S(2)}, u32[]{:S(2)}) collective-permute-start(bf16[32,4096]{1,0:T(8,128)(2,1)S(1)} %collective-permute-done.3.refs_4_), channel_id=1, source_target_pairs={{0,1},{1,0},{2,3},{3,2},{4,5},{5,4},{6,7},{7,6},{8,9},{9,8},{10,11... | collective-permute-start | bytes 786440 | tf_op jit(solution)/shard_map/ppermute | solution.py:307
  30.3 2.5 %collective-permute-start.8 = (bf16[32,4096]{1,0:T(8,128)(2,1)S(1)}, bf16[32,4096]{1,0:T(8,128)(2,1)S(1)}, u32[]{:S(2)}, u32[]{:S(2)}) collective-permute-start(bf16[32,4096]{1,0:T(8,128)(2,1)S(1)} %collective-permute-done.2.refs_3_), channel_id=1, source_target_pairs={{0,1},{1,0},{2,3},{3,2},{4,5},{5,4},{6,7},{7,6},{8,9},{9,8},{10,11... | collective-permute-start | bytes 786440 | tf_op jit(solution)/shard_map/ppermute | solution.py:307
  30.3 2.5 %collective-permute-start.10 = (bf16[32,4096]{1,0:T(8,128)(2,1)S(1)}, bf16[32,4096]{1,0:T(8,128)(2,1)S(1)}, u32[]{:S(2)}, u32[]{:S(2)}) collective-permute-start(bf16[32,4096]{1,0:T(8,128)(2,1)S(1)} %collective-permute-done.4.refs_5_), channel_id=1, source_target_pairs={{0,1},{1,0},{2,3},{3,2},{4,5},{5,4},{6,7},{7,6},{8,9},{9,8},{10,11... | collective-permute-start | bytes 786440 | tf_op jit(solution)/shard_map/ppermute | solution.py:307
  31.3 8.3 %collective-permute-start.13 = (bf16[32,4096]{1,0:T(8,128)(2,1)S(1)}, bf16[32,4096]{1,0:T(8,128)(2,1)S(1)}, u32[]{:S(2)}, u32[]{:S(2)}) collective-permute-start(bf16[32,4096]{1,0:T(8,128)(2,1)S(1)} %collective-permute-done.12.refs_0_), channel_id=1, source_target_pairs={{0,2},{1,3},{2,0},{3,1},{4,6},{5,7},{6,4},{7,5},{8,10},{9,11},{10,... | collective-permute-start | bytes 786440 | tf_op jit(solution)/shard_map/ppermute | solution.py:307
  37.4 2.2 %collective-permute-start.19 = (bf16[64,2048]{1,0:T(8,128)(2,1)S(1)}, bf16[64,2048]{1,0:T(8,128)(2,1)S(1)}, u32[]{:S(2)}, u32[]{:S(2)}) collective-permute-start(bf16[64,2048]{1,0:T(8,128)(2,1)S(1)} %get-tuple-element.57), channel_id=1, source_target_pairs={{0,1},{1,0},{2,3},{3,2},{4,5},{5,4},{6,7},{7,6},{8,9},{9,8},{10,11... | collective-permute-start | bytes 786440 | tf_op jit(solution)/shard_map/ppermute | solution.py:307
  37.5 2.2 %collective-permute-start.16 = (bf16[64,2048]{1,0:T(8,128)(2,1)S(1)}, bf16[64,2048]{1,0:T(8,128)(2,1)S(1)}, u32[]{:S(2)}, u32[]{:S(2)}) collective-permute-start(bf16[64,2048]{1,0:T(8,128)(2,1)S(1)} %get-tuple-element.58), channel_id=1, source_target_pairs={{0,1},{1,0},{2,3},{3,2},{4,5},{5,4},{6,7},{7,6},{8,9},{9,8},{10,11... | collective-permute-start | bytes 786440 | tf_op jit(solution)/shard_map/ppermute | solution.py:307
  38.0 1.8 %collective-permute-start.11 = (bf16[64,2048]{1,0:T(8,128)(2,1)S(1)}, bf16[64,2048]{1,0:T(8,128)(2,1)S(1)}, u32[]{:S(2)}, u32[]{:S(2)}) collective-permute-start(bf16[64,2048]{1,0:T(8,128)(2,1)S(1)} %get-tuple-element.59), channel_id=1, source_target_pairs={{0,1},{1,0},{2,3},{3,2},{4,5},{5,4},{6,7},{7,6},{8,9},{9,8},{10,11... | collective-permute-start | bytes 786440 | tf_op jit(solution)/shard_map/ppermute | solution.py:307
  38.1 4.2 %collective-permute-start.14 = (bf16[32,4096]{1,0:T(8,128)(2,1)S(1)}, bf16[32,4096]{1,0:T(8,128)(2,1)S(1)}, u32[]{:S(2)}, u32[]{:S(2)}) collective-permute-start(bf16[32,4096]{1,0:T(8,128)(2,1)S(1)} %collective-permute-done.12.refs_0_), channel_id=1, source_target_pairs={{0,1},{1,0},{2,3},{3,2},{4,5},{5,4},{6,7},{7,6},{8,9},{9,8},{10,11... | collective-permute-start | bytes 786440 | tf_op jit(solution)/shard_map/ppermute | solution.py:307
  39.6 2.6 %collective-permute-start.15 = (bf16[32,4096]{1,0:T(8,128)(2,1)S(1)}, bf16[32,4096]{1,0:T(8,128)(2,1)S(1)}, u32[]{:S(2)}, u32[]{:S(2)}) collective-permute-start(bf16[32,4096]{1,0:T(8,128)(2,1)S(1)} %after.4.refs_1_), channel_id=1, source_target_pairs={{0,1},{1,0},{2,3},{3,2},{4,5},{5,4},{6,7},{7,6},{8,9},{9,8},{10,11... | collective-permute-start | bytes 786440 | tf_op jit(solution)/shard_map/ppermute | solution.py:307
  40.0 6.4 %collective-permute-start.24 = (bf16[32,2048]{1,0:T(8,128)(2,1)S(1)}, bf16[32,2048]{1,0:T(8,128)(2,1)S(1)}, u32[]{:S(2)}, u32[]{:S(2)}) collective-permute-start(bf16[32,2048]{1,0:T(8,128)(2,1)S(1)} %slice.89.refs_12_), channel_id=1, source_target_pairs={{0,2},{1,3},{2,0},{3,1},{4,6},{5,7},{6,4},{7,5},{8,10},{9,11},{10,... | collective-permute-start | bytes 393224 | tf_op jit(solution)/shard_map/ppermute | solution.py:307
  41.5 9.0 %collective-permute-start.20 = (bf16[32,2048]{1,0:T(8,128)(2,1)S(1)}, bf16[32,2048]{1,0:T(8,128)(2,1)S(1)}, u32[]{:S(2)}, u32[]{:S(2)}) collective-permute-start(bf16[32,2048]{1,0:T(8,128)(2,1)S(1)} %slice.87), channel_id=1, source_target_pairs={{0,2},{1,3},{2,0},{3,1},{4,6},{5,7},{6,4},{7,5},{8,10},{9,11},{10,... | collective-permute-start | bytes 393224 | tf_op jit(solution)/shard_map/ppermute | solution.py:307
  44.0 5.0 %collective-permute-start.17 = (bf16[64,2048]{1,0:T(8,128)(2,1)S(1)}, bf16[64,2048]{1,0:T(8,128)(2,1)S(1)}, u32[]{:S(2)}, u32[]{:S(2)}) collective-permute-start(bf16[64,2048]{1,0:T(8,128)(2,1)S(1)} %get-tuple-element.47), channel_id=1, source_target_pairs={{0,1},{1,0},{2,3},{3,2},{4,5},{5,4},{6,7},{7,6},{8,9},{9,8},{10,11... | collective-permute-start | bytes 786440 | tf_op jit(solution)/shard_map/ppermute | solution.py:307
  46.4 14.6 %collective-permute-start.25 = (bf16[32,2048]{1,0:T(8,128)(2,1)S(1)}, bf16[32,2048]{1,0:T(8,128)(2,1)S(1)}, u32[]{:S(2)}, u32[]{:S(2)}) collective-permute-start(bf16[32,2048]{1,0:T(8,128)(2,1)S(1)} %fusion), channel_id=1, source_target_pairs={{0,12},{4,8},{8,4},{12,0},{1,13},{5,9},{9,5},{13,1},{2,14},{6,10},... | collective-permute-start | bytes 393224 | tf_op jit(solution)/shard_map/ppermute | solution.py:304
  49.0 5.0 %collective-permute-start.21 = (bf16[32,2048]{1,0:T(8,128)(2,1)S(1)}, bf16[32,2048]{1,0:T(8,128)(2,1)S(1)}, u32[]{:S(2)}, u32[]{:S(2)}) collective-permute-start(bf16[32,2048]{1,0:T(8,128)(2,1)S(1)} %slice.88.before), channel_id=1, source_target_pairs={{0,2},{1,3},{2,0},{3,1},{4,6},{5,7},{6,4},{7,5},{8,10},{9,11},{10,... | collective-permute-start | bytes 393224 | tf_op jit(solution)/shard_map/ppermute | solution.py:307
  52.7 5.0 %collective-permute-start.18 = (bf16[32,2048]{1,0:T(8,128)(2,1)S(1)}, bf16[32,2048]{1,0:T(8,128)(2,1)S(1)}, u32[]{:S(2)}, u32[]{:S(2)}) collective-permute-start(bf16[32,2048]{1,0:T(8,128)(2,1)S(1)} %after.5), channel_id=1, source_target_pairs={{0,2},{1,3},{2,0},{3,1},{4,6},{5,7},{6,4},{7,5},{8,10},{9,11},{10,... | collective-permute-start | bytes 393224 | tf_op jit(solution)/shard_map/ppermute | solution.py:307
  54.1 7.3 %collective-permute-start.23 = (bf16[32,2048]{1,0:T(8,128)(2,1)S(1)}, bf16[32,2048]{1,0:T(8,128)(2,1)S(1)}, u32[]{:S(2)}, u32[]{:S(2)}) collective-permute-start(bf16[32,2048]{1,0:T(8,128)(2,1)S(1)} %after.6.refs_1_.before), channel_id=1, source_target_pairs={{0,8},{4,12},{8,0},{12,4},{1,9},{5,13},{9,1},{13,5},{2,10},{6,14},... | collective-permute-start | bytes 393224 | tf_op jit(solution)/shard_map/ppermute | solution.py:304
  54.5 6.6 %collective-permute-start.22 = (bf16[32,2048]{1,0:T(8,128)(2,1)S(1)}, bf16[32,2048]{1,0:T(8,128)(2,1)S(1)}, u32[]{:S(2)}, u32[]{:S(2)}) collective-permute-start(bf16[32,2048]{1,0:T(8,128)(2,1)S(1)} %after.7), channel_id=1, source_target_pairs={{0,4},{4,0},{8,12},{12,8},{1,5},{5,1},{9,13},{13,9},{2,6},{6,2},{1... | collective-permute-start | bytes 393224 | tf_op jit(solution)/shard_map/ppermute | solution.py:304
